TPU v7x, 32 devices: a whole 2x2x4 slice. The times are simulated.
32 devices in a mesh: grp: 4 (over z), sp: 8 (over y, x, core).
Axes of the slice: x: 2, y: 2, z: 4, core: 2. Of those that a mesh axis runs over, the one named last changes fastest.
Arguments:
- query_input: bfloat16 [4096, 4096], P(('grp', 'sp')), may hold values from -6 to 6
- key_input: bfloat16 [4096, 4096], P(('grp', 'sp')), may hold values from -6 to 6
- value_heads_input: bfloat16 [4096, 4096], P(('grp', 'sp')), may hold values from -6 to 6
- conv_weight: float32 [3, 4, 4096], P(None, None, 'sp'), may hold values from -3 to 3
- feature_map: bfloat16 [128, 1024], replicated, may hold values from -0.5 to 0.5
- out_gain: float32 [4096], P('sp'), may hold values from 0.25 to 1.75
Outputs:
- attended: bfloat16 [4096, 4096], P(('grp', 'sp'))
All inputs are finite; a program needn't handle non-finite values.
Results may differ from a plain program's by a relative error of at most 0.0052.
Values may be sent and summed in bfloat16 or wider, within the bound.
No kernel may reach another device: no remote copies, remote signals or barrier semaphores. Data moves between devices by JAX's collectives and lax.ppermute only.
A program may use at most 128 MiB of HBM per device.

v0:
```python
import functools

import jax
import jax.numpy as jnp
from jax import lax
from jax.experimental import pallas as pl
from jax.experimental.pallas import tpu as pltpu
from jax.sharding import Mesh
from jax.sharding import PartitionSpec as P

H = 32
DH = 128
BLOCK = 256
TAIL = 8
RIM = 16
GROUP = ("part", "sp")


def dot(a, b):
    return jnp.dot(a, b, preferred_element_type=jnp.float32)


def dot_nt(a, b):
    return lax.dot_general(a, b, (((1,), (1,)), ((), ())), preferred_element_type=jnp.float32)


def conv(pad_ref, weights, begin):
    total = jnp.zeros((BLOCK, pad_ref.shape[1]), jnp.float32)
    for tap in range(weights.shape[0]):
        row = TAIL + begin - tap
        total = total + weights[tap][None, :] * pad_ref[row : row + BLOCK]
    return total.astype(jnp.bfloat16)


def relu16(x):
    return jnp.maximum(x, 0.0).astype(jnp.bfloat16)


def pack_kernel(starts, *refs):
    *sources, out_ref, held, sems = refs
    width = held.shape[-1] // sems.shape[1]
    copies = {}
    for piece in range(sems.shape[1]):
        for member, source in enumerate(sources):
            cols = pl.ds(piece * width, width)
            copies[piece, member] = pltpu.make_async_copy(
                source.at[:, cols], held.at[member, :, cols], sems.at[member, piece]
            )
            copies[piece, member].start()
    for piece in range(sems.shape[1]):
        for member in range(len(sources)):
            copies[piece, member].wait()
            for owner, start in enumerate(starts):
                if start // width == piece:
                    out_ref[owner, member] = held[member, :, start : start + DH]


def unpack_kernel(starts, *refs):
    *sources, out_ref = refs
    for head, source in enumerate(sources):
        for owner, start in enumerate(starts[head]):
            out_ref[:, start : start + DH] = source[owner]


def high_low(x):
    high = x.astype(jnp.bfloat16)
    return jnp.concatenate([high, (x - high.astype(jnp.float32)).astype(jnp.bfloat16)], 1)


def folded(x):
    return x[:, :DH] + x[:, DH:]


def fill(pad_ref, x_ref, member, begin, count):
    rows = x_ref.shape[2]
    chunks = count // rows
    held = x_ref[pl.ds(begin, chunks), member]
    pad_ref[TAIL : TAIL + count] = held.reshape(count, DH).astype(jnp.float32)


def totals_kernel(x_ref, halo_ref, w_ref, map_t_ref, sent_ref, k_pad, v_pad, state):
    count, _, rows, _ = x_ref.shape
    features = map_t_ref.shape[0]
    blocks, size = count * rows // BLOCK, k_pad.shape[0] - TAIL
    for member in range(3):
        held = slice(features + member * RIM, features + (member + 1) * RIM)
        sent_ref[held] = x_ref[count - 1, member, rows - RIM :]
    k_pad[:TAIL] = halo_ref[1, RIM - TAIL :].astype(jnp.float32)
    v_pad[:TAIL] = halo_ref[2, RIM - TAIL :].astype(jnp.float32)

    def step(i):
        fill(k_pad, x_ref, 1, i * (size // rows), size)
        fill(v_pad, x_ref, 2, i * (size // rows), size)
        update = None
        for begin in range(0, size, BLOCK):
            keys = conv(k_pad, w_ref[1], begin)
            values = conv(v_pad, w_ref[2], begin)
            part = dot(relu16(dot_nt(map_t_ref[...], keys)), values)
            update = part if update is None else update + part
        return update

    state[...] = step(0)

    def later(i, carry):
        k_pad[:TAIL] = k_pad[size:]
        v_pad[:TAIL] = v_pad[size:]
        state[...] += step(i)
        return carry

    lax.fori_loop(1, blocks * BLOCK // size, later, 0)
    sent_ref[:features] = state[...].astype(jnp.bfloat16)


def causal_scores(feats, feats_t):
    row = lax.broadcasted_iota(jnp.int32, (BLOCK, BLOCK), 0)
    col = lax.broadcasted_iota(jnp.int32, (BLOCK, BLOCK), 1)
    return jnp.where(col <= row, dot(feats, feats_t), 0.0).astype(jnp.bfloat16)


def span_kernel(x_ref, w_ref, map_ref, map_t_ref, part_ref, feat_ref, q_pad, k_pad, v_pad, state):
    count, _, rows, _ = x_ref.shape
    blocks, size = count * rows // BLOCK, q_pad.shape[0] - TAIL
    pads = (q_pad, k_pad, v_pad)

    def step(i, members):
        for member, pad in enumerate(pads):
            fill(pad, x_ref, member, i * (size // rows), size)
        for j in members:
            block = i * (size // BLOCK) + j
            queries, keys, values = (conv(pad, w_ref[m], j * BLOCK) for m, pad in enumerate(pads))
            feats_t = relu16(dot_nt(map_t_ref[...], keys))
            feats = relu16(dot(queries, map_ref[...]))
            feat_ref[block] = feats
            carried = folded(dot(feats, high_low(state[...])))
            part_ref[block] = dot(causal_scores(feats, feats_t), values) + carried
            state[...] += dot(feats_t, values)

    state[...] = jnp.zeros_like(state)
    for pad in pads:
        pad[:TAIL] = jnp.zeros((TAIL, DH), jnp.float32)
    step(0, range(1, size // BLOCK))

    def later(i, carry):
        for pad in pads:
            pad[:TAIL] = pad[size:]
        step(i, range(size // BLOCK))
        return carry

    lax.fori_loop(1, blocks * BLOCK // size, later, 0)


def finish_kernel(
    x_ref, came_ref, w_ref, map_ref, map_t_ref, part_ref, feat_ref, gain_ref,
    out_ref, q_pad, k_pad, v_pad,
):
    blocks, _, features = feat_ref.shape
    per_block = BLOCK // out_ref.shape[1]
    gain = gain_ref[...]
    state = came_ref[:features]

    def put(begin, end, numerator):
        scale = lax.rsqrt(jnp.mean(numerator * numerator, -1, keepdims=True) + 1e-06)
        done = (numerator * scale * gain).astype(jnp.bfloat16)
        held = slice(begin * per_block, end * per_block)
        out_ref[held] = done.reshape((end - begin) * per_block, BLOCK // per_block, DH)

    pads = (q_pad, k_pad, v_pad)
    for member, pad in enumerate(pads):
        end = features + (member + 1) * RIM
        pad[:TAIL] = came_ref[end - TAIL : end].astype(jnp.float32)
        fill(pad, x_ref, member, 0, BLOCK)
    queries, keys, values = (conv(pad, w_ref[member], 0) for member, pad in enumerate(pads))
    feats_t = relu16(dot_nt(map_t_ref[...], keys))
    feats = relu16(dot(queries, map_ref[...]))
    later = high_low(state.astype(jnp.float32) + dot(feats_t, values))
    put(0, 1, dot(causal_scores(feats, feats_t), values) + dot(feats, state))
    for begin in range(1, blocks, 2):
        end = min(begin + 2, blocks)
        feats = feat_ref[begin:end].reshape((end - begin) * BLOCK, features)
        part = part_ref[begin:end].reshape((end - begin) * BLOCK, DH)
        put(begin, end, part + folded(dot(feats, later)))


LIMIT = 24 * 1024 * 1024
MOST = 60 * 1024 * 1024
VMEM = pl.BlockSpec(memory_space=pltpu.VMEM)
HBM = pl.BlockSpec(memory_space=pltpu.HBM)


def whole_call(kernel, inputs, outputs, scratch=(), flops=0, place=VMEM, limit=LIMIT):
    moved = sum(x.size * x.dtype.itemsize for x in [*inputs, *outputs])
    return pl.pallas_call(
        kernel,
        in_specs=[place] * len(inputs),
        out_specs=[VMEM] * len(outputs),
        out_shape=outputs,
        scratch_shapes=scratch,
        compiler_params=pltpu.CompilerParams(vmem_limit_bytes=limit),
        cost_estimate=pl.CostEstimate(flops=flops, bytes_accessed=moved, transcendentals=0),
    )(*inputs)


def shaped(shape, dtype=jnp.bfloat16):
    return jax.ShapeDtypeStruct(shape, dtype)


def next_span(block, spans):
    return lax.ppermute(block, "span", [(i, i + 1) for i in range(spans - 1)])


def exchange(block):
    return lax.all_to_all(block, GROUP, split_axis=0, concat_axis=0, tiled=True)


def after(value, other):
    return lax.optimization_barrier((value, other))[0]


def local(spans, query_input, key_input, value_heads_input, conv_weight, feature_map, out_gain):
    rows, model = query_input.shape
    parts, members = lax.axis_size("part"), lax.axis_size("sp")
    count = parts * members
    width = model // count
    heads, tokens, features = width // DH, count * rows, feature_map.shape[1]
    blocks = tokens // BLOCK
    starts = [
        [((d % members) * parts + d // members) * width + head * DH for d in range(count)]
        for head in range(heads)
    ]
    column = lax.axis_index("part") * width
    weights = lax.dynamic_slice_in_dim(conv_weight, column, width, 2)
    gains = lax.dynamic_slice_in_dim(out_gain, column, width, 0)[None]
    map_t = feature_map.T

    inputs = [query_input, key_input, value_heads_input]
    work = tokens * DH * features
    size = BLOCK * (2 if blocks % 2 == 0 else 1)
    wide = pltpu.VMEM((TAIL + size, DH), jnp.float32)
    narrow = pltpu.VMEM((TAIL + BLOCK, DH), jnp.float32)
    whole_state = pltpu.VMEM((features, DH), jnp.float32)
    outputs, attended = [], None
    for head in range(heads):
        cols = slice(head * DH, (head + 1) * DH)
        taps = weights[:, :, cols]
        (x,) = whole_call(
            functools.partial(pack_kernel, starts[head]),
            inputs,
            [shaped((count, 3, rows, DH))],
            [pltpu.VMEM((3, rows, model), jnp.bfloat16), pltpu.SemaphoreType.DMA((3, 4))],
            place=HBM,
            limit=MOST,
        )
        x = exchange(x)
        halo = jnp.zeros((3, RIM, DH), jnp.bfloat16)
        if spans > 2:
            halo = next_span(x[count - 1, :, rows - RIM :], spans)
        (sent,) = whole_call(
            totals_kernel,
            [x, halo, taps, map_t],
            [shaped((features + 3 * RIM, DH))],
            [wide, wide, whole_state],
            4 * work,
        )
        if spans == 2:
            came = next_span(sent, spans)
        else:
            gathered = lax.all_gather(sent[:features], "span").astype(jnp.float32)
            mine = lax.axis_index("span")
            earlier = jnp.where((jnp.arange(spans) < mine)[:, None, None], gathered, 0.0)
            state = jnp.sum(earlier, 0).astype(jnp.bfloat16)
            came = jnp.concatenate([state, halo.reshape(3 * RIM, DH)])
        if attended is not None:
            outputs.append(exchange(after(attended, sent)))
        partial, feats = whole_call(
            span_kernel,
            [x, taps, feature_map, map_t],
            [
                shaped((blocks, BLOCK, DH), jnp.float32),
                shaped((blocks, BLOCK, features)),
            ],
            [wide, wide, wide, whole_state],
            10 * work,
        )
        (attended,) = whole_call(
            finish_kernel,
            [x, came, taps, feature_map, map_t, partial, feats, gains[:, cols]],
            [shaped((count, rows, DH))],
            [narrow, narrow, narrow],
            4 * work,
        )
    outputs.append(exchange(attended))
    (result,) = whole_call(
        functools.partial(unpack_kernel, starts), outputs, [shaped((rows, model))]
    )
    return result


def solution(mesh):
    groups, members = mesh.devices.shape
    parts = 1
    while groups % (4 * parts) == 0 and H % (2 * parts * members) == 0:
        parts *= 2
    spans = groups // parts
    split = Mesh(mesh.devices.reshape(spans, parts, members), ("span", "part", "sp"))
    tokens = P(("span", "part", "sp"), None)
    placed = (tokens, tokens, tokens, P(None, None, "sp"), P(), P("sp"))
    return jax.shard_map(
        functools.partial(local, spans),
        mesh=split, in_specs=placed, out_specs=tokens, check_vma=False,
    )
```

profile of v0, /device:TPU:0, one launch (start us, length us, event | category | flops | bytes accessed | tf_op | source)
XLA Modules:
  0.0 120.5 jit_solution(5015609034388895944)
XLA Ops:
  0.0 3.1 %shard_map.64 = bf16[16,3,128,128]{3,2,1,0:T(8,128)(2,1)} custom-call(bf16[128,4096]{1,0:T(8,128)(2,1)} %refs_0_.3, bf16[128,4096]{1,0:T(8,128)(2,1)} %refs_1_.3, bf16[128,4096]{1,0:T(8,128)(2,1)} %refs_2_.3), custom_call_target="tpu_custom_call" | custom-call | bytes 4718592 | tf_op jit(solution)/shard_map/pallas_call | solution.py:192
  3.1 6.3 %all-to-all-start = ((bf16[16,3,128,128]{3,2,1,0:T(8,128)(2,1)}), bf16[16,3,128,128]{3,2,1,0:T(8,128)(2,1)S(1)}, u32[]{:S(2)}, u32[]{:S(2)}) async-start(bf16[16,3,128,128]{3,2,1,0:T(8,128)(2,1)} %shard_map.64), calls=%async_computation | async-start | bytes 3145728 | tf_op jit(solution)/shard_map/all_to_all | solution.py:212
  9.4 3.1 %shard_map.68 = bf16[16,3,128,128]{3,2,1,0:T(8,128)(2,1)} custom-call(bf16[128,4096]{1,0:T(8,128)(2,1)} %refs_0_.3, bf16[128,4096]{1,0:T(8,128)(2,1)} %refs_1_.3, bf16[128,4096]{1,0:T(8,128)(2,1)} %refs_2_.3), custom_call_target="tpu_custom_call" | custom-call | bytes 4718592 | tf_op jit(solution)/shard_map/pallas_call | solution.py:192
  12.6 0.0 copy-start
  12.6 0.0 copy-start.8
  12.6 0.0 copy-start.7
  12.6 19.6 %all-to-all-done.x_ref = bf16[16,3,128,128]{3,2,1,0:T(8,128)(2,1)S(1)} async-done(((bf16[16,3,128,128]{3,2,1,0:T(8,128)(2,1)}), bf16[16,3,128,128]{3,2,1,0:T(8,128)(2,1)S(1)}, u32[]{:S(2)}, u32[]{:S(2)}) %all-to-all-start) | async-done | bytes 1572896 | tf_op jit(solution)/shard_map/all_to_all | solution.py:212
  32.2 3.9 %all-to-all-start.1 = ((bf16[16,3,128,128]{3,2,1,0:T(8,128)(2,1)}), bf16[16,3,128,128]{3,2,1,0:T(8,128)(2,1)S(1)}, u32[]{:S(2)}, u32[]{:S(2)}) async-start(bf16[16,3,128,128]{3,2,1,0:T(8,128)(2,1)} %shard_map.68), calls=%async_computation.1 | async-start | bytes 3145728 | tf_op jit(solution)/shard_map/all_to_all | solution.py:212
  36.1 0.8 copy.7
  37.0 0.1 dynamic_slice.7
  37.1 0.9 copy-done.1
  38.0 4.3 %shard_map.65 = bf16[1072,128]{1,0:T(8,128)(2,1)} custom-call(bf16[16,3,128,128]{3,2,1,0:T(8,128)(2,1)S(1)} %all-to-all-done.x_ref, bf16[3,16,128]{2,1,0:T(8,128)(2,1)S(1)} %broadcast_1_halo_ref.2.halo_ref, f32[3,4,128]{2,1,0:T(4,128)S(1)} %get-tuple-element.16.w_ref, bf16[1024,128]{1,0:T(8,128)(2,1)S(1)} %bitcast.2), custom_call_target="tpu_custom_call" | custom-call | flops 1073741824 | bytes 2127872 | tf_op jit(solution)/shard_map/pallas_call | solution.py:192
  42.3 5.2 %collective-permute-start = (bf16[1072,128]{1,0:T(8,128)(2,1)}, bf16[1072,128]{1,0:T(8,128)(2,1)}, u32[]{:S(2)}, u32[]{:S(2)}) collective-permute-start(bf16[1072,128]{1,0:T(8,128)(2,1)} %shard_map.65), channel_id=1, source_target_pairs={{0,16},{1,17},{2,18},{3,19},{4,20},{5,21},{6,22},{7,23},{8,24},{9,... | collective-permute-start | bytes 823304 | tf_op jit(solution)/shard_map/ppermute | solution.py:208
  47.5 11.4 %all-to-all-done.1.x_ref = bf16[16,3,128,128]{3,2,1,0:T(8,128)(2,1)S(1)} async-done(((bf16[16,3,128,128]{3,2,1,0:T(8,128)(2,1)}), bf16[16,3,128,128]{3,2,1,0:T(8,128)(2,1)S(1)}, u32[]{:S(2)}, u32[]{:S(2)}) %all-to-all-start.1) | async-done | bytes 1572896 | tf_op jit(solution)/shard_map/all_to_all | solution.py:212
  58.9 0.9 copy-done.2
  59.8 3.6 %shard_map.69 = bf16[1072,128]{1,0:T(8,128)(2,1)S(1)} custom-call(bf16[16,3,128,128]{3,2,1,0:T(8,128)(2,1)S(1)} %all-to-all-done.1.x_ref, bf16[3,16,128]{2,1,0:T(8,128)(2,1)S(1)} %broadcast_1_halo_ref.2.halo_ref, f32[3,4,128]{2,1,0:T(4,128)S(1)} %get-tuple-element.15.w_ref, bf16[1024,128]{1,0:T(8,128)(2,1)S(1)} %bitcast.3), custom_call_target="tpu_custom_call" | custom-call | flops 1073741824 | bytes 2127872 | tf_op jit(solution)/shard_map/pallas_call | solution.py:192
  63.4 0.7 copy-done.6
  64.1 6.6 %shard_map.66 = (f32[8,256,128]{2,1,0:T(8,128)S(1)}, bf16[8,256,1024]{2,1,0:T(8,128)(2,1)S(1)}) custom-call(bf16[16,3,128,128]{3,2,1,0:T(8,128)(2,1)S(1)} %all-to-all-done.x_ref, f32[3,4,128]{2,1,0:T(4,128)S(1)} %get-tuple-element.16.w_ref, bf16[128,1024]{1,0:T(8,128)(2,1)S(1)} %copy-done, bf16[1024,128]{1,0:T(8,128)(2,1)S(1)} %bitcast.4), custom_call_target="tpu_custom_call" | custom-call | flops 2684354560 | bytes 7346176 | tf_op jit(solution)/shard_map/pallas_call | solution.py:192
  70.7 0.0 collective-permute-done.came_ref
  70.7 2.9 %shard_map.67 = bf16[16,128,128]{2,1,0:T(8,128)(2,1)S(1)} custom-call(bf16[16,3,128,128]{3,2,1,0:T(8,128)(2,1)S(1)} %all-to-all-done.x_ref, bf16[1072,128]{1,0:T(8,128)(2,1)} %collective-permute-done.came_ref, f32[3,4,128]{2,1,0:T(4,128)S(1)} %get-tuple-element.16.w_ref, bf16[128,1024]{1,0:T(8,128)(2,1)S(1)} %copy-done, bf16[1024,128]{1,0:T(8,128)(2,1)S(1)} %bitcast.5, ...), custom_call_target="tpu_custom_call" | custom-call | flops 1073741824 | bytes 8145408 | tf_op jit(solution)/shard_map/pallas_call | solution.py:192
  73.7 0.0 copy-start.4
  73.7 0.8 copy-done.4
  74.5 4.2 %all-to-all-start.2 = ((bf16[16,128,128]{2,1,0:T(8,128)(2,1)}), bf16[16,128,128]{2,1,0:T(8,128)(2,1)}, u32[]{:S(2)}, u32[]{:S(2)}) async-start(bf16[16,128,128]{2,1,0:T(8,128)(2,1)} %copy-done.4), calls=%async_computation.2 | async-start | bytes 1048576 | tf_op jit(solution)/shard_map/all_to_all | solution.py:212
  78.7 9.0 %collective-permute-start.1 = (bf16[1072,128]{1,0:T(8,128)(2,1)}, bf16[1072,128]{1,0:T(8,128)(2,1)S(1)}, u32[]{:S(2)}, u32[]{:S(2)}) collective-permute-start(bf16[1072,128]{1,0:T(8,128)(2,1)} %copy-done.6), channel_id=1, source_target_pairs={{0,16},{1,17},{2,18},{3,19},{4,20},{5,21},{6,22},{7,23},{8,24},{9,... | collective-permute-start | bytes 823304 | tf_op jit(solution)/shard_map/ppermute | solution.py:208
  87.7 0.9 copy-done.3
  88.6 6.6 %shard_map.70 = (f32[8,256,128]{2,1,0:T(8,128)S(1)}, bf16[8,256,1024]{2,1,0:T(8,128)(2,1)S(1)}) custom-call(bf16[16,3,128,128]{3,2,1,0:T(8,128)(2,1)S(1)} %all-to-all-done.1.x_ref, f32[3,4,128]{2,1,0:T(4,128)S(1)} %get-tuple-element.15.w_ref, bf16[128,1024]{1,0:T(8,128)(2,1)S(1)} %copy-done, bf16[1024,128]{1,0:T(8,128)(2,1)S(1)} %bitcast.6), custom_call_target="tpu_custom_call" | custom-call | flops 2684354560 | bytes 7346176 | tf_op jit(solution)/shard_map/pallas_call | solution.py:192
  95.3 0.0 collective-permute-done.1.came_ref
  95.3 2.0 %shard_map.71 = bf16[16,128,128]{2,1,0:T(8,128)(2,1)S(1)} custom-call(bf16[16,3,128,128]{3,2,1,0:T(8,128)(2,1)S(1)} %all-to-all-done.1.x_ref, bf16[1072,128]{1,0:T(8,128)(2,1)S(1)} %collective-permute-done.1.came_ref, f32[3,4,128]{2,1,0:T(4,128)S(1)} %get-tuple-element.15.w_ref, bf16[128,1024]{1,0:T(8,128)(2,1)S(1)} %copy-done, ...), custom_call_target="tpu_custom_call" | custom-call | flops 1073741824 | bytes 8145408 | tf_op jit(solution)/shard_map/pallas_call | solution.py:192
  97.3 0.8 copy-done.5
  98.1 0.0 all-to-all-done.2.refs_0_
  98.1 20.1 %all_to_all.20.refs_1_ = bf16[16,128,128]{2,1,0:T(8,128)(2,1)S(1)} all-to-all(bf16[16,128,128]{2,1,0:T(8,128)(2,1)} %copy-done.5), channel_id=1, replica_groups=mesh['span'=2,'part'=2,'sp'=8] {'part','sp'}, dimensions={0} | all-to-all | bytes 1048576 | tf_op jit(solution)/shard_map/all_to_all | solution.py:212
  118.2 2.3 %shard_map.72 = bf16[128,4096]{1,0:T(8,128)(2,1)} custom-call(bf16[16,128,128]{2,1,0:T(8,128)(2,1)} %all-to-all-done.2.refs_0_, bf16[16,128,128]{2,1,0:T(8,128)(2,1)S(1)} %all_to_all.20.refs_1_), custom_call_target="tpu_custom_call" | custom-call | bytes 2097152 | tf_op jit(solution)/shard_map/pallas_call | solution.py:192
  (11 shorter events, 0.0 us)
Async XLA Ops:
  3.1 29.1 %all-to-all-start = ((bf16[16,3,128,128]{3,2,1,0:T(8,128)(2,1)}), bf16[16,3,128,128]{3,2,1,0:T(8,128)(2,1)S(1)}, u32[]{:S(2)}, u32[]{:S(2)}) async-start(bf16[16,3,128,128]{3,2,1,0:T(8,128)(2,1)} %shard_map.64), calls=%async_computation | async-start | bytes 3145728 | tf_op jit(solution)/shard_map/all_to_all | solution.py:212
  12.6 23.6 %copy-start = (bf16[128,1024]{1,0:T(8,128)(2,1)S(1)}, bf16[128,1024]{1,0:T(8,128)(2,1)}, u32[]{:S(2)}) copy-start(bf16[128,1024]{1,0:T(8,128)(2,1)} %map_ref.7) | copy-start | bytes 786436
  12.6 24.4 %copy-start.8 = (f32[512]{0:T(512)S(1)}, f32[512]{0:T(512)}, u32[]{:S(2)}) copy-start(f32[512]{0:T(512)} %param.11) | copy-start | bytes 6148
  12.6 24.5 %copy-start.7 = (f32[3,4,512]{2,1,0:T(4,128)S(1)}, f32[3,4,512]{2,1,0:T(4,128)}, u32[]{:S(2)}) copy-start(f32[3,4,512]{2,1,0:T(4,128)} %param.9) | copy-start | bytes 73732
  32.2 26.7 %all-to-all-start.1 = ((bf16[16,3,128,128]{3,2,1,0:T(8,128)(2,1)}), bf16[16,3,128,128]{3,2,1,0:T(8,128)(2,1)S(1)}, u32[]{:S(2)}, u32[]{:S(2)}) async-start(bf16[16,3,128,128]{3,2,1,0:T(8,128)(2,1)} %shard_map.68), calls=%async_computation.1 | async-start | bytes 3145728 | tf_op jit(solution)/shard_map/all_to_all | solution.py:212
  37.1 1.0 copy-start.1
  42.3 28.5 %collective-permute-start = (bf16[1072,128]{1,0:T(8,128)(2,1)}, bf16[1072,128]{1,0:T(8,128)(2,1)}, u32[]{:S(2)}, u32[]{:S(2)}) collective-permute-start(bf16[1072,128]{1,0:T(8,128)(2,1)} %shard_map.65), channel_id=1, source_target_pairs={{0,16},{1,17},{2,18},{3,19},{4,20},{5,21},{6,22},{7,23},{8,24},{9,... | collective-permute-start | bytes 823304 | tf_op jit(solution)/shard_map/ppermute | solution.py:208
  58.9 1.0 copy-start.2
  63.4 0.7 copy-start.6
  73.7 0.8 copy-start.4
  74.5 23.6 %all-to-all-start.2 = ((bf16[16,128,128]{2,1,0:T(8,128)(2,1)}), bf16[16,128,128]{2,1,0:T(8,128)(2,1)}, u32[]{:S(2)}, u32[]{:S(2)}) async-start(bf16[16,128,128]{2,1,0:T(8,128)(2,1)} %copy-done.4), calls=%async_computation.2 | async-start | bytes 1048576 | tf_op jit(solution)/shard_map/all_to_all | solution.py:212
  78.7 16.6 %collective-permute-start.1 = (bf16[1072,128]{1,0:T(8,128)(2,1)}, bf16[1072,128]{1,0:T(8,128)(2,1)S(1)}, u32[]{:S(2)}, u32[]{:S(2)}) collective-permute-start(bf16[1072,128]{1,0:T(8,128)(2,1)} %copy-done.6), channel_id=1, source_target_pairs={{0,16},{1,17},{2,18},{3,19},{4,20},{5,21},{6,22},{7,23},{8,24},{9,... | collective-permute-start | bytes 823304 | tf_op jit(solution)/shard_map/ppermute | solution.py:208
  87.7 1.0 copy-start.3
  97.3 0.8 copy-start.5
where the time goes:
time: 121 us; the launch traced here: 120 us
  Pallas kernels  34.5 us (29%)
  waiting for transfers between devices  31 us (26%)
  starting transfers between devices  28.6 us (24%)
  blocking collectives  20.1 us (17%)
  local copies, waits for them, and re-layouts  6.06 us (5%)
    pallas_call x9, Pallas kernels, whole_call(): pl.pallas_call(kernel, in_specs=[place] * len(inputs), out_specs=[VMEM] *...  34.5 us
    all_to_all x3, waiting for transfers between devices, exchange(): return lax.all_to_all(block, GROUP, split_axis=0, concat_axis=0, tiled=True)  31 us
    all_to_all x1, blocking collectives, exchange(): return lax.all_to_all(block, GROUP, split_axis=0, concat_axis=0, tiled=True)  20.1 us
    all_to_all x3, starting transfers between devices, exchange(): return lax.all_to_all(block, GROUP, split_axis=0, concat_axis=0, tiled=True)  14.5 us
    ppermute x2, starting transfers between devices, next_span(): return lax.ppermute(block, 'span', [(i, i + 1) for i in range(spans - 1)])  14.2 us
    unnamed x19, local copies, waits for them, and re-layouts  5.98 us
  transfers between devices with their start and end apart: 5, of which 2 were waited for; matrix products, arithmetic and copies ran while one was open for 1% of the time, Pallas kernels for 22%

commit v1 on v0

--- a/solution.py
+++ b/solution.py
@@ -33,33 +33,59 @@
 
 
 def relu16(x):
-    return jnp.maximum(x, 0.0).astype(jnp.bfloat16)
+    return jnp.maximum(x.astype(jnp.bfloat16), 0)
 
 
 def pack_kernel(starts, *refs):
-    *sources, out_ref, held, sems = refs
-    width = held.shape[-1] // sems.shape[1]
-    copies = {}
-    for piece in range(sems.shape[1]):
+    *sources, out_ref, held, packed, load_sems, store_sems = refs
+    pieces = load_sems.shape[1]
+    width = held.shape[-1] // pieces
+    loads = {}
+    for piece in range(pieces):
         for member, source in enumerate(sources):
             cols = pl.ds(piece * width, width)
-            copies[piece, member] = pltpu.make_async_copy(
-                source.at[:, cols], held.at[member, :, cols], sems.at[member, piece]
+            loads[piece, member] = pltpu.make_async_copy(
+                source.at[:, cols], held.at[member, :, cols], load_sems.at[member, piece]
             )
-            copies[piece, member].start()
-    for piece in range(sems.shape[1]):
+            loads[piece, member].start()
+    stores = []
+    for piece in range(pieces):
+        owners = [owner for owner, start in enumerate(starts) if start // width == piece]
         for member in range(len(sources)):
-            copies[piece, member].wait()
-            for owner, start in enumerate(starts):
+            loads[piece, member].wait()
+            for owner in owners:
+                start = starts[owner]
+                packed[owner, member] = held[member, :, start : start + DH]
+        for owner in owners:
+            stores.append(
+                pltpu.make_async_copy(packed.at[owner], out_ref.at[owner], store_sems.at[owner])
+            )
+            stores[-1].start()
+    for store in stores:
+        store.wait()
+
+
+def pack_whole_kernel(starts, *refs):
+    *sources, out_ref = refs
+    for member, source in enumerate(sources):
+        for owner, start in enumerate(starts):
+            out_ref[owner, member] = source[:, start : start + DH]
+
+
+def unpack_kernel(starts, *refs):
+    *sources, out_ref, held, sems = refs
+    width = out_ref.shape[1] // sems.shape[0]
+    stores = []
+    for piece in range(sems.shape[0]):
+        for head, source in enumerate(sources):
+            for owner, start in enumerate(starts[head]):
                 if start // width == piece:
-                    out_ref[owner, member] = held[member, :, start : start + DH]
-
-
-def unpack_kernel(starts, *refs):
-    *sources, out_ref = refs
-    for head, source in enumerate(sources):
-        for owner, start in enumerate(starts[head]):
-            out_ref[:, start : start + DH] = source[owner]
+                    held[:, start : start + DH] = source[owner]
+        cols = pl.ds(piece * width, width)
+        stores.append(pltpu.make_async_copy(held.at[:, cols], out_ref.at[:, cols], sems.at[piece]))
+        stores[-1].start()
+    for store in stores:
+        store.wait()
 
 
 def high_low(x):
@@ -151,18 +177,23 @@
 
 def finish_kernel(
     x_ref, came_ref, w_ref, map_ref, map_t_ref, part_ref, feat_ref, gain_ref,
-    out_ref, q_pad, k_pad, v_pad,
+    out_ref, q_pad, k_pad, v_pad, done, sems,
 ):
     blocks, _, features = feat_ref.shape
     per_block = BLOCK // out_ref.shape[1]
     gain = gain_ref[...]
     state = came_ref[:features]
 
+    stores = []
+
     def put(begin, end, numerator):
         scale = lax.rsqrt(jnp.mean(numerator * numerator, -1, keepdims=True) + 1e-06)
-        done = (numerator * scale * gain).astype(jnp.bfloat16)
-        held = slice(begin * per_block, end * per_block)
-        out_ref[held] = done.reshape((end - begin) * per_block, BLOCK // per_block, DH)
+        normed = (numerator * scale * gain).astype(jnp.bfloat16)
+        first, extent = begin * per_block, (end - begin) * per_block
+        done[first : first + extent] = normed.reshape(extent, BLOCK // per_block, DH)
+        held = pl.ds(first, extent)
+        stores.append(pltpu.make_async_copy(done.at[held], out_ref.at[held], sems.at[len(stores)]))
+        stores[-1].start()
 
     pads = (q_pad, k_pad, v_pad)
     for member, pad in enumerate(pads):
@@ -179,6 +210,8 @@
         feats = feat_ref[begin:end].reshape((end - begin) * BLOCK, features)
         part = part_ref[begin:end].reshape((end - begin) * BLOCK, DH)
         put(begin, end, part + folded(dot(feats, later)))
+    for store in stores:
+        store.wait()
 
 
 LIMIT = 24 * 1024 * 1024
@@ -187,16 +220,14 @@
 HBM = pl.BlockSpec(memory_space=pltpu.HBM)
 
 
-def whole_call(kernel, inputs, outputs, scratch=(), flops=0, place=VMEM, limit=LIMIT):
-    moved = sum(x.size * x.dtype.itemsize for x in [*inputs, *outputs])
+def whole_call(kernel, inputs, outputs, scratch=(), read=VMEM, written=VMEM, limit=LIMIT):
     return pl.pallas_call(
         kernel,
-        in_specs=[place] * len(inputs),
-        out_specs=[VMEM] * len(outputs),
+        in_specs=[read] * len(inputs),
+        out_specs=[written] * len(outputs),
         out_shape=outputs,
         scratch_shapes=scratch,
         compiler_params=pltpu.CompilerParams(vmem_limit_bytes=limit),
-        cost_estimate=pl.CostEstimate(flops=flops, bytes_accessed=moved, transcendentals=0),
     )(*inputs)
 
 
@@ -233,7 +264,6 @@
     map_t = feature_map.T
 
     inputs = [query_input, key_input, value_heads_input]
-    work = tokens * DH * features
     size = BLOCK * (2 if blocks % 2 == 0 else 1)
     wide = pltpu.VMEM((TAIL + size, DH), jnp.float32)
     narrow = pltpu.VMEM((TAIL + BLOCK, DH), jnp.float32)
@@ -242,15 +272,25 @@
     for head in range(heads):
         cols = slice(head * DH, (head + 1) * DH)
         taps = weights[:, :, cols]
-        (x,) = whole_call(
-            functools.partial(pack_kernel, starts[head]),
-            inputs,
-            [shaped((count, 3, rows, DH))],
-            [pltpu.VMEM((3, rows, model), jnp.bfloat16), pltpu.SemaphoreType.DMA((3, 4))],
-            place=HBM,
-            limit=MOST,
-        )
+        packed = shaped((count, 3, rows, DH))
+        if head == 0:
+            (x,) = whole_call(
+                functools.partial(pack_kernel, starts[head]),
+                inputs,
+                [packed],
+                [
+                    pltpu.VMEM((3, rows, model), jnp.bfloat16),
+                    pltpu.VMEM(packed.shape, packed.dtype),
+                    pltpu.SemaphoreType.DMA((3, 4)),
+                    pltpu.SemaphoreType.DMA((count,)),
+                ],
+                read=HBM, written=HBM, limit=MOST,
+            )
+        else:
+            (x,) = whole_call(functools.partial(pack_whole_kernel, starts[head]), inputs, [packed])
         x = exchange(x)
+        if attended is not None:
+            x = after(x, attended)
         halo = jnp.zeros((3, RIM, DH), jnp.bfloat16)
         if spans > 2:
             halo = next_span(x[count - 1, :, rows - RIM :], spans)
@@ -259,7 +299,6 @@
             [x, halo, taps, map_t],
             [shaped((features + 3 * RIM, DH))],
             [wide, wide, whole_state],
-            4 * work,
         )
         if spans == 2:
             came = next_span(sent, spans)
@@ -279,18 +318,25 @@
                 shaped((blocks, BLOCK, features)),
             ],
             [wide, wide, wide, whole_state],
-            10 * work,
         )
         (attended,) = whole_call(
             finish_kernel,
             [x, came, taps, feature_map, map_t, partial, feats, gains[:, cols]],
             [shaped((count, rows, DH))],
-            [narrow, narrow, narrow],
-            4 * work,
+            [
+                narrow, narrow, narrow,
+                pltpu.VMEM((count, rows, DH), jnp.bfloat16),
+                pltpu.SemaphoreType.DMA((blocks // 2 + 1,)),
+            ],
+            written=HBM,
         )
     outputs.append(exchange(attended))
     (result,) = whole_call(
-        functools.partial(unpack_kernel, starts), outputs, [shaped((rows, model))]
+        functools.partial(unpack_kernel, starts),
+        outputs,
+        [shaped((rows, model))],
+        [pltpu.VMEM((rows, model), jnp.bfloat16), pltpu.SemaphoreType.DMA((4,))],
+        written=HBM,
     )
     return result
 

time: 121 us -> 115 us (0.950)
  waiting for transfers between devices: 31 us -> 26.2 us
  starting transfers between devices: 28.6 us -> 24.7 us
  local copies, waits for them, and re-layouts: 6.06 us -> 7.6 us
    all_to_all x3, waiting for transfers between devices: 31 us -> 17.7 us  [exchange(): return lax.all_to_all(block, GROUP, split_axis=0, concat_axis=0, tiled=True)]
    ppermute x2, waiting for transfers between devices: 0.01 us -> 8.57 us  [next_span(): return lax.ppermute(block, 'span', [(i, i + 1) for i in range(spans - 1)])]
    ppermute x2, starting transfers between devices: 14.2 us -> 9.99 us  [next_span(): return lax.ppermute(block, 'span', [(i, i + 1) for i in range(spans - 1)])]
    unnamed x19 -> x21, local copies, waits for them, and re-layouts: 5.98 us -> 7.5 us
  transfers between devices with their start and end apart: 5 -> 5, of which waited for: 2 -> 3; matrix products, arithmetic and copies ran while one was open for 1% -> 1% of each run, Pallas kernels for 22% -> 23%
where the time goes in v1:
time: 115 us
  Pallas kernels  35.3 us (31%)
  waiting for transfers between devices  26.2 us (23%)
  starting transfers between devices  24.7 us (21%)
  blocking collectives  20.6 us (18%)
  local copies, waits for them, and re-layouts  7.6 us (7%)
    pallas_call x9, Pallas kernels, whole_call(): pl.pallas_call(kernel, in_specs=[read] * len(inputs), out_specs=[written]...  35.3 us
    all_to_all x1, blocking collectives, exchange(): return lax.all_to_all(block, GROUP, split_axis=0, concat_axis=0, tiled=True)  20.6 us
    all_to_all x3, waiting for transfers between devices, exchange(): return lax.all_to_all(block, GROUP, split_axis=0, concat_axis=0, tiled=True)  17.7 us
    all_to_all x3, starting transfers between devices, exchange(): return lax.all_to_all(block, GROUP, split_axis=0, concat_axis=0, tiled=True)  14.7 us
    ppermute x2, starting transfers between devices, next_span(): return lax.ppermute(block, 'span', [(i, i + 1) for i in range(spans - 1)])  9.99 us
    ppermute x2, waiting for transfers between devices, next_span(): return lax.ppermute(block, 'span', [(i, i + 1) for i in range(spans - 1)])  8.57 us
    unnamed x21, local copies, waits for them, and re-layouts  7.5 us
  transfers between devices with their start and end apart: 5, of which 3 were waited for; matrix products, arithmetic and copies ran while one was open for 1% of the time, Pallas kernels for 23%

profile of v1, /device:TPU:0, one launch (start us, length us, event | category | flops | bytes accessed | tf_op | source)
XLA Modules:
  0.0 114.8 jit_solution(14196509314685677587)
XLA Ops:
  0.0 2.8 %shard_map.64 = bf16[16,3,128,128]{3,2,1,0:T(8,128)(2,1)} custom-call(bf16[128,4096]{1,0:T(8,128)(2,1)} %refs_0_.3, bf16[128,4096]{1,0:T(8,128)(2,1)} %refs_1_.3, bf16[128,4096]{1,0:T(8,128)(2,1)} %refs_2_.3), custom_call_target="tpu_custom_call" | custom-call | tf_op jit(solution)/shard_map/pallas_call | solution.py:224
  2.8 6.3 %all-to-all-start = ((bf16[16,3,128,128]{3,2,1,0:T(8,128)(2,1)}), bf16[16,3,128,128]{3,2,1,0:T(8,128)(2,1)S(1)}, u32[]{:S(2)}, u32[]{:S(2)}) async-start(bf16[16,3,128,128]{3,2,1,0:T(8,128)(2,1)} %shard_map.64), calls=%async_computation | async-start | bytes 3145728 | tf_op jit(solution)/shard_map/all_to_all | solution.py:243
  9.2 0.0 copy-start.3
  9.2 1.2 %copy-done.3 = bf16[128,4096]{1,0:T(8,128)(2,1)S(1)} copy-done((bf16[128,4096]{1,0:T(8,128)(2,1)S(1)}, bf16[128,4096]{1,0:T(8,128)(2,1)}, u32[]{:S(2)}) %copy-start.3) | copy-done | bytes 1048600
  10.4 1.2 %copy-done.4 = bf16[128,4096]{1,0:T(8,128)(2,1)S(1)} copy-done((bf16[128,4096]{1,0:T(8,128)(2,1)S(1)}, bf16[128,4096]{1,0:T(8,128)(2,1)}, u32[]{:S(2)}) %copy-start.4) | copy-done | bytes 1048600
  11.6 1.2 %copy-done.5 = bf16[128,4096]{1,0:T(8,128)(2,1)S(1)} copy-done((bf16[128,4096]{1,0:T(8,128)(2,1)S(1)}, bf16[128,4096]{1,0:T(8,128)(2,1)}, u32[]{:S(2)}) %copy-start.5) | copy-done | bytes 1048600
  12.8 0.3 shard_map.68
  13.1 1.1 copy-done.2
  14.2 17.7 %all-to-all-done.x_ref = bf16[16,3,128,128]{3,2,1,0:T(8,128)(2,1)S(1)} async-done(((bf16[16,3,128,128]{3,2,1,0:T(8,128)(2,1)}), bf16[16,3,128,128]{3,2,1,0:T(8,128)(2,1)S(1)}, u32[]{:S(2)}, u32[]{:S(2)}) %all-to-all-start) | async-done | bytes 1572896 | tf_op jit(solution)/shard_map/all_to_all | solution.py:243
  31.9 3.9 %all-to-all-start.1 = ((bf16[16,3,128,128]{3,2,1,0:T(8,128)(2,1)}), bf16[16,3,128,128]{3,2,1,0:T(8,128)(2,1)S(1)}, u32[]{:S(2)}, u32[]{:S(2)}) async-start(bf16[16,3,128,128]{3,2,1,0:T(8,128)(2,1)} %copy-done.2), calls=%async_computation.1 | async-start | bytes 3145728 | tf_op jit(solution)/shard_map/all_to_all | solution.py:243
  35.8 0.0 copy-start.9
  35.9 1.1 copy.7
  37.0 0.0 copy-start
  37.0 3.6 %shard_map.65 = bf16[1072,128]{1,0:T(8,128)(2,1)S(1)} custom-call(bf16[16,3,128,128]{3,2,1,0:T(8,128)(2,1)S(1)} %all-to-all-done.x_ref, bf16[3,16,128]{2,1,0:T(8,128)(2,1)S(1)} %broadcast_1_halo_ref.2.halo_ref, f32[3,4,128]{2,1,0:T(4,128)S(1)} %get-tuple-element.18.w_ref, bf16[1024,128]{1,0:T(8,128)(2,1)S(1)} %bitcast.2), custom_call_target="tpu_custom_call" | custom-call | tf_op jit(solution)/shard_map/pallas_call | solution.py:224
  40.6 4.5 %collective-permute-start = (bf16[1072,128]{1,0:T(8,128)(2,1)S(1)}, bf16[1072,128]{1,0:T(8,128)(2,1)S(1)}, u32[]{:S(2)}, u32[]{:S(2)}) collective-permute-start(bf16[1072,128]{1,0:T(8,128)(2,1)S(1)} %shard_map.65), channel_id=1, source_target_pairs={{0,16},{1,17},{2,18},{3,19},{4,20},{5,21},{6,22},{7,23},{8,24},{9,... | collective-permute-start | bytes 823304 | tf_op jit(solution)/shard_map/ppermute | solution.py:239
  45.2 0.1 dynamic_slice.7
  45.2 6.6 %shard_map.66 = (f32[8,256,128]{2,1,0:T(8,128)S(1)}, bf16[8,256,1024]{2,1,0:T(8,128)(2,1)S(1)}) custom-call(bf16[16,3,128,128]{3,2,1,0:T(8,128)(2,1)S(1)} %all-to-all-done.x_ref, f32[3,4,128]{2,1,0:T(4,128)S(1)} %get-tuple-element.18.w_ref, bf16[128,1024]{1,0:T(8,128)(2,1)S(1)} %copy-done, bf16[1024,128]{1,0:T(8,128)(2,1)S(1)} %bitcast.3), custom_call_target="tpu_custom_call" | custom-call | tf_op jit(solution)/shard_map/pallas_call | solution.py:224
  51.9 8.1 %collective-permute-done.came_ref = bf16[1072,128]{1,0:T(8,128)(2,1)S(1)} collective-permute-done((bf16[1072,128]{1,0:T(8,128)(2,1)S(1)}, bf16[1072,128]{1,0:T(8,128)(2,1)S(1)}, u32[]{:S(2)}, u32[]{:S(2)}) %collective-permute-start) | collective-permute-done | bytes 274464 | tf_op jit(solution)/shard_map/ppermute | solution.py:239
  60.0 4.5 %shard_map.67 = bf16[16,128,128]{2,1,0:T(8,128)(2,1)S(1)} custom-call(bf16[16,3,128,128]{3,2,1,0:T(8,128)(2,1)S(1)} %all-to-all-done.x_ref, bf16[1072,128]{1,0:T(8,128)(2,1)S(1)} %collective-permute-done.came_ref, f32[3,4,128]{2,1,0:T(4,128)S(1)} %get-tuple-element.18.w_ref, bf16[128,1024]{1,0:T(8,128)(2,1)S(1)} %copy-done, bf16[1024,128]{1,0:T(8,128)(2,1)S(1)} %bitcast.4, ...), custom_call_target="tpu_custom_call" | custom-call | tf_op jit(solution)/shard_map/pallas_call | solution.py:224
  64.4 0.0 copy-start.6
  64.5 0.8 copy-done.6
  65.2 0.0 all-to-all-done.1.x_ref
  65.2 4.3 %shard_map.69 = bf16[1072,128]{1,0:T(8,128)(2,1)} custom-call(bf16[16,3,128,128]{3,2,1,0:T(8,128)(2,1)S(1)} %all-to-all-done.1.x_ref, bf16[3,16,128]{2,1,0:T(8,128)(2,1)S(1)} %broadcast_1_halo_ref.2.halo_ref, f32[3,4,128]{2,1,0:T(4,128)S(1)} %get-tuple-element.17.w_ref, bf16[1024,128]{1,0:T(8,128)(2,1)S(1)} %bitcast.5), custom_call_target="tpu_custom_call" | custom-call | tf_op jit(solution)/shard_map/pallas_call | solution.py:224
  69.6 4.5 %all-to-all-start.2 = ((bf16[16,128,128]{2,1,0:T(8,128)(2,1)}), bf16[16,128,128]{2,1,0:T(8,128)(2,1)}, u32[]{:S(2)}, u32[]{:S(2)}) async-start(bf16[16,128,128]{2,1,0:T(8,128)(2,1)} %copy-done.6), calls=%async_computation.2 | async-start | bytes 1048576 | tf_op jit(solution)/shard_map/all_to_all | solution.py:243
  74.0 5.5 %collective-permute-start.1 = (bf16[1072,128]{1,0:T(8,128)(2,1)}, bf16[1072,128]{1,0:T(8,128)(2,1)S(1)}, u32[]{:S(2)}, u32[]{:S(2)}) collective-permute-start(bf16[1072,128]{1,0:T(8,128)(2,1)} %shard_map.69), channel_id=1, source_target_pairs={{0,16},{1,17},{2,18},{3,19},{4,20},{5,21},{6,22},{7,23},{8,24},{9,... | collective-permute-start | bytes 823304 | tf_op jit(solution)/shard_map/ppermute | solution.py:239
  79.6 6.6 %shard_map.70 = (f32[8,256,128]{2,1,0:T(8,128)S(1)}, bf16[8,256,1024]{2,1,0:T(8,128)(2,1)S(1)}) custom-call(bf16[16,3,128,128]{3,2,1,0:T(8,128)(2,1)S(1)} %all-to-all-done.1.x_ref, f32[3,4,128]{2,1,0:T(4,128)S(1)} %get-tuple-element.17.w_ref, bf16[128,1024]{1,0:T(8,128)(2,1)S(1)} %copy-done.1, bf16[1024,128]{1,0:T(8,128)(2,1)S(1)} %bitcast.6), custom_call_target="tpu_custom_call" | custom-call | tf_op jit(solution)/shard_map/pallas_call | solution.py:224
  86.2 0.5 collective-permute-done.1.came_ref
  86.7 4.5 %shard_map.71 = bf16[16,128,128]{2,1,0:T(8,128)(2,1)S(1)} custom-call(bf16[16,3,128,128]{3,2,1,0:T(8,128)(2,1)S(1)} %all-to-all-done.1.x_ref, bf16[1072,128]{1,0:T(8,128)(2,1)S(1)} %collective-permute-done.1.came_ref, f32[3,4,128]{2,1,0:T(4,128)S(1)} %get-tuple-element.17.w_ref, bf16[128,1024]{1,0:T(8,128)(2,1)S(1)} %copy-done.1, ...), custom_call_target="tpu_custom_call" | custom-call | tf_op jit(solution)/shard_map/pallas_call | solution.py:224
  91.1 0.8 copy-done.7
  91.9 0.0 all-to-all-done.2.refs_0_
  91.9 20.6 %all_to_all.20.refs_1_ = bf16[16,128,128]{2,1,0:T(8,128)(2,1)S(1)} all-to-all(bf16[16,128,128]{2,1,0:T(8,128)(2,1)} %copy-done.7), channel_id=1, replica_groups=mesh['span'=2,'part'=2,'sp'=8] {'part','sp'}, dimensions={0} | all-to-all | bytes 1048576 | tf_op jit(solution)/shard_map/all_to_all | solution.py:243
  112.5 2.1 %shard_map.72 = bf16[128,4096]{1,0:T(8,128)(2,1)} custom-call(bf16[16,128,128]{2,1,0:T(8,128)(2,1)} %all-to-all-done.2.refs_0_, bf16[16,128,128]{2,1,0:T(8,128)(2,1)S(1)} %all_to_all.20.refs_1_), custom_call_target="tpu_custom_call" | custom-call | tf_op jit(solution)/shard_map/pallas_call | solution.py:224
  (13 shorter events, 0.0 us)
Async XLA Ops:
  2.8 29.1 %all-to-all-start = ((bf16[16,3,128,128]{3,2,1,0:T(8,128)(2,1)}), bf16[16,3,128,128]{3,2,1,0:T(8,128)(2,1)S(1)}, u32[]{:S(2)}, u32[]{:S(2)}) async-start(bf16[16,3,128,128]{3,2,1,0:T(8,128)(2,1)} %shard_map.64), calls=%async_computation | async-start | bytes 3145728 | tf_op jit(solution)/shard_map/all_to_all | solution.py:243
  9.2 1.2 %copy-start.3 = (bf16[128,4096]{1,0:T(8,128)(2,1)S(1)}, bf16[128,4096]{1,0:T(8,128)(2,1)}, u32[]{:S(2)}) copy-start(bf16[128,4096]{1,0:T(8,128)(2,1)} %refs_0_.3) | copy-start | bytes 3145732
  10.4 1.2 %copy-start.4 = (bf16[128,4096]{1,0:T(8,128)(2,1)S(1)}, bf16[128,4096]{1,0:T(8,128)(2,1)}, u32[]{:S(2)}) copy-start(bf16[128,4096]{1,0:T(8,128)(2,1)} %refs_1_.3) | copy-start | bytes 3145732
  11.6 1.2 %copy-start.5 = (bf16[128,4096]{1,0:T(8,128)(2,1)S(1)}, bf16[128,4096]{1,0:T(8,128)(2,1)}, u32[]{:S(2)}) copy-start(bf16[128,4096]{1,0:T(8,128)(2,1)} %refs_2_.3) | copy-start | bytes 3145732
  13.1 1.1 copy-start.2
  14.2 22.7 %copy-start.8 = (f32[3,4,512]{2,1,0:T(4,128)S(1)}, f32[3,4,512]{2,1,0:T(4,128)}, u32[]{:S(2)}) copy-start(f32[3,4,512]{2,1,0:T(4,128)} %param.9) | copy-start | bytes 73732
  31.9 33.3 %all-to-all-start.1 = ((bf16[16,3,128,128]{3,2,1,0:T(8,128)(2,1)}), bf16[16,3,128,128]{3,2,1,0:T(8,128)(2,1)S(1)}, u32[]{:S(2)}, u32[]{:S(2)}) async-start(bf16[16,3,128,128]{3,2,1,0:T(8,128)(2,1)} %copy-done.2), calls=%async_computation.1 | async-start | bytes 3145728 | tf_op jit(solution)/shard_map/all_to_all | solution.py:243
  35.8 9.3 %copy-start.9 = (f32[512]{0:T(512)S(1)}, f32[512]{0:T(512)}, u32[]{:S(2)}) copy-start(f32[512]{0:T(512)} %param.11) | copy-start | bytes 6148
  37.0 8.2 %copy-start = (bf16[128,1024]{1,0:T(8,128)(2,1)S(1)}, bf16[128,1024]{1,0:T(8,128)(2,1)}, u32[]{:S(2)}) copy-start(bf16[128,1024]{1,0:T(8,128)(2,1)} %map_ref.7) | copy-start | bytes 786436
  40.6 19.4 %collective-permute-start = (bf16[1072,128]{1,0:T(8,128)(2,1)S(1)}, bf16[1072,128]{1,0:T(8,128)(2,1)S(1)}, u32[]{:S(2)}, u32[]{:S(2)}) collective-permute-start(bf16[1072,128]{1,0:T(8,128)(2,1)S(1)} %shard_map.65), channel_id=1, source_target_pairs={{0,16},{1,17},{2,18},{3,19},{4,20},{5,21},{6,22},{7,23},{8,24},{9,... | collective-permute-start | bytes 823304 | tf_op jit(solution)/shard_map/ppermute | solution.py:239
  64.4 0.8 copy-start.6
  65.2 14.3 %copy-start.1 = (bf16[128,1024]{1,0:T(8,128)(2,1)S(1)}, bf16[128,1024]{1,0:T(8,128)(2,1)}, u32[]{:S(2)}) copy-start(bf16[128,1024]{1,0:T(8,128)(2,1)} %map_ref.7) | copy-start | bytes 786436
  69.6 22.4 %all-to-all-start.2 = ((bf16[16,128,128]{2,1,0:T(8,128)(2,1)}), bf16[16,128,128]{2,1,0:T(8,128)(2,1)}, u32[]{:S(2)}, u32[]{:S(2)}) async-start(bf16[16,128,128]{2,1,0:T(8,128)(2,1)} %copy-done.6), calls=%async_computation.2 | async-start | bytes 1048576 | tf_op jit(solution)/shard_map/all_to_all | solution.py:243
  74.0 12.6 %collective-permute-start.1 = (bf16[1072,128]{1,0:T(8,128)(2,1)}, bf16[1072,128]{1,0:T(8,128)(2,1)S(1)}, u32[]{:S(2)}, u32[]{:S(2)}) collective-permute-start(bf16[1072,128]{1,0:T(8,128)(2,1)} %shard_map.69), channel_id=1, source_target_pairs={{0,16},{1,17},{2,18},{3,19},{4,20},{5,21},{6,22},{7,23},{8,24},{9,... | collective-permute-start | bytes 823304 | tf_op jit(solution)/shard_map/ppermute | solution.py:239
  91.1 0.8 copy-start.7

commit v2 on v1

v2 whole, which is shorter than its diff:
```python
import functools

import jax
import jax.numpy as jnp
from jax import lax
from jax.experimental import pallas as pl
from jax.experimental.pallas import tpu as pltpu
from jax.sharding import Mesh
from jax.sharding import PartitionSpec as P

H = 32
DH = 128
BLOCK = 256
TAIL = 8
RIM = 16
GROUP = ("part", "sp")


def dot(a, b):
    return jnp.dot(a, b, preferred_element_type=jnp.float32)


def dot_nt(a, b):
    return lax.dot_general(a, b, (((1,), (1,)), ((), ())), preferred_element_type=jnp.float32)


def conv(pad_ref, weights, begin):
    total = jnp.zeros((BLOCK, pad_ref.shape[1]), jnp.float32)
    for tap in range(weights.shape[0]):
        row = TAIL + begin - tap
        total = total + weights[tap][None, :] * pad_ref[row : row + BLOCK]
    return total.astype(jnp.bfloat16)


def relu16(x):
    return jnp.maximum(x.astype(jnp.bfloat16), 0)


def pack_kernel(starts, *refs):
    *sources, out_ref, held, packed, load_sems, store_sems = refs
    pieces = load_sems.shape[1]
    width = held.shape[-1] // pieces
    loads = {}
    for piece in range(pieces):
        for member, source in enumerate(sources):
            cols = pl.ds(piece * width, width)
            loads[piece, member] = pltpu.make_async_copy(
                source.at[:, cols], held.at[member, :, cols], load_sems.at[member, piece]
            )
            loads[piece, member].start()
    stores = []
    for piece in range(pieces):
        owners = [owner for owner, start in enumerate(starts) if start // width == piece]
        for member in range(len(sources)):
            loads[piece, member].wait()
            for owner in owners:
                start = starts[owner]
                packed[owner, member] = held[member, :, start : start + DH]
        for owner in owners:
            stores.append(
                pltpu.make_async_copy(packed.at[owner], out_ref.at[owner], store_sems.at[owner])
            )
            stores[-1].start()
    for store in stores:
        store.wait()


def pack_whole_kernel(starts, *refs):
    *sources, out_ref = refs
    for member, source in enumerate(sources):
        for owner, start in enumerate(starts):
            out_ref[owner, member] = source[:, start : start + DH]


def unpack_kernel(x_ref, out_ref):
    parts, members, heads, _, _ = x_ref.shape
    for member in range(members):
        for part in range(parts):
            for head in range(heads):
                start = ((member * parts + part) * heads + head) * DH
                out_ref[:, start : start + DH] = x_ref[part, member, head]


def high_low(x):
    high = x.astype(jnp.bfloat16)
    return jnp.concatenate([high, (x - high.astype(jnp.float32)).astype(jnp.bfloat16)], 1)


def folded(x):
    return x[:, :DH] + x[:, DH:]


def fill(pad_ref, held):
    count = pad_ref.shape[0] - TAIL
    pad_ref[TAIL:] = held.reshape(count, DH).astype(jnp.float32)


def carry_tail(pads, first, halo):
    for member, pad in enumerate(pads):
        count = pad.shape[0] - TAIL

        @pl.when(first)
        def _(pad=pad, member=member):
            pad[:TAIL] = halo(member)

        @pl.when(jnp.logical_not(first))
        def _(pad=pad, count=count):
            pad[:TAIL] = pad[count:]


def totals_kernel(k_ref, v_ref, rim_ref, halo_ref, w_ref, map_t_ref, sent_ref, k_pad, v_pad, state):
    rows, features = k_ref.shape[2], map_t_ref.shape[0]
    size = k_pad.shape[0] - TAIL
    first = pl.program_id(0) == 0
    carry_tail(
        (k_pad, v_pad), first,
        lambda member: halo_ref[member + 1, RIM - TAIL :].astype(jnp.float32),
    )
    fill(k_pad, k_ref[...])
    fill(v_pad, v_ref[...])

    @pl.when(first)
    def _():
        state[...] = jnp.zeros_like(state)

    for begin in range(0, size, BLOCK):
        keys = conv(k_pad, w_ref[1], begin)
        values = conv(v_pad, w_ref[2], begin)
        state[...] += dot(relu16(dot_nt(map_t_ref[...], keys)), values)

    @pl.when(pl.program_id(0) == pl.num_programs(0) - 1)
    def _():
        sent_ref[:features] = state[...].astype(jnp.bfloat16)
        for member in range(3):
            held = slice(features + member * RIM, features + (member + 1) * RIM)
            sent_ref[held] = rim_ref[0, member, rows - RIM :]


def causal_scores(feats, feats_t):
    row = lax.broadcasted_iota(jnp.int32, (BLOCK, BLOCK), 0)
    col = lax.broadcasted_iota(jnp.int32, (BLOCK, BLOCK), 1)
    return jnp.where(col <= row, dot(feats, feats_t), 0.0).astype(jnp.bfloat16)


def span_kernel(x_ref, w_ref, map_ref, map_t_ref, part_ref, feat_ref, q_pad, k_pad, v_pad, state):
    first = pl.program_id(0) == 0
    pads = (q_pad, k_pad, v_pad)
    carry_tail(pads, first, lambda member: jnp.zeros((TAIL, DH), jnp.float32))
    for member, pad in enumerate(pads):
        fill(pad, x_ref[:, member])

    def one(j):
        queries, keys, values = (conv(pad, w_ref[m], j * BLOCK) for m, pad in enumerate(pads))
        feats_t = relu16(dot_nt(map_t_ref[...], keys))
        feats = relu16(dot(queries, map_ref[...]))
        feat_ref[j] = feats
        carried = folded(dot(feats, high_low(state[...])))
        part_ref[j] = dot(causal_scores(feats, feats_t), values) + carried
        state[...] += dot(feats_t, values)

    @pl.when(first)
    def _():
        state[...] = jnp.zeros_like(state)

    @pl.when(jnp.logical_not(first))
    def _():
        one(0)

    for j in range(1, part_ref.shape[0]):
        one(j)


def finish_kernel(
    x_ref, came_ref, w_ref, map_ref, map_t_ref, part_ref, feat_ref, gain_ref, *refs
):
    *others, out_ref, q_pad, k_pad, v_pad, later = refs
    blocks, _, features = feat_ref.shape
    per_block = BLOCK // out_ref.shape[2]
    gain = gain_ref[...]
    first = pl.program_id(0) == 0
    for place, other in enumerate(others):
        out_ref[:, place] = other[:, 0]

    def put(begin, end, numerator):
        scale = lax.rsqrt(jnp.mean(numerator * numerator, -1, keepdims=True) + 1e-06)
        normed = (numerator * scale * gain).astype(jnp.bfloat16)
        held = slice(begin * per_block, end * per_block)
        extent = (end - begin) * per_block
        out_ref[held, len(others)] = normed.reshape(extent, BLOCK // per_block, DH)

    def rest(begin):
        extent = (blocks - begin) * BLOCK
        feats = feat_ref[begin:].reshape(extent, features)
        put(begin, blocks, part_ref[begin:].reshape(extent, DH) + folded(dot(feats, later[...])))

    @pl.when(first)
    def _():
        state = came_ref[:features]
        pads = (q_pad, k_pad, v_pad)
        for member, pad in enumerate(pads):
            end = features + (member + 1) * RIM
            pad[:TAIL] = came_ref[end - TAIL : end].astype(jnp.float32)
            fill(pad, x_ref[:, member])
        queries, keys, values = (conv(pad, w_ref[member], 0) for member, pad in enumerate(pads))
        feats_t = relu16(dot_nt(map_t_ref[...], keys))
        feats = relu16(dot(queries, map_ref[...]))
        later[...] = high_low(state.astype(jnp.float32) + dot(feats_t, values))
        put(0, 1, dot(causal_scores(feats, feats_t), values) + dot(feats, state))
        if blocks > 1:
            rest(1)

    @pl.when(jnp.logical_not(first))
    def _():
        rest(0)


LIMIT = 24 * 1024 * 1024
MOST = 60 * 1024 * 1024
VMEM = pl.BlockSpec(memory_space=pltpu.VMEM)
HBM = pl.BlockSpec(memory_space=pltpu.HBM)


COST = pl.CostEstimate(flops=1000, bytes_accessed=1000, transcendentals=0)
GRID = pltpu.CompilerParams(dimension_semantics=("arbitrary",), vmem_limit_bytes=LIMIT)


def whole_call(kernel, inputs, outputs, scratch=(), read=VMEM, written=VMEM, limit=LIMIT):
    return pl.pallas_call(
        kernel,
        in_specs=[read] * len(inputs),
        out_specs=[written] * len(outputs),
        out_shape=outputs,
        scratch_shapes=scratch,
        compiler_params=pltpu.CompilerParams(vmem_limit_bytes=limit),
        cost_estimate=COST,
    )(*inputs)


def stepped(kernel, steps, inputs, specs, out_specs, outputs, scratch):
    return pl.pallas_call(
        kernel,
        grid=(steps,),
        in_specs=specs,
        out_specs=out_specs,
        out_shape=outputs,
        scratch_shapes=scratch,
        compiler_params=GRID,
        cost_estimate=COST,
    )(*inputs)


def whole(array):
    zeros = (0,) * array.ndim
    return pl.BlockSpec(array.shape, lambda i: zeros)


def leading(*shape):
    zeros = (0,) * (len(shape) - 1)
    return pl.BlockSpec(shape, lambda i: (i, *zeros))


def shaped(shape, dtype=jnp.bfloat16):
    return jax.ShapeDtypeStruct(shape, dtype)


def next_span(block, spans):
    return lax.ppermute(block, "span", [(i, i + 1) for i in range(spans - 1)])


def exchange(block):
    return lax.all_to_all(block, GROUP, split_axis=0, concat_axis=0, tiled=True)


def after(value, other):
    return lax.optimization_barrier((value, other))[0]


def local(spans, query_input, key_input, value_heads_input, conv_weight, feature_map, out_gain):
    rows, model = query_input.shape
    parts, members = lax.axis_size("part"), lax.axis_size("sp")
    count = parts * members
    width = model // count
    heads, tokens, features = width // DH, count * rows, feature_map.shape[1]
    blocks = tokens // BLOCK
    starts = [
        [((d % members) * parts + d // members) * width + head * DH for d in range(count)]
        for head in range(heads)
    ]
    column = lax.axis_index("part") * width
    weights = lax.dynamic_slice_in_dim(conv_weight, column, width, 2)
    gains = lax.dynamic_slice_in_dim(out_gain, column, width, 0)[None]
    map_t = feature_map.T

    inputs = [query_input, key_input, value_heads_input]
    size = BLOCK * (2 if blocks % 2 == 0 else 1)
    wide = pltpu.VMEM((TAIL + size, DH), jnp.float32)
    narrow = pltpu.VMEM((TAIL + BLOCK, DH), jnp.float32)
    whole_state = pltpu.VMEM((features, DH), jnp.float32)
    chunks = size // rows
    xs, sents, spans_done = [], [], []
    for head in range(heads):
        taps = weights[:, :, head * DH : (head + 1) * DH]
        packed = shaped((count, 3, rows, DH))
        if head == 0:
            (x,) = whole_call(
                functools.partial(pack_kernel, starts[head]),
                inputs,
                [packed],
                [
                    pltpu.VMEM((3, rows, model), jnp.bfloat16),
                    pltpu.VMEM(packed.shape, packed.dtype),
                    pltpu.SemaphoreType.DMA((3, 4)),
                    pltpu.SemaphoreType.DMA((count,)),
                ],
                read=HBM, written=HBM, limit=MOST,
            )
        else:
            (x,) = whole_call(functools.partial(pack_whole_kernel, starts[head]), inputs, [packed])
        x = exchange(x)
        if spans_done:
            x = after(x, spans_done[-1][1])
        halo = jnp.zeros((3, RIM, DH), jnp.bfloat16)
        if spans > 2:
            halo = next_span(x[count - 1, :, rows - RIM :], spans)
        big = chunks * (2 if count % (2 * chunks) == 0 else 1)
        tall = pltpu.VMEM((TAIL + big * rows, DH), jnp.float32)
        sent = stepped(
            totals_kernel,
            count // big,
            [x, x, x, halo, taps, map_t],
            [
                pl.BlockSpec((big, 1, rows, DH), lambda i: (i, 1, 0, 0)),
                pl.BlockSpec((big, 1, rows, DH), lambda i: (i, 2, 0, 0)),
                pl.BlockSpec((1, 3, rows, DH), lambda i: (count - 1, 0, 0, 0)),
                whole(halo), whole(taps), whole(map_t),
            ],
            pl.BlockSpec((features + 3 * RIM, DH), lambda i: (0, 0)),
            shaped((features + 3 * RIM, DH)),
            [tall, tall, whole_state],
        )
        if spans == 2:
            came = next_span(sent, spans)
        else:
            gathered = lax.all_gather(sent[:features], "span").astype(jnp.float32)
            mine = lax.axis_index("span")
            earlier = jnp.where((jnp.arange(spans) < mine)[:, None, None], gathered, 0.0)
            state = jnp.sum(earlier, 0).astype(jnp.bfloat16)
            came = jnp.concatenate([state, halo.reshape(3 * RIM, DH)])
        done = stepped(
            span_kernel,
            count // chunks,
            [x, taps, feature_map, map_t],
            [leading(chunks, 3, rows, DH), whole(taps), whole(feature_map), whole(map_t)],
            [leading(size // BLOCK, BLOCK, DH), leading(size // BLOCK, BLOCK, features)],
            [
                shaped((blocks, BLOCK, DH), jnp.float32),
                shaped((blocks, BLOCK, features)),
            ],
            [wide, wide, wide, whole_state],
        )
        xs.append((x, came, taps))
        sents.append(sent)
        spans_done.append(done)

    attended = []
    for head in range(heads):
        x, came, taps = xs[head]
        partial, feats = spans_done[head]
        gain = gains[:, head * DH : (head + 1) * DH]
        if head < heads - 1:
            gain = after(gain, sents[-1])
        others = attended if head == heads - 1 else []
        piece = shaped((count, len(others) + 1, rows, DH))
        out = stepped(
            finish_kernel,
            count // chunks,
            [x, came, taps, feature_map, map_t, partial, feats, gain, *others],
            [
                pl.BlockSpec((BLOCK // rows, 3, rows, DH), lambda i: (0, 0, 0, 0)),
                whole(came), whole(taps), whole(feature_map), whole(map_t),
                leading(size // BLOCK, BLOCK, DH), leading(size // BLOCK, BLOCK, features),
                whole(gain), *[leading(chunks, 1, rows, DH)] * len(others),
            ],
            leading(chunks, *piece.shape[1:]),
            piece,
            [narrow, narrow, narrow, pltpu.VMEM((features, 2 * DH), jnp.bfloat16)],
        )
        attended.append(out)
    landed = exchange(attended[-1]).reshape(parts, members, heads, rows, DH)
    held = max(1, members // 4)
    return stepped(
        unpack_kernel,
        members // held,
        [landed],
        [pl.BlockSpec((parts, held, heads, rows, DH), lambda i: (0, i, 0, 0, 0))],
        pl.BlockSpec((rows, held * parts * width), lambda i: (0, i)),
        shaped((rows, model)),
        [],
    )


def solution(mesh):
    groups, members = mesh.devices.shape
    parts = 1
    while groups % (4 * parts) == 0 and H % (2 * parts * members) == 0:
        parts *= 2
    spans = groups // parts
    split = Mesh(mesh.devices.reshape(spans, parts, members), ("span", "part", "sp"))
    tokens = P(("span", "part", "sp"), None)
    placed = (tokens, tokens, tokens, P(None, None, "sp"), P(), P("sp"))
    return jax.shard_map(
        functools.partial(local, spans),
        mesh=split, in_specs=placed, out_specs=tokens, check_vma=False,
    )
```

time: 115 us -> 107 us (0.930)
  waiting for transfers between devices: 26.2 us -> 20.4 us
  starting transfers between devices: 24.7 us -> 21.4 us
  Pallas kernels: 35.3 us -> 32.2 us
  blocking collectives: 20.6 us -> 23 us
  local copies, waits for them, and re-layouts: 7.6 us -> 9.01 us
    pallas_call x9 -> x2, Pallas kernels: 35.3 us -> 3.11 us  [whole_call(): pl.pallas_call(kernel, in_specs=[read] * len(inputs), out_specs=[written]...]
    pallas_call x0 -> x7, Pallas kernels: none -> 29.1 us  [stepped(): pl.pallas_call(kernel, grid=(steps,), in_specs=specs, out_specs=out_specs...]
    ppermute x2, waiting for transfers between devices: 8.57 us -> 0.01 us  [next_span(): return lax.ppermute(block, 'span', [(i, i + 1) for i in range(spans - 1)])]
    all_to_all x3 -> x2, starting transfers between devices: 14.7 us -> 10.2 us  [exchange(): return lax.all_to_all(block, GROUP, split_axis=0, concat_axis=0, tiled=True)]
    all_to_all x3 -> x2, waiting for transfers between devices: 17.7 us -> 20.4 us  [exchange(): return lax.all_to_all(block, GROUP, split_axis=0, concat_axis=0, tiled=True)]
    all_to_all x1, blocking collectives: 20.6 us -> 23 us  [exchange(): return lax.all_to_all(block, GROUP, split_axis=0, concat_axis=0, tiled=True)]
    unnamed x21 -> x25, local copies, waits for them, and re-layouts: 7.5 us -> 8.91 us
    ppermute x2, starting transfers between devices: 9.99 us -> 11.2 us  [next_span(): return lax.ppermute(block, 'span', [(i, i + 1) for i in range(spans - 1)])]
  transfers between devices with their start and end apart: 5 -> 4, of which waited for: 3 -> 2; matrix products, arithmetic and copies ran while one was open for 1% -> 1% of each run, Pallas kernels for 23% -> 23%
where the time goes in v2:
time: 107 us; the launch traced here: 106 us
  Pallas kernels  32.2 us (30%)
  blocking collectives  23 us (21%)
  starting transfers between devices  21.4 us (20%)
  waiting for transfers between devices  20.4 us (19%)
  local copies, waits for them, and re-layouts  9.01 us (8%)
    pallas_call x7, Pallas kernels, stepped(): pl.pallas_call(kernel, grid=(steps,), in_specs=specs, out_specs=out_specs...  29.1 us
    all_to_all x1, blocking collectives, exchange(): return lax.all_to_all(block, GROUP, split_axis=0, concat_axis=0, tiled=True)  23 us
    all_to_all x2, waiting for transfers between devices, exchange(): return lax.all_to_all(block, GROUP, split_axis=0, concat_axis=0, tiled=True)  20.4 us
    ppermute x2, starting transfers between devices, next_span(): return lax.ppermute(block, 'span', [(i, i + 1) for i in range(spans - 1)])  11.2 us
    all_to_all x2, starting transfers between devices, exchange(): return lax.all_to_all(block, GROUP, split_axis=0, concat_axis=0, tiled=True)  10.2 us
    unnamed x25, local copies, waits for them, and re-layouts  8.91 us
    pallas_call x2, Pallas kernels, whole_call(): pl.pallas_call(kernel, in_specs=[read] * len(inputs), out_specs=[written]...  3.11 us
  transfers between devices with their start and end apart: 4, of which 2 were waited for; matrix products, arithmetic and copies ran while one was open for 1% of the time, Pallas kernels for 23%

profile of v2, /device:TPU:0, one launch (start us, length us, event | category | flops | bytes accessed | tf_op | source)
XLA Modules:
  0.0 106.3 jit_solution(9267487926556547715)
XLA Ops:
  0.0 2.8 %shard_map.65 = bf16[16,3,128,128]{3,2,1,0:T(8,128)(2,1)} custom-call(bf16[128,4096]{1,0:T(8,128)(2,1)} %refs_0_.3, bf16[128,4096]{1,0:T(8,128)(2,1)} %refs_1_.3, bf16[128,4096]{1,0:T(8,128)(2,1)} %refs_2_.3), custom_call_target="tpu_custom_call" | custom-call | flops 1000 | bytes 1000 | tf_op jit(solution)/shard_map/pallas_call | solution.py:228
  2.8 6.3 %all-to-all-start.1 = ((bf16[16,3,128,128]{3,2,1,0:T(8,128)(2,1)}), bf16[16,3,128,128]{3,2,1,0:T(8,128)(2,1)S(1)}, u32[]{:S(2)}, u32[]{:S(2)}) async-start(bf16[16,3,128,128]{3,2,1,0:T(8,128)(2,1)} %shard_map.65), calls=%async_computation.1 | async-start | bytes 3145728 | tf_op jit(solution)/shard_map/all_to_all | solution.py:271
  9.2 0.0 copy-start.5
  9.2 1.2 %copy-done.5 = bf16[128,4096]{1,0:T(8,128)(2,1)S(1)} copy-done((bf16[128,4096]{1,0:T(8,128)(2,1)S(1)}, bf16[128,4096]{1,0:T(8,128)(2,1)}, u32[]{:S(2)}) %copy-start.5) | copy-done | bytes 1048600
  10.4 1.2 %copy-done.6 = bf16[128,4096]{1,0:T(8,128)(2,1)S(1)} copy-done((bf16[128,4096]{1,0:T(8,128)(2,1)S(1)}, bf16[128,4096]{1,0:T(8,128)(2,1)}, u32[]{:S(2)}) %copy-start.6) | copy-done | bytes 1048600
  11.6 1.2 %copy-done.7 = bf16[128,4096]{1,0:T(8,128)(2,1)S(1)} copy-done((bf16[128,4096]{1,0:T(8,128)(2,1)S(1)}, bf16[128,4096]{1,0:T(8,128)(2,1)}, u32[]{:S(2)}) %copy-start.7) | copy-done | bytes 1048600
  12.8 0.3 shard_map.64
  13.1 0.0 copy-start.2
  13.1 1.2 %copy-done.2 = bf16[16,3,128,128]{3,2,1,0:T(8,128)(2,1)} copy-done((bf16[16,3,128,128]{3,2,1,0:T(8,128)(2,1)}, bf16[16,3,128,128]{3,2,1,0:T(8,128)(2,1)S(1)}, u32[]{:S(2)}) %copy-start.2) | copy-done | bytes 1572888
  14.3 17.6 %all-to-all-done.1.x_ref.k_ref.v_ref.rim_ref = bf16[16,3,128,128]{3,2,1,0:T(8,128)(2,1)S(1)} async-done(((bf16[16,3,128,128]{3,2,1,0:T(8,128)(2,1)}), bf16[16,3,128,128]{3,2,1,0:T(8,128)(2,1)S(1)}, u32[]{:S(2)}, u32[]{:S(2)}) %all-to-all-start.1) | async-done | bytes 1572896 | tf_op jit(solution)/shard_map/all_to_all | solution.py:271
  31.9 3.9 %all-to-all-start = ((bf16[16,3,128,128]{3,2,1,0:T(8,128)(2,1)}), bf16[16,3,128,128]{3,2,1,0:T(8,128)(2,1)S(1)}, u32[]{:S(2)}, u32[]{:S(2)}) async-start(bf16[16,3,128,128]{3,2,1,0:T(8,128)(2,1)} %copy-done.2), calls=%async_computation | async-start | bytes 3145728 | tf_op jit(solution)/shard_map/all_to_all | solution.py:271
  35.8 1.1 %copy.7 = bf16[128,1024]{0,1:T(8,128)(2,1)S(1)} copy(bf16[128,1024]{1,0:T(8,128)(2,1)} %map_ref.7) | data formatting | bytes 524288 | tf_op args[4]
  37.0 0.0 copy-done.10
  37.0 0.0 copy-start
  37.0 3.8 %shard_map.69 = bf16[1072,128]{1,0:T(8,128)(2,1)} custom-call(bf16[16,3,128,128]{3,2,1,0:T(8,128)(2,1)S(1)} %all-to-all-done.1.x_ref.k_ref.v_ref.rim_ref, bf16[16,3,128,128]{3,2,1,0:T(8,128)(2,1)S(1)} %all-to-all-done.1.x_ref.k_ref.v_ref.rim_ref, bf16[16,3,128,128]{3,2,1,0:T(8,128)(2,1)S(1)} %all-to-all-done.1.x_ref.k_ref.v_ref.rim_ref, ...), custom_call_target="tpu_custom_call" | custom-call | flops 1000 | bytes 1000 | tf_op jit(solution)/shard_map/pallas_call | solution.py:240
  40.8 5.2 %collective-permute-start.1 = (bf16[1072,128]{1,0:T(8,128)(2,1)}, bf16[1072,128]{1,0:T(8,128)(2,1)}, u32[]{:S(2)}, u32[]{:S(2)}) collective-permute-start(bf16[1072,128]{1,0:T(8,128)(2,1)} %shard_map.69), channel_id=1, source_target_pairs={{0,16},{1,17},{2,18},{3,19},{4,20},{5,21},{6,22},{7,23},{8,24},{9,... | collective-permute-start | bytes 823304 | tf_op jit(solution)/shard_map/ppermute | solution.py:267
  46.0 0.0 copy-done
  46.0 7.0 %shard_map.66 = (f32[8,256,128]{2,1,0:T(8,128)S(1)}, bf16[8,256,1024]{2,1,0:T(8,128)(2,1)S(1)}) custom-call(bf16[16,3,128,128]{3,2,1,0:T(8,128)(2,1)S(1)} %all-to-all-done.1.x_ref.k_ref.v_ref.rim_ref, f32[3,4,128]{2,1,0:T(4,128)S(1)} %get-tuple-element.18.w_ref, bf16[128,1024]{1,0:T(8,128)(2,1)S(1)} %copy-done, bf16[1024,128]{1,0:T(8,128)(2,1)S(1)} %bitcast.4), custom_call_target="tpu_custom_call" | custom-call | flops 1000 | bytes 1000 | tf_op jit(solution)/shard_map/pallas_call | solution.py:240
  52.9 1.9 %copy-done.3 = bf16[8,256,1024]{2,1,0:T(8,128)(2,1)} copy-done((bf16[8,256,1024]{2,1,0:T(8,128)(2,1)}, bf16[8,256,1024]{2,1,0:T(8,128)(2,1)S(1)}, u32[]{:S(2)}) %copy-start.3) | copy-done | bytes 4194328
  54.9 1.0 copy-done.8
  55.9 2.8 %all-to-all-done.k_ref.v_ref.rim_ref.x_ref = bf16[16,3,128,128]{3,2,1,0:T(8,128)(2,1)S(1)} async-done(((bf16[16,3,128,128]{3,2,1,0:T(8,128)(2,1)}), bf16[16,3,128,128]{3,2,1,0:T(8,128)(2,1)S(1)}, u32[]{:S(2)}, u32[]{:S(2)}) %all-to-all-start) | async-done | bytes 1572896 | tf_op jit(solution)/shard_map/all_to_all | solution.py:271
  58.6 3.1 %shard_map.67 = bf16[1072,128]{1,0:T(8,128)(2,1)S(1)} custom-call(bf16[16,3,128,128]{3,2,1,0:T(8,128)(2,1)S(1)} %all-to-all-done.k_ref.v_ref.rim_ref.x_ref, bf16[16,3,128,128]{3,2,1,0:T(8,128)(2,1)S(1)} %all-to-all-done.k_ref.v_ref.rim_ref.x_ref, bf16[16,3,128,128]{3,2,1,0:T(8,128)(2,1)S(1)} %all-to-all-done.k_ref.v_ref.rim_ref.x_ref, ...), custom_call_target="tpu_custom_call" | custom-call | flops 1000 | bytes 1000 | tf_op jit(solution)/shard_map/pallas_call | solution.py:240
  61.7 0.0 copy-start.9
  61.7 6.0 %collective-permute-start = (bf16[1072,128]{1,0:T(8,128)(2,1)S(1)}, bf16[1072,128]{1,0:T(8,128)(2,1)S(1)}, u32[]{:S(2)}, u32[]{:S(2)}) collective-permute-start(bf16[1072,128]{1,0:T(8,128)(2,1)S(1)} %shard_map.67), channel_id=1, source_target_pairs={{0,16},{1,17},{2,18},{3,19},{4,20},{5,21},{6,22},{7,23},{8,24},{9,... | collective-permute-start | bytes 823304 | tf_op jit(solution)/shard_map/ppermute | solution.py:267
  67.7 0.1 dynamic_slice.7
  67.8 6.9 %shard_map.68 = (f32[8,256,128]{2,1,0:T(8,128)S(1)}, bf16[8,256,1024]{2,1,0:T(8,128)(2,1)S(1)}) custom-call(bf16[16,3,128,128]{3,2,1,0:T(8,128)(2,1)S(1)} %all-to-all-done.k_ref.v_ref.rim_ref.x_ref, f32[3,4,128]{2,1,0:T(4,128)S(1)} %get-tuple-element.17.w_ref, bf16[128,1024]{1,0:T(8,128)(2,1)S(1)} %copy-done.1, bf16[1024,128]{1,0:T(8,128)(2,1)S(1)} %bitcast.6), custom_call_target="tpu_custom_call" | custom-call | flops 1000 | bytes 1000 | tf_op jit(solution)/shard_map/pallas_call | solution.py:240
  74.8 0.0 collective-permute-done.1.came_ref
  74.8 3.8 %shard_map.70.refs_0_ = bf16[16,1,128,128]{3,2,1,0:T(8,128)(2,1)S(1)} custom-call(bf16[16,3,128,128]{3,2,1,0:T(8,128)(2,1)S(1)} %all-to-all-done.1.x_ref.k_ref.v_ref.rim_ref, bf16[1072,128]{1,0:T(8,128)(2,1)} %collective-permute-done.1.came_ref, f32[3,4,128]{2,1,0:T(4,128)S(1)} %get-tuple-element.18.w_ref, bf16[128,1024]{1,0:T(8,128)(2,1)S(1)} %copy-done.1, ...), custom_call_target="tpu_custom_call" | custom-call | flops 1000 | bytes 1000 | tf_op jit(solution)/shard_map/pallas_call | solution.py:240
  78.6 0.0 collective-permute-done.came_ref
  78.7 2.9 %shard_map.71 = bf16[16,2,128,128]{3,2,1,0:T(8,128)(2,1)S(1)} custom-call(bf16[16,3,128,128]{3,2,1,0:T(8,128)(2,1)S(1)} %all-to-all-done.k_ref.v_ref.rim_ref.x_ref, bf16[1072,128]{1,0:T(8,128)(2,1)S(1)} %collective-permute-done.came_ref, f32[3,4,128]{2,1,0:T(4,128)S(1)} %get-tuple-element.17.w_ref, bf16[128,1024]{1,0:T(8,128)(2,1)S(1)} %copy-done.1, ...), custom_call_target="tpu_custom_call" | custom-call | flops 1000 | bytes 1000 | tf_op jit(solution)/shard_map/pallas_call | solution.py:240
  81.5 23.0 %all_to_all.15 = bf16[16,2,128,128]{3,2,1,0:T(8,128)(2,1)S(1)} all-to-all(bf16[16,2,128,128]{3,2,1,0:T(8,128)(2,1)S(1)} %shard_map.71), channel_id=1, replica_groups=mesh['span'=2,'part'=2,'sp'=8] {'part','sp'}, dimensions={0} | all-to-all | bytes 2097152 | tf_op jit(solution)/shard_map/all_to_all | solution.py:271
  104.6 1.7 %shard_map.72 = bf16[128,4096]{1,0:T(8,128)(2,1)} custom-call(bf16[2,8,2,128,128]{4,3,2,1,0:T(8,128)(2,1)S(1)} %bitcast.9), custom_call_target="tpu_custom_call" | custom-call | flops 1000 | bytes 1000 | tf_op jit(solution)/shard_map/pallas_call | solution.py:240
  (15 shorter events, 0.0 us)
Async XLA Ops:
  2.8 29.1 %all-to-all-start.1 = ((bf16[16,3,128,128]{3,2,1,0:T(8,128)(2,1)}), bf16[16,3,128,128]{3,2,1,0:T(8,128)(2,1)S(1)}, u32[]{:S(2)}, u32[]{:S(2)}) async-start(bf16[16,3,128,128]{3,2,1,0:T(8,128)(2,1)} %shard_map.65), calls=%async_computation.1 | async-start | bytes 3145728 | tf_op jit(solution)/shard_map/all_to_all | solution.py:271
  9.2 1.2 %copy-start.5 = (bf16[128,4096]{1,0:T(8,128)(2,1)S(1)}, bf16[128,4096]{1,0:T(8,128)(2,1)}, u32[]{:S(2)}) copy-start(bf16[128,4096]{1,0:T(8,128)(2,1)} %refs_0_.3) | copy-start | bytes 3145732
  10.4 1.2 %copy-start.6 = (bf16[128,4096]{1,0:T(8,128)(2,1)S(1)}, bf16[128,4096]{1,0:T(8,128)(2,1)}, u32[]{:S(2)}) copy-start(bf16[128,4096]{1,0:T(8,128)(2,1)} %refs_1_.3) | copy-start | bytes 3145732
  11.6 1.2 %copy-start.7 = (bf16[128,4096]{1,0:T(8,128)(2,1)S(1)}, bf16[128,4096]{1,0:T(8,128)(2,1)}, u32[]{:S(2)}) copy-start(bf16[128,4096]{1,0:T(8,128)(2,1)} %refs_2_.3) | copy-start | bytes 3145732
  13.1 1.2 %copy-start.2 = (bf16[16,3,128,128]{3,2,1,0:T(8,128)(2,1)}, bf16[16,3,128,128]{3,2,1,0:T(8,128)(2,1)S(1)}, u32[]{:S(2)}) copy-start(bf16[16,3,128,128]{3,2,1,0:T(8,128)(2,1)S(1)} %shard_map.64) | copy-start | bytes 4718596
  14.3 22.7 %copy-start.10 = (f32[3,4,512]{2,1,0:T(4,128)S(1)}, f32[3,4,512]{2,1,0:T(4,128)}, u32[]{:S(2)}) copy-start(f32[3,4,512]{2,1,0:T(4,128)} %param.9) | copy-start | bytes 73732
  31.9 26.7 %all-to-all-start = ((bf16[16,3,128,128]{3,2,1,0:T(8,128)(2,1)}), bf16[16,3,128,128]{3,2,1,0:T(8,128)(2,1)S(1)}, u32[]{:S(2)}, u32[]{:S(2)}) async-start(bf16[16,3,128,128]{3,2,1,0:T(8,128)(2,1)} %copy-done.2), calls=%async_computation | async-start | bytes 3145728 | tf_op jit(solution)/shard_map/all_to_all | solution.py:271
  37.0 9.0 %copy-start = (bf16[128,1024]{1,0:T(8,128)(2,1)S(1)}, bf16[128,1024]{1,0:T(8,128)(2,1)}, u32[]{:S(2)}) copy-start(bf16[128,1024]{1,0:T(8,128)(2,1)} %map_ref.7) | copy-start | bytes 786436
  40.8 34.0 %collective-permute-start.1 = (bf16[1072,128]{1,0:T(8,128)(2,1)}, bf16[1072,128]{1,0:T(8,128)(2,1)}, u32[]{:S(2)}, u32[]{:S(2)}) collective-permute-start(bf16[1072,128]{1,0:T(8,128)(2,1)} %shard_map.69), channel_id=1, source_target_pairs={{0,16},{1,17},{2,18},{3,19},{4,20},{5,21},{6,22},{7,23},{8,24},{9,... | collective-permute-start | bytes 823304 | tf_op jit(solution)/shard_map/ppermute | solution.py:267
  52.9 1.9 %copy-start.3 = (bf16[8,256,1024]{2,1,0:T(8,128)(2,1)}, bf16[8,256,1024]{2,1,0:T(8,128)(2,1)S(1)}, u32[]{:S(2)}) copy-start(bf16[8,256,1024]{2,1,0:T(8,128)(2,1)S(1)} %get-tuple-element.11.feat_ref) | copy-start | bytes 12582916
  54.9 1.0 copy-start.8
  58.6 9.1 %copy-start.11 = (f32[512]{0:T(512)S(1)}, f32[512]{0:T(512)}, u32[]{:S(2)}) copy-start(f32[512]{0:T(512)} %param.11) | copy-start | bytes 6148
  58.6 9.2 %copy-start.1 = (bf16[128,1024]{1,0:T(8,128)(2,1)S(1)}, bf16[128,1024]{1,0:T(8,128)(2,1)}, u32[]{:S(2)}) copy-start(bf16[128,1024]{1,0:T(8,128)(2,1)} %map_ref.7) | copy-start | bytes 786436
  58.6 16.2 %copy-start.4 = (bf16[8,256,1024]{2,1,0:T(8,128)(2,1)S(1)}, bf16[8,256,1024]{2,1,0:T(8,128)(2,1)}, u32[]{:S(2)}) copy-start(bf16[8,256,1024]{2,1,0:T(8,128)(2,1)} %copy-done.3) | copy-start | bytes 12582916
  61.7 13.1 %copy-start.9 = (f32[8,256,128]{2,1,0:T(8,128)S(1)}, f32[8,256,128]{2,1,0:T(8,128)}, u32[]{:S(2)}) copy-start(f32[8,256,128]{2,1,0:T(8,128)} %copy-done.8) | copy-start | bytes 3145732
  61.7 17.0 %collective-permute-start = (bf16[1072,128]{1,0:T(8,128)(2,1)S(1)}, bf16[1072,128]{1,0:T(8,128)(2,1)S(1)}, u32[]{:S(2)}, u32[]{:S(2)}) collective-permute-start(bf16[1072,128]{1,0:T(8,128)(2,1)S(1)} %shard_map.67), channel_id=1, source_target_pairs={{0,16},{1,17},{2,18},{3,19},{4,20},{5,21},{6,22},{7,23},{8,24},{9,... | collective-permute-start | bytes 823304 | tf_op jit(solution)/shard_map/ppermute | solution.py:267

commit v3 on v2

--- a/solution.py
+++ b/solution.py
@@ -24,11 +24,11 @@
     return lax.dot_general(a, b, (((1,), (1,)), ((), ())), preferred_element_type=jnp.float32)
 
 
-def conv(pad_ref, weights, begin):
-    total = jnp.zeros((BLOCK, pad_ref.shape[1]), jnp.float32)
+def conv(pad_ref, weights, begin, count=BLOCK):
+    total = jnp.zeros((count, pad_ref.shape[1]), jnp.float32)
     for tap in range(weights.shape[0]):
         row = TAIL + begin - tap
-        total = total + weights[tap][None, :] * pad_ref[row : row + BLOCK]
+        total = total + weights[tap][None, :] * pad_ref[row : row + count]
     return total.astype(jnp.bfloat16)
 
 
@@ -123,9 +123,10 @@
     def _():
         state[...] = jnp.zeros_like(state)
 
-    for begin in range(0, size, BLOCK):
-        keys = conv(k_pad, w_ref[1], begin)
-        values = conv(v_pad, w_ref[2], begin)
+    extent = 2 * BLOCK if size % (2 * BLOCK) == 0 else BLOCK
+    for begin in range(0, size, extent):
+        keys = conv(k_pad, w_ref[1], begin, extent)
+        values = conv(v_pad, w_ref[2], begin, extent)
         state[...] += dot(relu16(dot_nt(map_t_ref[...], keys)), values)
 
     @pl.when(pl.program_id(0) == pl.num_programs(0) - 1)
@@ -195,11 +196,12 @@
 
     @pl.when(first)
     def _():
-        state = came_ref[:features]
+        follows = lax.axis_index("span") > 0
+        state = jnp.where(follows, came_ref[:features], jnp.zeros((features, DH), jnp.bfloat16))
         pads = (q_pad, k_pad, v_pad)
         for member, pad in enumerate(pads):
             end = features + (member + 1) * RIM
-            pad[:TAIL] = came_ref[end - TAIL : end].astype(jnp.float32)
+            pad[:TAIL] = jnp.where(follows, came_ref[end - TAIL : end].astype(jnp.float32), 0.0)
             fill(pad, x_ref[:, member])
         queries, keys, values = (conv(pad, w_ref[member], 0) for member, pad in enumerate(pads))
         feats_t = relu16(dot_nt(map_t_ref[...], keys))
@@ -339,7 +341,7 @@
             [tall, tall, whole_state],
         )
         if spans == 2:
-            came = next_span(sent, spans)
+            came = lax.ppermute(sent, "span", [(0, 1), (1, 0)])
         else:
             gathered = lax.all_gather(sent[:features], "span").astype(jnp.float32)
             mine = lax.axis_index("span")

time: 107 us -> 107 us (level)
  waiting for transfers between devices: 20.4 us -> 32.5 us
  starting transfers between devices: 21.4 us -> 12.9 us
  blocking collectives: 23 us -> 19.3 us
    ppermute x2, starting transfers between devices: 11.2 us -> 2.66 us  [local(): came = lax.ppermute(sent, 'span', [(0, 1), (1, 0)])]
    all_to_all x2, waiting for transfers between devices: 20.4 us -> 28.6 us  [exchange(): return lax.all_to_all(block, GROUP, split_axis=0, concat_axis=0, tiled=True)]
    ppermute x2, waiting for transfers between devices: 0.01 us -> 3.92 us  [local(): came = lax.ppermute(sent, 'span', [(0, 1), (1, 0)])]
    all_to_all x1, blocking collectives: 23 us -> 19.3 us  [exchange(): return lax.all_to_all(block, GROUP, split_axis=0, concat_axis=0, tiled=True)]
  transfers between devices with their start and end apart: 4 -> 4, of which waited for: 2 -> 3; matrix products, arithmetic and copies ran while one was open for 1% -> 1% of each run, Pallas kernels for 23% -> 23%
where the time goes in v3:
time: 107 us; the launch traced here: 106 us
  waiting for transfers between devices  32.5 us (30%)
  Pallas kernels  32.2 us (30%)
  blocking collectives  19.3 us (18%)
  starting transfers between devices  12.9 us (12%)
  local copies, waits for them, and re-layouts  9.01 us (8%)
    pallas_call x7, Pallas kernels, stepped(): pl.pallas_call(kernel, grid=(steps,), in_specs=specs, out_specs=out_specs...  29.1 us
    all_to_all x2, waiting for transfers between devices, exchange(): return lax.all_to_all(block, GROUP, split_axis=0, concat_axis=0, tiled=True)  28.6 us
    all_to_all x1, blocking collectives, exchange(): return lax.all_to_all(block, GROUP, split_axis=0, concat_axis=0, tiled=True)  19.3 us
    all_to_all x2, starting transfers between devices, exchange(): return lax.all_to_all(block, GROUP, split_axis=0, concat_axis=0, tiled=True)  10.2 us
    unnamed x25, local copies, waits for them, and re-layouts  8.91 us
    ppermute x2, waiting for transfers between devices, local(): came = lax.ppermute(sent, 'span', [(0, 1), (1, 0)])  3.92 us
    pallas_call x2, Pallas kernels, whole_call(): pl.pallas_call(kernel, in_specs=[read] * len(inputs), out_specs=[written]...  3.11 us
    ppermute x2, starting transfers between devices, local(): came = lax.ppermute(sent, 'span', [(0, 1), (1, 0)])  2.66 us
  transfers between devices with their start and end apart: 4, of which 3 were waited for; matrix products, arithmetic and copies ran while one was open for 1% of the time, Pallas kernels for 23%

profile of v3, /device:TPU:0, one launch (start us, length us, event | category | flops | bytes accessed | tf_op | source)
XLA Modules:
  0.0 106.1 jit_solution(10246739581674960341)
XLA Ops:
  0.0 2.8 %shard_map.65 = bf16[16,3,128,128]{3,2,1,0:T(8,128)(2,1)} custom-call(bf16[128,4096]{1,0:T(8,128)(2,1)} %refs_0_.3, bf16[128,4096]{1,0:T(8,128)(2,1)} %refs_1_.3, bf16[128,4096]{1,0:T(8,128)(2,1)} %refs_2_.3), custom_call_target="tpu_custom_call" | custom-call | flops 1000 | bytes 1000 | tf_op jit(solution)/shard_map/pallas_call | solution.py:230
  2.8 6.3 %all-to-all-start.1 = ((bf16[16,3,128,128]{3,2,1,0:T(8,128)(2,1)}), bf16[16,3,128,128]{3,2,1,0:T(8,128)(2,1)S(1)}, u32[]{:S(2)}, u32[]{:S(2)}) async-start(bf16[16,3,128,128]{3,2,1,0:T(8,128)(2,1)} %shard_map.65), calls=%async_computation.1 | async-start | bytes 3145728 | tf_op jit(solution)/shard_map/all_to_all | solution.py:273
  9.2 0.0 copy-start.5
  9.2 1.2 %copy-done.5 = bf16[128,4096]{1,0:T(8,128)(2,1)S(1)} copy-done((bf16[128,4096]{1,0:T(8,128)(2,1)S(1)}, bf16[128,4096]{1,0:T(8,128)(2,1)}, u32[]{:S(2)}) %copy-start.5) | copy-done | bytes 1048600
  10.4 1.2 %copy-done.6 = bf16[128,4096]{1,0:T(8,128)(2,1)S(1)} copy-done((bf16[128,4096]{1,0:T(8,128)(2,1)S(1)}, bf16[128,4096]{1,0:T(8,128)(2,1)}, u32[]{:S(2)}) %copy-start.6) | copy-done | bytes 1048600
  11.6 1.2 %copy-done.7 = bf16[128,4096]{1,0:T(8,128)(2,1)S(1)} copy-done((bf16[128,4096]{1,0:T(8,128)(2,1)S(1)}, bf16[128,4096]{1,0:T(8,128)(2,1)}, u32[]{:S(2)}) %copy-start.7) | copy-done | bytes 1048600
  12.8 0.3 shard_map.64
  13.1 0.0 copy-start.2
  13.1 1.2 %copy-done.2 = bf16[16,3,128,128]{3,2,1,0:T(8,128)(2,1)} copy-done((bf16[16,3,128,128]{3,2,1,0:T(8,128)(2,1)}, bf16[16,3,128,128]{3,2,1,0:T(8,128)(2,1)S(1)}, u32[]{:S(2)}) %copy-start.2) | copy-done | bytes 1572888
  14.3 17.6 %all-to-all-done.1.x_ref.k_ref.v_ref.rim_ref = bf16[16,3,128,128]{3,2,1,0:T(8,128)(2,1)S(1)} async-done(((bf16[16,3,128,128]{3,2,1,0:T(8,128)(2,1)}), bf16[16,3,128,128]{3,2,1,0:T(8,128)(2,1)S(1)}, u32[]{:S(2)}, u32[]{:S(2)}) %all-to-all-start.1) | async-done | bytes 1572896 | tf_op jit(solution)/shard_map/all_to_all | solution.py:273
  31.9 3.9 %all-to-all-start = ((bf16[16,3,128,128]{3,2,1,0:T(8,128)(2,1)}), bf16[16,3,128,128]{3,2,1,0:T(8,128)(2,1)S(1)}, u32[]{:S(2)}, u32[]{:S(2)}) async-start(bf16[16,3,128,128]{3,2,1,0:T(8,128)(2,1)} %copy-done.2), calls=%async_computation | async-start | bytes 3145728 | tf_op jit(solution)/shard_map/all_to_all | solution.py:273
  35.8 1.1 %copy.7 = bf16[128,1024]{0,1:T(8,128)(2,1)S(1)} copy(bf16[128,1024]{1,0:T(8,128)(2,1)} %map_ref.7) | data formatting | bytes 524288 | tf_op args[4]
  37.0 0.0 copy-done.10
  37.0 0.0 copy-start
  37.0 3.8 %shard_map.69 = bf16[1072,128]{1,0:T(8,128)(2,1)} custom-call(bf16[16,3,128,128]{3,2,1,0:T(8,128)(2,1)S(1)} %all-to-all-done.1.x_ref.k_ref.v_ref.rim_ref, bf16[16,3,128,128]{3,2,1,0:T(8,128)(2,1)S(1)} %all-to-all-done.1.x_ref.k_ref.v_ref.rim_ref, bf16[16,3,128,128]{3,2,1,0:T(8,128)(2,1)S(1)} %all-to-all-done.1.x_ref.k_ref.v_ref.rim_ref, ...), custom_call_target="tpu_custom_call" | custom-call | flops 1000 | bytes 1000 | tf_op jit(solution)/shard_map/pallas_call | solution.py:242
  40.8 2.6 %collective-permute-start.1 = (bf16[1072,128]{1,0:T(8,128)(2,1)}, bf16[1072,128]{1,0:T(8,128)(2,1)}, u32[]{:S(2)}, u32[]{:S(2)}) collective-permute-start(bf16[1072,128]{1,0:T(8,128)(2,1)} %shard_map.69), channel_id=1, source_target_pairs={{0,16},{16,0},{1,17},{17,1},{2,18},{18,2},{3,19},{19,3},{4,20},{20... | collective-permute-start | bytes 823304 | tf_op jit(solution)/shard_map/ppermute | solution.py:344
  43.4 7.0 %shard_map.66 = (f32[8,256,128]{2,1,0:T(8,128)S(1)}, bf16[8,256,1024]{2,1,0:T(8,128)(2,1)S(1)}) custom-call(bf16[16,3,128,128]{3,2,1,0:T(8,128)(2,1)S(1)} %all-to-all-done.1.x_ref.k_ref.v_ref.rim_ref, f32[3,4,128]{2,1,0:T(4,128)S(1)} %get-tuple-element.18.w_ref, bf16[128,1024]{1,0:T(8,128)(2,1)S(1)} %copy-done, bf16[1024,128]{1,0:T(8,128)(2,1)S(1)} %bitcast.4), custom_call_target="tpu_custom_call" | custom-call | flops 1000 | bytes 1000 | tf_op jit(solution)/shard_map/pallas_call | solution.py:242
  50.4 1.9 %copy-done.3 = bf16[8,256,1024]{2,1,0:T(8,128)(2,1)} copy-done((bf16[8,256,1024]{2,1,0:T(8,128)(2,1)}, bf16[8,256,1024]{2,1,0:T(8,128)(2,1)S(1)}, u32[]{:S(2)}) %copy-start.3) | copy-done | bytes 4194328
  52.3 1.0 copy-done.8
  53.3 11.0 %all-to-all-done.k_ref.v_ref.rim_ref.x_ref = bf16[16,3,128,128]{3,2,1,0:T(8,128)(2,1)S(1)} async-done(((bf16[16,3,128,128]{3,2,1,0:T(8,128)(2,1)}), bf16[16,3,128,128]{3,2,1,0:T(8,128)(2,1)S(1)}, u32[]{:S(2)}, u32[]{:S(2)}) %all-to-all-start) | async-done | bytes 1572896 | tf_op jit(solution)/shard_map/all_to_all | solution.py:273
  64.3 3.1 %shard_map.67 = bf16[1072,128]{1,0:T(8,128)(2,1)S(1)} custom-call(bf16[16,3,128,128]{3,2,1,0:T(8,128)(2,1)S(1)} %all-to-all-done.k_ref.v_ref.rim_ref.x_ref, bf16[16,3,128,128]{3,2,1,0:T(8,128)(2,1)S(1)} %all-to-all-done.k_ref.v_ref.rim_ref.x_ref, bf16[16,3,128,128]{3,2,1,0:T(8,128)(2,1)S(1)} %all-to-all-done.k_ref.v_ref.rim_ref.x_ref, ...), custom_call_target="tpu_custom_call" | custom-call | flops 1000 | bytes 1000 | tf_op jit(solution)/shard_map/pallas_call | solution.py:242
  67.3 0.0 copy-start.9
  67.3 0.1 collective-permute-start
  67.4 0.0 copy-done.11
  67.4 0.1 dynamic_slice.7
  67.5 6.9 %shard_map.68 = (f32[8,256,128]{2,1,0:T(8,128)S(1)}, bf16[8,256,1024]{2,1,0:T(8,128)(2,1)S(1)}) custom-call(bf16[16,3,128,128]{3,2,1,0:T(8,128)(2,1)S(1)} %all-to-all-done.k_ref.v_ref.rim_ref.x_ref, f32[3,4,128]{2,1,0:T(4,128)S(1)} %get-tuple-element.17.w_ref, bf16[128,1024]{1,0:T(8,128)(2,1)S(1)} %copy-done.1, bf16[1024,128]{1,0:T(8,128)(2,1)S(1)} %bitcast.6), custom_call_target="tpu_custom_call" | custom-call | flops 1000 | bytes 1000 | tf_op jit(solution)/shard_map/pallas_call | solution.py:242
  74.5 0.0 collective-permute-done.1.came_ref
  74.5 3.8 %shard_map.70.refs_0_ = bf16[16,1,128,128]{3,2,1,0:T(8,128)(2,1)S(1)} custom-call(bf16[16,3,128,128]{3,2,1,0:T(8,128)(2,1)S(1)} %all-to-all-done.1.x_ref.k_ref.v_ref.rim_ref, bf16[1072,128]{1,0:T(8,128)(2,1)} %collective-permute-done.1.came_ref, f32[3,4,128]{2,1,0:T(4,128)S(1)} %get-tuple-element.18.w_ref, bf16[128,1024]{1,0:T(8,128)(2,1)S(1)} %copy-done.1, ...), custom_call_target="tpu_custom_call" | custom-call | flops 1000 | bytes 1000 | tf_op jit(solution)/shard_map/pallas_call | solution.py:242
  78.3 3.9 %collective-permute-done.came_ref = bf16[1072,128]{1,0:T(8,128)(2,1)S(1)} collective-permute-done((bf16[1072,128]{1,0:T(8,128)(2,1)S(1)}, bf16[1072,128]{1,0:T(8,128)(2,1)S(1)}, u32[]{:S(2)}, u32[]{:S(2)}) %collective-permute-start) | collective-permute-done | bytes 274464 | tf_op jit(solution)/shard_map/ppermute | solution.py:344
  82.3 2.9 %shard_map.71 = bf16[16,2,128,128]{3,2,1,0:T(8,128)(2,1)S(1)} custom-call(bf16[16,3,128,128]{3,2,1,0:T(8,128)(2,1)S(1)} %all-to-all-done.k_ref.v_ref.rim_ref.x_ref, bf16[1072,128]{1,0:T(8,128)(2,1)S(1)} %collective-permute-done.came_ref, f32[3,4,128]{2,1,0:T(4,128)S(1)} %get-tuple-element.17.w_ref, bf16[128,1024]{1,0:T(8,128)(2,1)S(1)} %copy-done.1, ...), custom_call_target="tpu_custom_call" | custom-call | flops 1000 | bytes 1000 | tf_op jit(solution)/shard_map/pallas_call | solution.py:242
  85.1 19.3 %all_to_all.15 = bf16[16,2,128,128]{3,2,1,0:T(8,128)(2,1)S(1)} all-to-all(bf16[16,2,128,128]{3,2,1,0:T(8,128)(2,1)S(1)} %shard_map.71), channel_id=1, replica_groups=mesh['span'=2,'part'=2,'sp'=8] {'part','sp'}, dimensions={0} | all-to-all | bytes 2097152 | tf_op jit(solution)/shard_map/all_to_all | solution.py:273
  104.4 1.7 %shard_map.72 = bf16[128,4096]{1,0:T(8,128)(2,1)} custom-call(bf16[2,8,2,128,128]{4,3,2,1,0:T(8,128)(2,1)S(1)} %bitcast.9), custom_call_target="tpu_custom_call" | custom-call | flops 1000 | bytes 1000 | tf_op jit(solution)/shard_map/pallas_call | solution.py:242
  (15 shorter events, 0.0 us)
Async XLA Ops:
  2.8 29.1 %all-to-all-start.1 = ((bf16[16,3,128,128]{3,2,1,0:T(8,128)(2,1)}), bf16[16,3,128,128]{3,2,1,0:T(8,128)(2,1)S(1)}, u32[]{:S(2)}, u32[]{:S(2)}) async-start(bf16[16,3,128,128]{3,2,1,0:T(8,128)(2,1)} %shard_map.65), calls=%async_computation.1 | async-start | bytes 3145728 | tf_op jit(solution)/shard_map/all_to_all | solution.py:273
  9.2 1.2 %copy-start.5 = (bf16[128,4096]{1,0:T(8,128)(2,1)S(1)}, bf16[128,4096]{1,0:T(8,128)(2,1)}, u32[]{:S(2)}) copy-start(bf16[128,4096]{1,0:T(8,128)(2,1)} %refs_0_.3) | copy-start | bytes 3145732
  10.4 1.2 %copy-start.6 = (bf16[128,4096]{1,0:T(8,128)(2,1)S(1)}, bf16[128,4096]{1,0:T(8,128)(2,1)}, u32[]{:S(2)}) copy-start(bf16[128,4096]{1,0:T(8,128)(2,1)} %refs_1_.3) | copy-start | bytes 3145732
  11.6 1.2 %copy-start.7 = (bf16[128,4096]{1,0:T(8,128)(2,1)S(1)}, bf16[128,4096]{1,0:T(8,128)(2,1)}, u32[]{:S(2)}) copy-start(bf16[128,4096]{1,0:T(8,128)(2,1)} %refs_2_.3) | copy-start | bytes 3145732
  13.1 1.2 %copy-start.2 = (bf16[16,3,128,128]{3,2,1,0:T(8,128)(2,1)}, bf16[16,3,128,128]{3,2,1,0:T(8,128)(2,1)S(1)}, u32[]{:S(2)}) copy-start(bf16[16,3,128,128]{3,2,1,0:T(8,128)(2,1)S(1)} %shard_map.64) | copy-start | bytes 4718596
  14.3 22.7 %copy-start.10 = (f32[3,4,512]{2,1,0:T(4,128)S(1)}, f32[3,4,512]{2,1,0:T(4,128)}, u32[]{:S(2)}) copy-start(f32[3,4,512]{2,1,0:T(4,128)} %param.9) | copy-start | bytes 73732
  31.9 32.3 %all-to-all-start = ((bf16[16,3,128,128]{3,2,1,0:T(8,128)(2,1)}), bf16[16,3,128,128]{3,2,1,0:T(8,128)(2,1)S(1)}, u32[]{:S(2)}, u32[]{:S(2)}) async-start(bf16[16,3,128,128]{3,2,1,0:T(8,128)(2,1)} %copy-done.2), calls=%async_computation | async-start | bytes 3145728 | tf_op jit(solution)/shard_map/all_to_all | solution.py:273
  37.0 6.4 %copy-start = (bf16[128,1024]{1,0:T(8,128)(2,1)S(1)}, bf16[128,1024]{1,0:T(8,128)(2,1)}, u32[]{:S(2)}) copy-start(bf16[128,1024]{1,0:T(8,128)(2,1)} %map_ref.7) | copy-start | bytes 786436
  40.8 33.7 %collective-permute-start.1 = (bf16[1072,128]{1,0:T(8,128)(2,1)}, bf16[1072,128]{1,0:T(8,128)(2,1)}, u32[]{:S(2)}, u32[]{:S(2)}) collective-permute-start(bf16[1072,128]{1,0:T(8,128)(2,1)} %shard_map.69), channel_id=1, source_target_pairs={{0,16},{16,0},{1,17},{17,1},{2,18},{18,2},{3,19},{19,3},{4,20},{20... | collective-permute-start | bytes 823304 | tf_op jit(solution)/shard_map/ppermute | solution.py:344
  50.3 1.9 %copy-start.3 = (bf16[8,256,1024]{2,1,0:T(8,128)(2,1)}, bf16[8,256,1024]{2,1,0:T(8,128)(2,1)S(1)}, u32[]{:S(2)}) copy-start(bf16[8,256,1024]{2,1,0:T(8,128)(2,1)S(1)} %get-tuple-element.11.feat_ref) | copy-start | bytes 12582916
  52.3 1.0 copy-start.8
  64.3 3.2 %copy-start.11 = (f32[512]{0:T(512)S(1)}, f32[512]{0:T(512)}, u32[]{:S(2)}) copy-start(f32[512]{0:T(512)} %param.11) | copy-start | bytes 6148
  64.3 3.3 %copy-start.1 = (bf16[128,1024]{1,0:T(8,128)(2,1)S(1)}, bf16[128,1024]{1,0:T(8,128)(2,1)}, u32[]{:S(2)}) copy-start(bf16[128,1024]{1,0:T(8,128)(2,1)} %map_ref.7) | copy-start | bytes 786436
  64.3 10.2 %copy-start.4 = (bf16[8,256,1024]{2,1,0:T(8,128)(2,1)S(1)}, bf16[8,256,1024]{2,1,0:T(8,128)(2,1)}, u32[]{:S(2)}) copy-start(bf16[8,256,1024]{2,1,0:T(8,128)(2,1)} %copy-done.3) | copy-start | bytes 12582916
  67.3 7.2 %copy-start.9 = (f32[8,256,128]{2,1,0:T(8,128)S(1)}, f32[8,256,128]{2,1,0:T(8,128)}, u32[]{:S(2)}) copy-start(f32[8,256,128]{2,1,0:T(8,128)} %copy-done.8) | copy-start | bytes 3145732
  67.3 14.9 %collective-permute-start = (bf16[1072,128]{1,0:T(8,128)(2,1)S(1)}, bf16[1072,128]{1,0:T(8,128)(2,1)S(1)}, u32[]{:S(2)}, u32[]{:S(2)}) collective-permute-start(bf16[1072,128]{1,0:T(8,128)(2,1)S(1)} %shard_map.67), channel_id=1, source_target_pairs={{0,16},{16,0},{1,17},{17,1},{2,18},{18,2},{3,19},{19,3},{4,20},{20... | collective-permute-start | bytes 823304 | tf_op jit(solution)/shard_map/ppermute | solution.py:344

commit v4 on v3

--- a/solution.py
+++ b/solution.py
@@ -144,41 +144,44 @@
 
 
 def span_kernel(x_ref, w_ref, map_ref, map_t_ref, part_ref, feat_ref, q_pad, k_pad, v_pad, state):
-    first = pl.program_id(0) == 0
+    blocks, size = part_ref.shape[0], q_pad.shape[0] - TAIL
+    chunks, group = size // x_ref.shape[2], size // BLOCK
     pads = (q_pad, k_pad, v_pad)
-    carry_tail(pads, first, lambda member: jnp.zeros((TAIL, DH), jnp.float32))
-    for member, pad in enumerate(pads):
-        fill(pad, x_ref[:, member])
-
-    def one(j):
-        queries, keys, values = (conv(pad, w_ref[m], j * BLOCK) for m, pad in enumerate(pads))
-        feats_t = relu16(dot_nt(map_t_ref[...], keys))
-        feats = relu16(dot(queries, map_ref[...]))
-        feat_ref[j] = feats
-        carried = folded(dot(feats, high_low(state[...])))
-        part_ref[j] = dot(causal_scores(feats, feats_t), values) + carried
-        state[...] += dot(feats_t, values)
-
-    @pl.when(first)
-    def _():
-        state[...] = jnp.zeros_like(state)
-
-    @pl.when(jnp.logical_not(first))
-    def _():
-        one(0)
-
-    for j in range(1, part_ref.shape[0]):
-        one(j)
+
+    def step(i, members):
+        for member, pad in enumerate(pads):
+            fill(pad, x_ref[pl.ds(i * chunks, chunks), member])
+        for j in members:
+            queries, keys, values = (conv(pad, w_ref[m], j * BLOCK) for m, pad in enumerate(pads))
+            feats_t = relu16(dot_nt(map_t_ref[...], keys))
+            feats = relu16(dot(queries, map_ref[...]))
+            block = i * group + j
+            feat_ref[block] = feats
+            carried = folded(dot(feats, high_low(state[...])))
+            part_ref[block] = dot(causal_scores(feats, feats_t), values) + carried
+            state[...] += dot(feats_t, values)
+
+    state[...] = jnp.zeros_like(state)
+    for pad in pads:
+        pad[:TAIL] = jnp.zeros((TAIL, DH), jnp.float32)
+    step(0, range(1, group))
+
+    def later(i, carry):
+        for pad in pads:
+            pad[:TAIL] = pad[size:]
+        step(i, range(group))
+        return carry
+
+    lax.fori_loop(1, blocks // group, later, 0)
 
 
 def finish_kernel(
     x_ref, came_ref, w_ref, map_ref, map_t_ref, part_ref, feat_ref, gain_ref, *refs
 ):
-    *others, out_ref, q_pad, k_pad, v_pad, later = refs
+    *others, out_ref, q_pad, k_pad, v_pad = refs
     blocks, _, features = feat_ref.shape
     per_block = BLOCK // out_ref.shape[2]
     gain = gain_ref[...]
-    first = pl.program_id(0) == 0
     for place, other in enumerate(others):
         out_ref[:, place] = other[:, 0]
 
@@ -189,31 +192,23 @@
         extent = (end - begin) * per_block
         out_ref[held, len(others)] = normed.reshape(extent, BLOCK // per_block, DH)
 
-    def rest(begin):
-        extent = (blocks - begin) * BLOCK
-        feats = feat_ref[begin:].reshape(extent, features)
-        put(begin, blocks, part_ref[begin:].reshape(extent, DH) + folded(dot(feats, later[...])))
-
-    @pl.when(first)
-    def _():
-        follows = lax.axis_index("span") > 0
-        state = jnp.where(follows, came_ref[:features], jnp.zeros((features, DH), jnp.bfloat16))
-        pads = (q_pad, k_pad, v_pad)
-        for member, pad in enumerate(pads):
-            end = features + (member + 1) * RIM
-            pad[:TAIL] = jnp.where(follows, came_ref[end - TAIL : end].astype(jnp.float32), 0.0)
-            fill(pad, x_ref[:, member])
-        queries, keys, values = (conv(pad, w_ref[member], 0) for member, pad in enumerate(pads))
-        feats_t = relu16(dot_nt(map_t_ref[...], keys))
-        feats = relu16(dot(queries, map_ref[...]))
-        later[...] = high_low(state.astype(jnp.float32) + dot(feats_t, values))
-        put(0, 1, dot(causal_scores(feats, feats_t), values) + dot(feats, state))
-        if blocks > 1:
-            rest(1)
-
-    @pl.when(jnp.logical_not(first))
-    def _():
-        rest(0)
+    follows = lax.axis_index("span") > 0
+    state = jnp.where(follows, came_ref[:features], jnp.zeros((features, DH), jnp.bfloat16))
+    pads = (q_pad, k_pad, v_pad)
+    for member, pad in enumerate(pads):
+        end = features + (member + 1) * RIM
+        pad[:TAIL] = jnp.where(follows, came_ref[end - TAIL : end].astype(jnp.float32), 0.0)
+        fill(pad, x_ref[: (pad.shape[0] - TAIL) // x_ref.shape[2], member])
+    queries, keys, values = (conv(pad, w_ref[member], 0) for member, pad in enumerate(pads))
+    feats_t = relu16(dot_nt(map_t_ref[...], keys))
+    feats = relu16(dot(queries, map_ref[...]))
+    later = high_low(state.astype(jnp.float32) + dot(feats_t, values))
+    put(0, 1, dot(causal_scores(feats, feats_t), values) + dot(feats, state))
+    for begin in range(1, blocks, 2):
+        end = min(begin + 2, blocks)
+        extent = (end - begin) * BLOCK
+        feats = feat_ref[begin:end].reshape(extent, features)
+        put(begin, end, part_ref[begin:end].reshape(extent, DH) + folded(dot(feats, later)))
 
 
 LIMIT = 24 * 1024 * 1024
@@ -254,11 +249,6 @@
 def whole(array):
     zeros = (0,) * array.ndim
     return pl.BlockSpec(array.shape, lambda i: zeros)
-
-
-def leading(*shape):
-    zeros = (0,) * (len(shape) - 1)
-    return pl.BlockSpec(shape, lambda i: (i, *zeros))
 
 
 def shaped(shape, dtype=jnp.bfloat16):
@@ -295,7 +285,6 @@
 
     inputs = [query_input, key_input, value_heads_input]
     size = BLOCK * (2 if blocks % 2 == 0 else 1)
-    wide = pltpu.VMEM((TAIL + size, DH), jnp.float32)
     narrow = pltpu.VMEM((TAIL + BLOCK, DH), jnp.float32)
     whole_state = pltpu.VMEM((features, DH), jnp.float32)
     chunks = size // rows
@@ -341,24 +330,22 @@
             [tall, tall, whole_state],
         )
         if spans == 2:
-            came = lax.ppermute(sent, "span", [(0, 1), (1, 0)])
+            both = head == heads - 1
+            came = lax.ppermute(sent, "span", [(0, 1), (1, 0)] if both else [(0, 1)])
         else:
             gathered = lax.all_gather(sent[:features], "span").astype(jnp.float32)
             mine = lax.axis_index("span")
             earlier = jnp.where((jnp.arange(spans) < mine)[:, None, None], gathered, 0.0)
             state = jnp.sum(earlier, 0).astype(jnp.bfloat16)
             came = jnp.concatenate([state, halo.reshape(3 * RIM, DH)])
-        done = stepped(
+        done = whole_call(
             span_kernel,
-            count // chunks,
             [x, taps, feature_map, map_t],
-            [leading(chunks, 3, rows, DH), whole(taps), whole(feature_map), whole(map_t)],
-            [leading(size // BLOCK, BLOCK, DH), leading(size // BLOCK, BLOCK, features)],
             [
                 shaped((blocks, BLOCK, DH), jnp.float32),
                 shaped((blocks, BLOCK, features)),
             ],
-            [wide, wide, wide, whole_state],
+            [tall, tall, tall, whole_state],
         )
         xs.append((x, came, taps))
         sents.append(sent)
@@ -373,19 +360,11 @@
             gain = after(gain, sents[-1])
         others = attended if head == heads - 1 else []
         piece = shaped((count, len(others) + 1, rows, DH))
-        out = stepped(
+        (out,) = whole_call(
             finish_kernel,
-            count // chunks,
             [x, came, taps, feature_map, map_t, partial, feats, gain, *others],
-            [
-                pl.BlockSpec((BLOCK // rows, 3, rows, DH), lambda i: (0, 0, 0, 0)),
-                whole(came), whole(taps), whole(feature_map), whole(map_t),
-                leading(size // BLOCK, BLOCK, DH), leading(size // BLOCK, BLOCK, features),
-                whole(gain), *[leading(chunks, 1, rows, DH)] * len(others),
-            ],
-            leading(chunks, *piece.shape[1:]),
-            piece,
-            [narrow, narrow, narrow, pltpu.VMEM((features, 2 * DH), jnp.bfloat16)],
+            [piece],
+            [narrow, narrow, narrow],
         )
         attended.append(out)
     landed = exchange(attended[-1]).reshape(parts, members, heads, rows, DH)

time: 107 us -> 103 us (0.963)
  waiting for transfers between devices: 32.5 us -> 24.5 us
  starting transfers between devices: 12.9 us -> 19.4 us
  Pallas kernels: 32.2 us -> 28.9 us
    pallas_call x7 -> x3, Pallas kernels: 29.1 us -> 8.51 us  [stepped(): pl.pallas_call(kernel, grid=(steps,), in_specs=specs, out_specs=out_specs...]
    pallas_call x2 -> x6, Pallas kernels: 3.11 us -> 20.3 us  [whole_call(): pl.pallas_call(kernel, in_specs=[read] * len(inputs), out_specs=[written]...]
    all_to_all x2, waiting for transfers between devices: 28.6 us -> 21.2 us  [exchange(): return lax.all_to_all(block, GROUP, split_axis=0, concat_axis=0, tiled=True)]
    ppermute x2, starting transfers between devices: 2.66 us -> 9.23 us  [local(): came = lax.ppermute(sent, 'span', [(0, 1), (1, 0)] if both else [(0, 1)])]
  transfers between devices with their start and end apart: 4 -> 4, of which waited for: 3 -> 3; matrix products, arithmetic and copies ran while one was open for 1% -> 1% of each run, Pallas kernels for 23% -> 22%
where the time goes in v4:
time: 103 us; the launch traced here: 102 us
  Pallas kernels  28.9 us (28%)
  waiting for transfers between devices  24.5 us (24%)
  blocking collectives  20.3 us (20%)
  starting transfers between devices  19.4 us (19%)
  local copies, waits for them, and re-layouts  9.01 us (9%)
    all_to_all x2, waiting for transfers between devices, exchange(): return lax.all_to_all(block, GROUP, split_axis=0, concat_axis=0, tiled=True)  21.2 us
    pallas_call x6, Pallas kernels, whole_call(): pl.pallas_call(kernel, in_specs=[read] * len(inputs), out_specs=[written]...  20.3 us
    all_to_all x1, blocking collectives, exchange(): return lax.all_to_all(block, GROUP, split_axis=0, concat_axis=0, tiled=True)  20.3 us
    all_to_all x2, starting transfers between devices, exchange(): return lax.all_to_all(block, GROUP, split_axis=0, concat_axis=0, tiled=True)  10.2 us
    ppermute x2, starting transfers between devices, local(): came = lax.ppermute(sent, 'span', [(0, 1), (1, 0)] if both else [(0, 1)])  9.23 us
    unnamed x25, local copies, waits for them, and re-layouts  8.91 us
    pallas_call x3, Pallas kernels, stepped(): pl.pallas_call(kernel, grid=(steps,), in_specs=specs, out_specs=out_specs...  8.51 us
    ppermute x2, waiting for transfers between devices, local(): came = lax.ppermute(sent, 'span', [(0, 1), (1, 0)] if both else [(0, 1)])  3.33 us
  transfers between devices with their start and end apart: 4, of which 3 were waited for; matrix products, arithmetic and copies ran while one was open for 1% of the time, Pallas kernels for 22%

profile of v4, /device:TPU:0, one launch (start us, length us, event | category | flops | bytes accessed | tf_op | source)
XLA Modules:
  0.0 102.3 jit_solution(6547084283824964689)
XLA Ops:
  0.0 2.8 %shard_map.65 = bf16[16,3,128,128]{3,2,1,0:T(8,128)(2,1)} custom-call(bf16[128,4096]{1,0:T(8,128)(2,1)} %refs_0_.3, bf16[128,4096]{1,0:T(8,128)(2,1)} %refs_1_.3, bf16[128,4096]{1,0:T(8,128)(2,1)} %refs_2_.3), custom_call_target="tpu_custom_call" | custom-call | flops 1000 | bytes 1000 | tf_op jit(solution)/shard_map/pallas_call | solution.py:225
  2.8 6.3 %all-to-all-start.1 = ((bf16[16,3,128,128]{3,2,1,0:T(8,128)(2,1)}), bf16[16,3,128,128]{3,2,1,0:T(8,128)(2,1)S(1)}, u32[]{:S(2)}, u32[]{:S(2)}) async-start(bf16[16,3,128,128]{3,2,1,0:T(8,128)(2,1)} %shard_map.65), calls=%async_computation.1 | async-start | bytes 3145728 | tf_op jit(solution)/shard_map/all_to_all | solution.py:263
  9.2 0.0 copy-start.5
  9.2 1.2 %copy-done.5 = bf16[128,4096]{1,0:T(8,128)(2,1)S(1)} copy-done((bf16[128,4096]{1,0:T(8,128)(2,1)S(1)}, bf16[128,4096]{1,0:T(8,128)(2,1)}, u32[]{:S(2)}) %copy-start.5) | copy-done | bytes 1048600
  10.4 1.2 %copy-done.6 = bf16[128,4096]{1,0:T(8,128)(2,1)S(1)} copy-done((bf16[128,4096]{1,0:T(8,128)(2,1)S(1)}, bf16[128,4096]{1,0:T(8,128)(2,1)}, u32[]{:S(2)}) %copy-start.6) | copy-done | bytes 1048600
  11.6 1.2 %copy-done.7 = bf16[128,4096]{1,0:T(8,128)(2,1)S(1)} copy-done((bf16[128,4096]{1,0:T(8,128)(2,1)S(1)}, bf16[128,4096]{1,0:T(8,128)(2,1)}, u32[]{:S(2)}) %copy-start.7) | copy-done | bytes 1048600
  12.8 0.3 shard_map.64
  13.1 0.0 copy-start.2
  13.1 1.2 %copy-done.2 = bf16[16,3,128,128]{3,2,1,0:T(8,128)(2,1)} copy-done((bf16[16,3,128,128]{3,2,1,0:T(8,128)(2,1)}, bf16[16,3,128,128]{3,2,1,0:T(8,128)(2,1)S(1)}, u32[]{:S(2)}) %copy-start.2) | copy-done | bytes 1572888
  14.3 17.6 %all-to-all-done.1.x_ref.k_ref.v_ref.rim_ref = bf16[16,3,128,128]{3,2,1,0:T(8,128)(2,1)S(1)} async-done(((bf16[16,3,128,128]{3,2,1,0:T(8,128)(2,1)}), bf16[16,3,128,128]{3,2,1,0:T(8,128)(2,1)S(1)}, u32[]{:S(2)}, u32[]{:S(2)}) %all-to-all-start.1) | async-done | bytes 1572896 | tf_op jit(solution)/shard_map/all_to_all | solution.py:263
  31.9 3.9 %all-to-all-start = ((bf16[16,3,128,128]{3,2,1,0:T(8,128)(2,1)}), bf16[16,3,128,128]{3,2,1,0:T(8,128)(2,1)S(1)}, u32[]{:S(2)}, u32[]{:S(2)}) async-start(bf16[16,3,128,128]{3,2,1,0:T(8,128)(2,1)} %copy-done.2), calls=%async_computation | async-start | bytes 3145728 | tf_op jit(solution)/shard_map/all_to_all | solution.py:263
  35.8 1.1 %copy.7 = bf16[128,1024]{0,1:T(8,128)(2,1)S(1)} copy(bf16[128,1024]{1,0:T(8,128)(2,1)} %map_ref.7) | data formatting | bytes 524288 | tf_op args[4]
  37.0 0.0 copy-start
  37.0 3.8 %shard_map.69 = bf16[1072,128]{1,0:T(8,128)(2,1)} custom-call(bf16[16,3,128,128]{3,2,1,0:T(8,128)(2,1)S(1)} %all-to-all-done.1.x_ref.k_ref.v_ref.rim_ref, bf16[16,3,128,128]{3,2,1,0:T(8,128)(2,1)S(1)} %all-to-all-done.1.x_ref.k_ref.v_ref.rim_ref, bf16[16,3,128,128]{3,2,1,0:T(8,128)(2,1)S(1)} %all-to-all-done.1.x_ref.k_ref.v_ref.rim_ref, ...), custom_call_target="tpu_custom_call" | custom-call | flops 1000 | bytes 1000 | tf_op jit(solution)/shard_map/pallas_call | solution.py:237
  40.8 5.2 %collective-permute-start.1 = (bf16[1072,128]{1,0:T(8,128)(2,1)}, bf16[1072,128]{1,0:T(8,128)(2,1)}, u32[]{:S(2)}, u32[]{:S(2)}) collective-permute-start(bf16[1072,128]{1,0:T(8,128)(2,1)} %shard_map.69), channel_id=1, source_target_pairs={{0,16},{1,17},{2,18},{3,19},{4,20},{5,21},{6,22},{7,23},{8,24},{9,... | collective-permute-start | bytes 823304 | tf_op jit(solution)/shard_map/ppermute | solution.py:334
  46.0 6.1 %shard_map.66 = (f32[8,256,128]{2,1,0:T(8,128)S(1)}, bf16[8,256,1024]{2,1,0:T(8,128)(2,1)S(1)}) custom-call(bf16[16,3,128,128]{3,2,1,0:T(8,128)(2,1)S(1)} %all-to-all-done.1.x_ref.k_ref.v_ref.rim_ref, f32[3,4,128]{2,1,0:T(4,128)S(1)} %get-tuple-element.18.w_ref, bf16[128,1024]{1,0:T(8,128)(2,1)S(1)} %copy-done, bf16[1024,128]{1,0:T(8,128)(2,1)S(1)} %bitcast.4), custom_call_target="tpu_custom_call" | custom-call | flops 1000 | bytes 1000 | tf_op jit(solution)/shard_map/pallas_call | solution.py:225
  52.1 0.0 copy-start.3
  52.1 1.9 %copy-done.3 = bf16[8,256,1024]{2,1,0:T(8,128)(2,1)} copy-done((bf16[8,256,1024]{2,1,0:T(8,128)(2,1)}, bf16[8,256,1024]{2,1,0:T(8,128)(2,1)S(1)}, u32[]{:S(2)}) %copy-start.3) | copy-done | bytes 4194328
  54.1 1.0 copy-done.8
  55.0 3.6 %all-to-all-done.k_ref.v_ref.rim_ref.x_ref = bf16[16,3,128,128]{3,2,1,0:T(8,128)(2,1)S(1)} async-done(((bf16[16,3,128,128]{3,2,1,0:T(8,128)(2,1)}), bf16[16,3,128,128]{3,2,1,0:T(8,128)(2,1)S(1)}, u32[]{:S(2)}, u32[]{:S(2)}) %all-to-all-start) | async-done | bytes 1572896 | tf_op jit(solution)/shard_map/all_to_all | solution.py:263
  58.6 3.1 %shard_map.67 = bf16[1072,128]{1,0:T(8,128)(2,1)S(1)} custom-call(bf16[16,3,128,128]{3,2,1,0:T(8,128)(2,1)S(1)} %all-to-all-done.k_ref.v_ref.rim_ref.x_ref, bf16[16,3,128,128]{3,2,1,0:T(8,128)(2,1)S(1)} %all-to-all-done.k_ref.v_ref.rim_ref.x_ref, bf16[16,3,128,128]{3,2,1,0:T(8,128)(2,1)S(1)} %all-to-all-done.k_ref.v_ref.rim_ref.x_ref, ...), custom_call_target="tpu_custom_call" | custom-call | flops 1000 | bytes 1000 | tf_op jit(solution)/shard_map/pallas_call | solution.py:237
  61.7 0.0 copy-start.9
  61.7 4.1 %collective-permute-start = (bf16[1072,128]{1,0:T(8,128)(2,1)S(1)}, bf16[1072,128]{1,0:T(8,128)(2,1)S(1)}, u32[]{:S(2)}, u32[]{:S(2)}) collective-permute-start(bf16[1072,128]{1,0:T(8,128)(2,1)S(1)} %shard_map.67), channel_id=1, source_target_pairs={{0,16},{16,0},{1,17},{17,1},{2,18},{18,2},{3,19},{19,3},{4,20},{20... | collective-permute-start | bytes 823304 | tf_op jit(solution)/shard_map/ppermute | solution.py:334
  65.7 0.1 dynamic_slice.7
  65.8 0.0 copy-done.1
  65.8 6.1 %shard_map.68 = (f32[8,256,128]{2,1,0:T(8,128)S(1)}, bf16[8,256,1024]{2,1,0:T(8,128)(2,1)S(1)}) custom-call(bf16[16,3,128,128]{3,2,1,0:T(8,128)(2,1)S(1)} %all-to-all-done.k_ref.v_ref.rim_ref.x_ref, f32[3,4,128]{2,1,0:T(4,128)S(1)} %get-tuple-element.17.w_ref, bf16[128,1024]{1,0:T(8,128)(2,1)S(1)} %copy-done.1, bf16[1024,128]{1,0:T(8,128)(2,1)S(1)} %bitcast.6), custom_call_target="tpu_custom_call" | custom-call | flops 1000 | bytes 1000 | tf_op jit(solution)/shard_map/pallas_call | solution.py:225
  72.0 0.0 collective-permute-done.1.came_ref
  72.0 3.0 %shard_map.70.refs_0_ = bf16[16,1,128,128]{3,2,1,0:T(8,128)(2,1)S(1)} custom-call(bf16[16,3,128,128]{3,2,1,0:T(8,128)(2,1)S(1)} %all-to-all-done.1.x_ref.k_ref.v_ref.rim_ref, bf16[1072,128]{1,0:T(8,128)(2,1)} %collective-permute-done.1.came_ref, f32[3,4,128]{2,1,0:T(4,128)S(1)} %get-tuple-element.18.w_ref, bf16[128,1024]{1,0:T(8,128)(2,1)S(1)} %copy-done.1, ...), custom_call_target="tpu_custom_call" | custom-call | flops 1000 | bytes 1000 | tf_op jit(solution)/shard_map/pallas_call | solution.py:225
  75.0 3.3 %collective-permute-done.came_ref = bf16[1072,128]{1,0:T(8,128)(2,1)S(1)} collective-permute-done((bf16[1072,128]{1,0:T(8,128)(2,1)S(1)}, bf16[1072,128]{1,0:T(8,128)(2,1)S(1)}, u32[]{:S(2)}, u32[]{:S(2)}) %collective-permute-start) | collective-permute-done | bytes 274464 | tf_op jit(solution)/shard_map/ppermute | solution.py:334
  78.3 2.0 %shard_map.71 = bf16[16,2,128,128]{3,2,1,0:T(8,128)(2,1)S(1)} custom-call(bf16[16,3,128,128]{3,2,1,0:T(8,128)(2,1)S(1)} %all-to-all-done.k_ref.v_ref.rim_ref.x_ref, bf16[1072,128]{1,0:T(8,128)(2,1)S(1)} %collective-permute-done.came_ref, f32[3,4,128]{2,1,0:T(4,128)S(1)} %get-tuple-element.17.w_ref, bf16[128,1024]{1,0:T(8,128)(2,1)S(1)} %copy-done.1, ...), custom_call_target="tpu_custom_call" | custom-call | flops 1000 | bytes 1000 | tf_op jit(solution)/shard_map/pallas_call | solution.py:225
  80.3 20.3 %all_to_all.15 = bf16[16,2,128,128]{3,2,1,0:T(8,128)(2,1)S(1)} all-to-all(bf16[16,2,128,128]{3,2,1,0:T(8,128)(2,1)S(1)} %shard_map.71), channel_id=1, replica_groups=mesh['span'=2,'part'=2,'sp'=8] {'part','sp'}, dimensions={0} | all-to-all | bytes 2097152 | tf_op jit(solution)/shard_map/all_to_all | solution.py:263
  100.6 1.7 %shard_map.72 = bf16[128,4096]{1,0:T(8,128)(2,1)} custom-call(bf16[2,8,2,128,128]{4,3,2,1,0:T(8,128)(2,1)S(1)} %bitcast.9), custom_call_target="tpu_custom_call" | custom-call | flops 1000 | bytes 1000 | tf_op jit(solution)/shard_map/pallas_call | solution.py:237
  (15 shorter events, 0.0 us)
Async XLA Ops:
  2.8 29.1 %all-to-all-start.1 = ((bf16[16,3,128,128]{3,2,1,0:T(8,128)(2,1)}), bf16[16,3,128,128]{3,2,1,0:T(8,128)(2,1)S(1)}, u32[]{:S(2)}, u32[]{:S(2)}) async-start(bf16[16,3,128,128]{3,2,1,0:T(8,128)(2,1)} %shard_map.65), calls=%async_computation.1 | async-start | bytes 3145728 | tf_op jit(solution)/shard_map/all_to_all | solution.py:263
  9.2 1.2 %copy-start.5 = (bf16[128,4096]{1,0:T(8,128)(2,1)S(1)}, bf16[128,4096]{1,0:T(8,128)(2,1)}, u32[]{:S(2)}) copy-start(bf16[128,4096]{1,0:T(8,128)(2,1)} %refs_0_.3) | copy-start | bytes 3145732
  10.4 1.2 %copy-start.6 = (bf16[128,4096]{1,0:T(8,128)(2,1)S(1)}, bf16[128,4096]{1,0:T(8,128)(2,1)}, u32[]{:S(2)}) copy-start(bf16[128,4096]{1,0:T(8,128)(2,1)} %refs_1_.3) | copy-start | bytes 3145732
  11.6 1.2 %copy-start.7 = (bf16[128,4096]{1,0:T(8,128)(2,1)S(1)}, bf16[128,4096]{1,0:T(8,128)(2,1)}, u32[]{:S(2)}) copy-start(bf16[128,4096]{1,0:T(8,128)(2,1)} %refs_2_.3) | copy-start | bytes 3145732
  13.1 1.2 %copy-start.2 = (bf16[16,3,128,128]{3,2,1,0:T(8,128)(2,1)}, bf16[16,3,128,128]{3,2,1,0:T(8,128)(2,1)S(1)}, u32[]{:S(2)}) copy-start(bf16[16,3,128,128]{3,2,1,0:T(8,128)(2,1)S(1)} %shard_map.64) | copy-start | bytes 4718596
  14.3 22.7 %copy-start.10 = (f32[3,4,512]{2,1,0:T(4,128)S(1)}, f32[3,4,512]{2,1,0:T(4,128)}, u32[]{:S(2)}) copy-start(f32[3,4,512]{2,1,0:T(4,128)} %param.9) | copy-start | bytes 73732
  31.9 26.7 %all-to-all-start = ((bf16[16,3,128,128]{3,2,1,0:T(8,128)(2,1)}), bf16[16,3,128,128]{3,2,1,0:T(8,128)(2,1)S(1)}, u32[]{:S(2)}, u32[]{:S(2)}) async-start(bf16[16,3,128,128]{3,2,1,0:T(8,128)(2,1)} %copy-done.2), calls=%async_computation | async-start | bytes 3145728 | tf_op jit(solution)/shard_map/all_to_all | solution.py:263
  37.0 9.0 %copy-start = (bf16[128,1024]{1,0:T(8,128)(2,1)S(1)}, bf16[128,1024]{1,0:T(8,128)(2,1)}, u32[]{:S(2)}) copy-start(bf16[128,1024]{1,0:T(8,128)(2,1)} %map_ref.7) | copy-start | bytes 786436
  40.8 31.2 %collective-permute-start.1 = (bf16[1072,128]{1,0:T(8,128)(2,1)}, bf16[1072,128]{1,0:T(8,128)(2,1)}, u32[]{:S(2)}, u32[]{:S(2)}) collective-permute-start(bf16[1072,128]{1,0:T(8,128)(2,1)} %shard_map.69), channel_id=1, source_target_pairs={{0,16},{1,17},{2,18},{3,19},{4,20},{5,21},{6,22},{7,23},{8,24},{9,... | collective-permute-start | bytes 823304 | tf_op jit(solution)/shard_map/ppermute | solution.py:334
  52.1 1.9 %copy-start.3 = (bf16[8,256,1024]{2,1,0:T(8,128)(2,1)}, bf16[8,256,1024]{2,1,0:T(8,128)(2,1)S(1)}, u32[]{:S(2)}) copy-start(bf16[8,256,1024]{2,1,0:T(8,128)(2,1)S(1)} %get-tuple-element.11.feat_ref) | copy-start | bytes 12582916
  54.1 1.0 copy-start.8
  58.6 7.1 %copy-start.11 = (f32[512]{0:T(512)S(1)}, f32[512]{0:T(512)}, u32[]{:S(2)}) copy-start(f32[512]{0:T(512)} %param.11) | copy-start | bytes 6148
  58.6 7.2 %copy-start.1 = (bf16[128,1024]{1,0:T(8,128)(2,1)S(1)}, bf16[128,1024]{1,0:T(8,128)(2,1)}, u32[]{:S(2)}) copy-start(bf16[128,1024]{1,0:T(8,128)(2,1)} %map_ref.7) | copy-start | bytes 786436
  58.6 13.4 %copy-start.4 = (bf16[8,256,1024]{2,1,0:T(8,128)(2,1)S(1)}, bf16[8,256,1024]{2,1,0:T(8,128)(2,1)}, u32[]{:S(2)}) copy-start(bf16[8,256,1024]{2,1,0:T(8,128)(2,1)} %copy-done.3) | copy-start | bytes 12582916
  61.7 10.3 %copy-start.9 = (f32[8,256,128]{2,1,0:T(8,128)S(1)}, f32[8,256,128]{2,1,0:T(8,128)}, u32[]{:S(2)}) copy-start(f32[8,256,128]{2,1,0:T(8,128)} %copy-done.8) | copy-start | bytes 3145732
  61.7 16.6 %collective-permute-start = (bf16[1072,128]{1,0:T(8,128)(2,1)S(1)}, bf16[1072,128]{1,0:T(8,128)(2,1)S(1)}, u32[]{:S(2)}, u32[]{:S(2)}) collective-permute-start(bf16[1072,128]{1,0:T(8,128)(2,1)S(1)} %shard_map.67), channel_id=1, source_target_pairs={{0,16},{16,0},{1,17},{17,1},{2,18},{18,2},{3,19},{19,3},{4,20},{20... | collective-permute-start | bytes 823304 | tf_op jit(solution)/shard_map/ppermute | solution.py:334

commit v5 on v4

--- a/solution.py
+++ b/solution.py
@@ -95,46 +95,39 @@
     pad_ref[TAIL:] = held.reshape(count, DH).astype(jnp.float32)
 
 
-def carry_tail(pads, first, halo):
-    for member, pad in enumerate(pads):
-        count = pad.shape[0] - TAIL
-
-        @pl.when(first)
-        def _(pad=pad, member=member):
-            pad[:TAIL] = halo(member)
-
-        @pl.when(jnp.logical_not(first))
-        def _(pad=pad, count=count):
-            pad[:TAIL] = pad[count:]
-
-
-def totals_kernel(k_ref, v_ref, rim_ref, halo_ref, w_ref, map_t_ref, sent_ref, k_pad, v_pad, state):
-    rows, features = k_ref.shape[2], map_t_ref.shape[0]
-    size = k_pad.shape[0] - TAIL
-    first = pl.program_id(0) == 0
-    carry_tail(
-        (k_pad, v_pad), first,
-        lambda member: halo_ref[member + 1, RIM - TAIL :].astype(jnp.float32),
-    )
-    fill(k_pad, k_ref[...])
-    fill(v_pad, v_ref[...])
-
-    @pl.when(first)
-    def _():
-        state[...] = jnp.zeros_like(state)
-
+def totals_kernel(x_ref, halo_ref, w_ref, map_t_ref, sent_ref, k_pad, v_pad, state):
+    count, _, rows, _ = x_ref.shape
+    features, size = map_t_ref.shape[0], k_pad.shape[0] - TAIL
+    chunks = size // rows
+    for member in range(3):
+        held = slice(features + member * RIM, features + (member + 1) * RIM)
+        sent_ref[held] = x_ref[count - 1, member, rows - RIM :]
+    k_pad[:TAIL] = halo_ref[1, RIM - TAIL :].astype(jnp.float32)
+    v_pad[:TAIL] = halo_ref[2, RIM - TAIL :].astype(jnp.float32)
     extent = 2 * BLOCK if size % (2 * BLOCK) == 0 else BLOCK
-    for begin in range(0, size, extent):
-        keys = conv(k_pad, w_ref[1], begin, extent)
-        values = conv(v_pad, w_ref[2], begin, extent)
-        state[...] += dot(relu16(dot_nt(map_t_ref[...], keys)), values)
-
-    @pl.when(pl.program_id(0) == pl.num_programs(0) - 1)
-    def _():
-        sent_ref[:features] = state[...].astype(jnp.bfloat16)
-        for member in range(3):
-            held = slice(features + member * RIM, features + (member + 1) * RIM)
-            sent_ref[held] = rim_ref[0, member, rows - RIM :]
+
+    def step(i):
+        fill(k_pad, x_ref[pl.ds(i * chunks, chunks), 1])
+        fill(v_pad, x_ref[pl.ds(i * chunks, chunks), 2])
+        for begin in range(0, size, extent):
+            keys = conv(k_pad, w_ref[1], begin, extent)
+            values = conv(v_pad, w_ref[2], begin, extent)
+            update = dot(relu16(dot_nt(map_t_ref[...], keys)), values)
+            if isinstance(i, int) and begin == 0:
+                state[...] = update
+            else:
+                state[...] += update
+
+    step(0)
+
+    def later(i, carry):
+        for pad in (k_pad, v_pad):
+            pad[:TAIL] = pad[size:]
+        step(i)
+        return carry
+
+    lax.fori_loop(1, count // chunks, later, 0)
+    sent_ref[:features] = state[...].astype(jnp.bfloat16)
 
 
 def causal_scores(feats, feats_t):
@@ -218,7 +211,6 @@
 
 
 COST = pl.CostEstimate(flops=1000, bytes_accessed=1000, transcendentals=0)
-GRID = pltpu.CompilerParams(dimension_semantics=("arbitrary",), vmem_limit_bytes=LIMIT)
 
 
 def whole_call(kernel, inputs, outputs, scratch=(), read=VMEM, written=VMEM, limit=LIMIT):
@@ -231,24 +223,6 @@
         compiler_params=pltpu.CompilerParams(vmem_limit_bytes=limit),
         cost_estimate=COST,
     )(*inputs)
-
-
-def stepped(kernel, steps, inputs, specs, out_specs, outputs, scratch):
-    return pl.pallas_call(
-        kernel,
-        grid=(steps,),
-        in_specs=specs,
-        out_specs=out_specs,
-        out_shape=outputs,
-        scratch_shapes=scratch,
-        compiler_params=GRID,
-        cost_estimate=COST,
-    )(*inputs)
-
-
-def whole(array):
-    zeros = (0,) * array.ndim
-    return pl.BlockSpec(array.shape, lambda i: zeros)
 
 
 def shaped(shape, dtype=jnp.bfloat16):
@@ -315,18 +289,10 @@
             halo = next_span(x[count - 1, :, rows - RIM :], spans)
         big = chunks * (2 if count % (2 * chunks) == 0 else 1)
         tall = pltpu.VMEM((TAIL + big * rows, DH), jnp.float32)
-        sent = stepped(
+        (sent,) = whole_call(
             totals_kernel,
-            count // big,
-            [x, x, x, halo, taps, map_t],
-            [
-                pl.BlockSpec((big, 1, rows, DH), lambda i: (i, 1, 0, 0)),
-                pl.BlockSpec((big, 1, rows, DH), lambda i: (i, 2, 0, 0)),
-                pl.BlockSpec((1, 3, rows, DH), lambda i: (count - 1, 0, 0, 0)),
-                whole(halo), whole(taps), whole(map_t),
-            ],
-            pl.BlockSpec((features + 3 * RIM, DH), lambda i: (0, 0)),
-            shaped((features + 3 * RIM, DH)),
+            [x, halo, taps, map_t],
+            [shaped((features + 3 * RIM, DH))],
             [tall, tall, whole_state],
         )
         if spans == 2:
@@ -368,16 +334,8 @@
         )
         attended.append(out)
     landed = exchange(attended[-1]).reshape(parts, members, heads, rows, DH)
-    held = max(1, members // 4)
-    return stepped(
-        unpack_kernel,
-        members // held,
-        [landed],
-        [pl.BlockSpec((parts, held, heads, rows, DH), lambda i: (0, i, 0, 0, 0))],
-        pl.BlockSpec((rows, held * parts * width), lambda i: (0, i)),
-        shaped((rows, model)),
-        [],
-    )
+    (result,) = whole_call(unpack_kernel, [landed], [shaped((rows, model))])
+    return result
 
 
 def solution(mesh):

time: 103 us -> 104 us (level)
  local copies, waits for them, and re-layouts: 9.01 us -> 11.2 us
  waiting for transfers between devices: 24.5 us -> 22.6 us
  blocking collectives: 20.3 us -> 22.1 us
  Pallas kernels: 28.9 us -> 27.6 us
    pallas_call x3 -> x0, Pallas kernels: 8.51 us -> none  [stepped(): pl.pallas_call(kernel, grid=(steps,), in_specs=specs, out_specs=out_specs...]
    pallas_call x6 -> x9, Pallas kernels: 20.3 us -> 27.6 us  [whole_call(): pl.pallas_call(kernel, in_specs=[read] * len(inputs), out_specs=[written]...]
    ppermute x2, waiting for transfers between devices: 3.33 us -> 0.96 us  [local(): came = lax.ppermute(sent, 'span', [(0, 1), (1, 0)] if both else [(0, 1)])]
    unnamed x25, local copies, waits for them, and re-layouts: 8.91 us -> 11.1 us
    all_to_all x1, blocking collectives: 20.3 us -> 22.1 us  [exchange(): return lax.all_to_all(block, GROUP, split_axis=0, concat_axis=0, tiled=True)]
  transfers between devices with their start and end apart: 4 -> 4, of which waited for: 3 -> 3; matrix products, arithmetic and copies ran while one was open for 1% -> 1% of each run, Pallas kernels for 22% -> 21%
where the time goes in v5:
time: 104 us; the launch traced here: 103 us
  Pallas kernels  27.6 us (27%)
  waiting for transfers between devices  22.6 us (22%)
  blocking collectives  22.1 us (21%)
  starting transfers between devices  19.5 us (19%)
  local copies, waits for them, and re-layouts  11.2 us (11%)
    pallas_call x9, Pallas kernels, whole_call(): pl.pallas_call(kernel, in_specs=[read] * len(inputs), out_specs=[written]...  27.6 us
    all_to_all x1, blocking collectives, exchange(): return lax.all_to_all(block, GROUP, split_axis=0, concat_axis=0, tiled=True)  22.1 us
    all_to_all x2, waiting for transfers between devices, exchange(): return lax.all_to_all(block, GROUP, split_axis=0, concat_axis=0, tiled=True)  21.7 us
    unnamed x25, local copies, waits for them, and re-layouts  11.1 us
    all_to_all x2, starting transfers between devices, exchange(): return lax.all_to_all(block, GROUP, split_axis=0, concat_axis=0, tiled=True)  10.2 us
    ppermute x2, starting transfers between devices, local(): came = lax.ppermute(sent, 'span', [(0, 1), (1, 0)] if both else [(0, 1)])  9.25 us
  transfers between devices with their start and end apart: 4, of which 3 were waited for; matrix products, arithmetic and copies ran while one was open for 1% of the time, Pallas kernels for 21%

profile of v5, /device:TPU:0, one launch (start us, length us, event | category | flops | bytes accessed | tf_op | source)
XLA Modules:
  0.0 103.1 jit_solution(12687735348139029171)
XLA Ops:
  0.0 2.8 %shard_map.65 = bf16[16,3,128,128]{3,2,1,0:T(8,128)(2,1)} custom-call(bf16[128,4096]{1,0:T(8,128)(2,1)} %refs_0_.3, bf16[128,4096]{1,0:T(8,128)(2,1)} %refs_1_.3, bf16[128,4096]{1,0:T(8,128)(2,1)} %refs_2_.3), custom_call_target="tpu_custom_call" | custom-call | flops 1000 | bytes 1000 | tf_op jit(solution)/shard_map/pallas_call | solution.py:217
  2.8 6.3 %all-to-all-start.1 = ((bf16[16,3,128,128]{3,2,1,0:T(8,128)(2,1)}), bf16[16,3,128,128]{3,2,1,0:T(8,128)(2,1)S(1)}, u32[]{:S(2)}, u32[]{:S(2)}) async-start(bf16[16,3,128,128]{3,2,1,0:T(8,128)(2,1)} %shard_map.65), calls=%async_computation.1 | async-start | bytes 3145728 | tf_op jit(solution)/shard_map/all_to_all | solution.py:237
  9.2 0.0 copy-start.5
  9.2 1.2 %copy-done.5 = bf16[128,4096]{1,0:T(8,128)(2,1)S(1)} copy-done((bf16[128,4096]{1,0:T(8,128)(2,1)S(1)}, bf16[128,4096]{1,0:T(8,128)(2,1)}, u32[]{:S(2)}) %copy-start.5) | copy-done | bytes 1048600
  10.4 1.2 %copy-done.6 = bf16[128,4096]{1,0:T(8,128)(2,1)S(1)} copy-done((bf16[128,4096]{1,0:T(8,128)(2,1)S(1)}, bf16[128,4096]{1,0:T(8,128)(2,1)}, u32[]{:S(2)}) %copy-start.6) | copy-done | bytes 1048600
  11.6 1.2 %copy-done.7 = bf16[128,4096]{1,0:T(8,128)(2,1)S(1)} copy-done((bf16[128,4096]{1,0:T(8,128)(2,1)S(1)}, bf16[128,4096]{1,0:T(8,128)(2,1)}, u32[]{:S(2)}) %copy-start.7) | copy-done | bytes 1048600
  12.8 0.3 shard_map.64
  13.1 1.2 %copy-done.2 = bf16[16,3,128,128]{3,2,1,0:T(8,128)(2,1)} copy-done((bf16[16,3,128,128]{3,2,1,0:T(8,128)(2,1)}, bf16[16,3,128,128]{3,2,1,0:T(8,128)(2,1)S(1)}, u32[]{:S(2)}) %copy-start.2) | copy-done | bytes 1572888
  14.3 17.6 %all-to-all-done.1.x_ref = bf16[16,3,128,128]{3,2,1,0:T(8,128)(2,1)S(1)} async-done(((bf16[16,3,128,128]{3,2,1,0:T(8,128)(2,1)}), bf16[16,3,128,128]{3,2,1,0:T(8,128)(2,1)S(1)}, u32[]{:S(2)}, u32[]{:S(2)}) %all-to-all-start.1) | async-done | bytes 1572896 | tf_op jit(solution)/shard_map/all_to_all | solution.py:237
  31.9 3.9 %all-to-all-start = ((bf16[16,3,128,128]{3,2,1,0:T(8,128)(2,1)}), bf16[16,3,128,128]{3,2,1,0:T(8,128)(2,1)S(1)}, u32[]{:S(2)}, u32[]{:S(2)}) async-start(bf16[16,3,128,128]{3,2,1,0:T(8,128)(2,1)} %copy-done.2), calls=%async_computation | async-start | bytes 3145728 | tf_op jit(solution)/shard_map/all_to_all | solution.py:237
  35.8 1.1 %copy.7 = bf16[128,1024]{0,1:T(8,128)(2,1)S(1)} copy(bf16[128,1024]{1,0:T(8,128)(2,1)} %map_ref.7) | data formatting | bytes 524288 | tf_op args[4]
  37.0 0.0 copy-start
  37.0 3.3 %shard_map.69 = bf16[1072,128]{1,0:T(8,128)(2,1)} custom-call(bf16[16,3,128,128]{3,2,1,0:T(8,128)(2,1)S(1)} %all-to-all-done.1.x_ref, bf16[3,16,128]{2,1,0:T(8,128)(2,1)S(1)} %broadcast_1_halo_ref.2.halo_ref, f32[3,4,128]{2,1,0:T(4,128)S(1)} %get-tuple-element.18.w_ref, bf16[1024,128]{1,0:T(8,128)(2,1)S(1)} %bitcast.3), custom_call_target="tpu_custom_call" | custom-call | flops 1000 | bytes 1000 | tf_op jit(solution)/shard_map/pallas_call | solution.py:217
  40.3 5.2 %collective-permute-start.1 = (bf16[1072,128]{1,0:T(8,128)(2,1)}, bf16[1072,128]{1,0:T(8,128)(2,1)}, u32[]{:S(2)}, u32[]{:S(2)}) collective-permute-start(bf16[1072,128]{1,0:T(8,128)(2,1)} %shard_map.69), channel_id=1, source_target_pairs={{0,16},{1,17},{2,18},{3,19},{4,20},{5,21},{6,22},{7,23},{8,24},{9,... | collective-permute-start | bytes 823304 | tf_op jit(solution)/shard_map/ppermute | solution.py:300
  45.5 6.1 %shard_map.66 = (f32[8,256,128]{2,1,0:T(8,128)S(1)}, bf16[8,256,1024]{2,1,0:T(8,128)(2,1)S(1)}) custom-call(bf16[16,3,128,128]{3,2,1,0:T(8,128)(2,1)S(1)} %all-to-all-done.1.x_ref, f32[3,4,128]{2,1,0:T(4,128)S(1)} %get-tuple-element.18.w_ref, bf16[128,1024]{1,0:T(8,128)(2,1)S(1)} %copy-done, bf16[1024,128]{1,0:T(8,128)(2,1)S(1)} %bitcast.4), custom_call_target="tpu_custom_call" | custom-call | flops 1000 | bytes 1000 | tf_op jit(solution)/shard_map/pallas_call | solution.py:217
  51.6 0.0 copy-start.3
  51.6 1.9 %copy-done.3 = bf16[8,256,1024]{2,1,0:T(8,128)(2,1)} copy-done((bf16[8,256,1024]{2,1,0:T(8,128)(2,1)}, bf16[8,256,1024]{2,1,0:T(8,128)(2,1)S(1)}, u32[]{:S(2)}) %copy-start.3) | copy-done | bytes 4194328
  53.6 1.0 copy-done.8
  54.6 4.1 %all-to-all-done.x_ref = bf16[16,3,128,128]{3,2,1,0:T(8,128)(2,1)S(1)} async-done(((bf16[16,3,128,128]{3,2,1,0:T(8,128)(2,1)}), bf16[16,3,128,128]{3,2,1,0:T(8,128)(2,1)S(1)}, u32[]{:S(2)}, u32[]{:S(2)}) %all-to-all-start) | async-done | bytes 1572896 | tf_op jit(solution)/shard_map/all_to_all | solution.py:237
  58.6 2.6 %shard_map.67 = bf16[1072,128]{1,0:T(8,128)(2,1)S(1)} custom-call(bf16[16,3,128,128]{3,2,1,0:T(8,128)(2,1)S(1)} %all-to-all-done.x_ref, bf16[3,16,128]{2,1,0:T(8,128)(2,1)S(1)} %broadcast_1_halo_ref.2.halo_ref, f32[3,4,128]{2,1,0:T(4,128)S(1)} %get-tuple-element.17.w_ref, bf16[1024,128]{1,0:T(8,128)(2,1)S(1)} %bitcast.5), custom_call_target="tpu_custom_call" | custom-call | flops 1000 | bytes 1000 | tf_op jit(solution)/shard_map/pallas_call | solution.py:217
  61.2 0.0 copy-start.9
  61.2 4.1 %collective-permute-start = (bf16[1072,128]{1,0:T(8,128)(2,1)S(1)}, bf16[1072,128]{1,0:T(8,128)(2,1)S(1)}, u32[]{:S(2)}, u32[]{:S(2)}) collective-permute-start(bf16[1072,128]{1,0:T(8,128)(2,1)S(1)} %shard_map.67), channel_id=1, source_target_pairs={{0,16},{16,0},{1,17},{17,1},{2,18},{18,2},{3,19},{19,3},{4,20},{20... | collective-permute-start | bytes 823304 | tf_op jit(solution)/shard_map/ppermute | solution.py:300
  65.3 0.0 copy-done.11
  65.3 0.1 dynamic_slice.7
  65.3 6.3 %shard_map.68 = (f32[8,256,128]{2,1,0:T(8,128)S(1)}, bf16[8,256,1024]{2,1,0:T(8,128)(2,1)S(1)}) custom-call(bf16[16,3,128,128]{3,2,1,0:T(8,128)(2,1)S(1)} %all-to-all-done.x_ref, f32[3,4,128]{2,1,0:T(4,128)S(1)} %get-tuple-element.17.w_ref, bf16[128,1024]{1,0:T(8,128)(2,1)S(1)} %copy-done.1, bf16[1024,128]{1,0:T(8,128)(2,1)S(1)} %bitcast.6), custom_call_target="tpu_custom_call" | custom-call | flops 1000 | bytes 1000 | tf_op jit(solution)/shard_map/pallas_call | solution.py:217
  71.7 0.0 collective-permute-done.1.came_ref
  71.7 2.2 %copy-done.4 = bf16[8,256,1024]{2,1,0:T(8,128)(2,1)S(1)} copy-done((bf16[8,256,1024]{2,1,0:T(8,128)(2,1)S(1)}, bf16[8,256,1024]{2,1,0:T(8,128)(2,1)}, u32[]{:S(2)}) %copy-start.4) | copy-done | bytes 4194328
  73.9 2.9 %shard_map.70.refs_0_ = bf16[16,1,128,128]{3,2,1,0:T(8,128)(2,1)S(1)} custom-call(bf16[16,3,128,128]{3,2,1,0:T(8,128)(2,1)S(1)} %all-to-all-done.1.x_ref, bf16[1072,128]{1,0:T(8,128)(2,1)} %collective-permute-done.1.came_ref, f32[3,4,128]{2,1,0:T(4,128)S(1)} %get-tuple-element.18.w_ref, bf16[128,1024]{1,0:T(8,128)(2,1)S(1)} %copy-done.1, ...), custom_call_target="tpu_custom_call" | custom-call | flops 1000 | bytes 1000 | tf_op jit(solution)/shard_map/pallas_call | solution.py:217
  76.8 1.0 collective-permute-done.came_ref
  77.8 2.0 %shard_map.71 = bf16[16,2,128,128]{3,2,1,0:T(8,128)(2,1)S(1)} custom-call(bf16[16,3,128,128]{3,2,1,0:T(8,128)(2,1)S(1)} %all-to-all-done.x_ref, bf16[1072,128]{1,0:T(8,128)(2,1)S(1)} %collective-permute-done.came_ref, f32[3,4,128]{2,1,0:T(4,128)S(1)} %get-tuple-element.17.w_ref, bf16[128,1024]{1,0:T(8,128)(2,1)S(1)} %copy-done.1, ...), custom_call_target="tpu_custom_call" | custom-call | flops 1000 | bytes 1000 | tf_op jit(solution)/shard_map/pallas_call | solution.py:217
  79.8 22.1 %all_to_all.15 = bf16[16,2,128,128]{3,2,1,0:T(8,128)(2,1)S(1)} all-to-all(bf16[16,2,128,128]{3,2,1,0:T(8,128)(2,1)S(1)} %shard_map.71), channel_id=1, replica_groups=mesh['span'=2,'part'=2,'sp'=8] {'part','sp'}, dimensions={0} | all-to-all | bytes 2097152 | tf_op jit(solution)/shard_map/all_to_all | solution.py:237
  101.9 1.2 %shard_map.72 = bf16[128,4096]{1,0:T(8,128)(2,1)} custom-call(bf16[2,8,2,128,128]{4,3,2,1,0:T(8,128)(2,1)S(1)} %bitcast.9), custom_call_target="tpu_custom_call" | custom-call | flops 1000 | bytes 1000 | tf_op jit(solution)/shard_map/pallas_call | solution.py:217
  (15 shorter events, 0.0 us)
Async XLA Ops:
  2.8 29.1 %all-to-all-start.1 = ((bf16[16,3,128,128]{3,2,1,0:T(8,128)(2,1)}), bf16[16,3,128,128]{3,2,1,0:T(8,128)(2,1)S(1)}, u32[]{:S(2)}, u32[]{:S(2)}) async-start(bf16[16,3,128,128]{3,2,1,0:T(8,128)(2,1)} %shard_map.65), calls=%async_computation.1 | async-start | bytes 3145728 | tf_op jit(solution)/shard_map/all_to_all | solution.py:237
  9.2 1.2 %copy-start.5 = (bf16[128,4096]{1,0:T(8,128)(2,1)S(1)}, bf16[128,4096]{1,0:T(8,128)(2,1)}, u32[]{:S(2)}) copy-start(bf16[128,4096]{1,0:T(8,128)(2,1)} %refs_0_.3) | copy-start | bytes 3145732
  10.4 1.2 %copy-start.6 = (bf16[128,4096]{1,0:T(8,128)(2,1)S(1)}, bf16[128,4096]{1,0:T(8,128)(2,1)}, u32[]{:S(2)}) copy-start(bf16[128,4096]{1,0:T(8,128)(2,1)} %refs_1_.3) | copy-start | bytes 3145732
  11.6 1.2 %copy-start.7 = (bf16[128,4096]{1,0:T(8,128)(2,1)S(1)}, bf16[128,4096]{1,0:T(8,128)(2,1)}, u32[]{:S(2)}) copy-start(bf16[128,4096]{1,0:T(8,128)(2,1)} %refs_2_.3) | copy-start | bytes 3145732
  13.1 1.2 %copy-start.2 = (bf16[16,3,128,128]{3,2,1,0:T(8,128)(2,1)}, bf16[16,3,128,128]{3,2,1,0:T(8,128)(2,1)S(1)}, u32[]{:S(2)}) copy-start(bf16[16,3,128,128]{3,2,1,0:T(8,128)(2,1)S(1)} %shard_map.64) | copy-start | bytes 4718596
  14.3 22.7 %copy-start.10 = (f32[3,4,512]{2,1,0:T(4,128)S(1)}, f32[3,4,512]{2,1,0:T(4,128)}, u32[]{:S(2)}) copy-start(f32[3,4,512]{2,1,0:T(4,128)} %param.9) | copy-start | bytes 73732
  31.9 26.7 %all-to-all-start = ((bf16[16,3,128,128]{3,2,1,0:T(8,128)(2,1)}), bf16[16,3,128,128]{3,2,1,0:T(8,128)(2,1)S(1)}, u32[]{:S(2)}, u32[]{:S(2)}) async-start(bf16[16,3,128,128]{3,2,1,0:T(8,128)(2,1)} %copy-done.2), calls=%async_computation | async-start | bytes 3145728 | tf_op jit(solution)/shard_map/all_to_all | solution.py:237
  37.0 8.5 %copy-start = (bf16[128,1024]{1,0:T(8,128)(2,1)S(1)}, bf16[128,1024]{1,0:T(8,128)(2,1)}, u32[]{:S(2)}) copy-start(bf16[128,1024]{1,0:T(8,128)(2,1)} %map_ref.7) | copy-start | bytes 786436
  40.3 31.4 %collective-permute-start.1 = (bf16[1072,128]{1,0:T(8,128)(2,1)}, bf16[1072,128]{1,0:T(8,128)(2,1)}, u32[]{:S(2)}, u32[]{:S(2)}) collective-permute-start(bf16[1072,128]{1,0:T(8,128)(2,1)} %shard_map.69), channel_id=1, source_target_pairs={{0,16},{1,17},{2,18},{3,19},{4,20},{5,21},{6,22},{7,23},{8,24},{9,... | collective-permute-start | bytes 823304 | tf_op jit(solution)/shard_map/ppermute | solution.py:300
  51.6 1.9 %copy-start.3 = (bf16[8,256,1024]{2,1,0:T(8,128)(2,1)}, bf16[8,256,1024]{2,1,0:T(8,128)(2,1)S(1)}, u32[]{:S(2)}) copy-start(bf16[8,256,1024]{2,1,0:T(8,128)(2,1)S(1)} %get-tuple-element.11.feat_ref) | copy-start | bytes 12582916
  53.6 1.0 copy-start.8
  54.6 10.7 %copy-start.11 = (f32[512]{0:T(512)S(1)}, f32[512]{0:T(512)}, u32[]{:S(2)}) copy-start(f32[512]{0:T(512)} %param.11) | copy-start | bytes 6148
  58.6 6.7 %copy-start.1 = (bf16[128,1024]{1,0:T(8,128)(2,1)S(1)}, bf16[128,1024]{1,0:T(8,128)(2,1)}, u32[]{:S(2)}) copy-start(bf16[128,1024]{1,0:T(8,128)(2,1)} %map_ref.7) | copy-start | bytes 786436
  61.2 10.5 %copy-start.9 = (f32[8,256,128]{2,1,0:T(8,128)S(1)}, f32[8,256,128]{2,1,0:T(8,128)}, u32[]{:S(2)}) copy-start(f32[8,256,128]{2,1,0:T(8,128)} %copy-done.8) | copy-start | bytes 3145732
  61.2 16.6 %collective-permute-start = (bf16[1072,128]{1,0:T(8,128)(2,1)S(1)}, bf16[1072,128]{1,0:T(8,128)(2,1)S(1)}, u32[]{:S(2)}, u32[]{:S(2)}) collective-permute-start(bf16[1072,128]{1,0:T(8,128)(2,1)S(1)} %shard_map.67), channel_id=1, source_target_pairs={{0,16},{16,0},{1,17},{17,1},{2,18},{18,2},{3,19},{19,3},{4,20},{20... | collective-permute-start | bytes 823304 | tf_op jit(solution)/shard_map/ppermute | solution.py:300
  71.7 2.2 %copy-start.4 = (bf16[8,256,1024]{2,1,0:T(8,128)(2,1)S(1)}, bf16[8,256,1024]{2,1,0:T(8,128)(2,1)}, u32[]{:S(2)}) copy-start(bf16[8,256,1024]{2,1,0:T(8,128)(2,1)} %copy-done.3) | copy-start | bytes 12582916

commit v6 on v5

--- a/solution.py
+++ b/solution.py
@@ -72,13 +72,10 @@
             out_ref[owner, member] = source[:, start : start + DH]
 
 
-def unpack_kernel(x_ref, out_ref):
-    parts, members, heads, _, _ = x_ref.shape
-    for member in range(members):
-        for part in range(parts):
-            for head in range(heads):
-                start = ((member * parts + part) * heads + head) * DH
-                out_ref[:, start : start + DH] = x_ref[part, member, head]
+def unpack_kernel(starts, x_ref, out_ref):
+    for head, owners in enumerate(starts):
+        for owner, start in enumerate(owners):
+            out_ref[:, start : start + DH] = x_ref[owner, head]
 
 
 def high_low(x):
@@ -262,7 +259,7 @@
     narrow = pltpu.VMEM((TAIL + BLOCK, DH), jnp.float32)
     whole_state = pltpu.VMEM((features, DH), jnp.float32)
     chunks = size // rows
-    xs, sents, spans_done = [], [], []
+    attended = []
     for head in range(heads):
         taps = weights[:, :, head * DH : (head + 1) * DH]
         packed = shaped((count, 3, rows, DH))
@@ -282,8 +279,8 @@
         else:
             (x,) = whole_call(functools.partial(pack_whole_kernel, starts[head]), inputs, [packed])
         x = exchange(x)
-        if spans_done:
-            x = after(x, spans_done[-1][1])
+        if attended:
+            x = after(x, attended[-1])
         halo = jnp.zeros((3, RIM, DH), jnp.bfloat16)
         if spans > 2:
             halo = next_span(x[count - 1, :, rows - RIM :], spans)
@@ -304,7 +301,7 @@
             earlier = jnp.where((jnp.arange(spans) < mine)[:, None, None], gathered, 0.0)
             state = jnp.sum(earlier, 0).astype(jnp.bfloat16)
             came = jnp.concatenate([state, halo.reshape(3 * RIM, DH)])
-        done = whole_call(
+        partial, feats = whole_call(
             span_kernel,
             [x, taps, feature_map, map_t],
             [
@@ -313,28 +310,19 @@
             ],
             [tall, tall, tall, whole_state],
         )
-        xs.append((x, came, taps))
-        sents.append(sent)
-        spans_done.append(done)
-
-    attended = []
-    for head in range(heads):
-        x, came, taps = xs[head]
-        partial, feats = spans_done[head]
         gain = gains[:, head * DH : (head + 1) * DH]
-        if head < heads - 1:
-            gain = after(gain, sents[-1])
         others = attended if head == heads - 1 else []
-        piece = shaped((count, len(others) + 1, rows, DH))
         (out,) = whole_call(
             finish_kernel,
             [x, came, taps, feature_map, map_t, partial, feats, gain, *others],
-            [piece],
+            [shaped((count, len(others) + 1, rows, DH))],
             [narrow, narrow, narrow],
         )
         attended.append(out)
-    landed = exchange(attended[-1]).reshape(parts, members, heads, rows, DH)
-    (result,) = whole_call(unpack_kernel, [landed], [shaped((rows, model))])
+    landed = exchange(attended[-1])
+    (result,) = whole_call(
+        functools.partial(unpack_kernel, starts), [landed], [shaped((rows, model))]
+    )
     return result
 
 

time: 104 us -> 105 us (level)
  waiting for transfers between devices: 22.6 us -> 33.2 us
  local copies, waits for them, and re-layouts: 11.2 us -> 6.87 us
  blocking collectives: 22.1 us -> 19.7 us
  Pallas kernels: 27.6 us -> 26 us
  starting transfers between devices: 19.5 us -> 18.3 us
    ppermute x2, waiting for transfers between devices: 0.96 us -> 15.6 us  [local(): came = lax.ppermute(sent, 'span', [(0, 1), (1, 0)] if both else [(0, 1)])]
    unnamed x25 -> x23, local copies, waits for them, and re-layouts: 11.1 us -> 6.77 us
    all_to_all x2, waiting for transfers between devices: 21.7 us -> 17.6 us  [exchange(): return lax.all_to_all(block, GROUP, split_axis=0, concat_axis=0, tiled=True)]
    all_to_all x1, blocking collectives: 22.1 us -> 19.7 us  [exchange(): return lax.all_to_all(block, GROUP, split_axis=0, concat_axis=0, tiled=True)]
    pallas_call x9, Pallas kernels: 27.6 us -> 26 us  [whole_call(): pl.pallas_call(kernel, in_specs=[read] * len(inputs), out_specs=[written]...]
    ppermute x2, starting transfers between devices: 9.25 us -> 8.14 us  [local(): came = lax.ppermute(sent, 'span', [(0, 1), (1, 0)] if both else [(0, 1)])]
  transfers between devices with their start and end apart: 4 -> 4, of which waited for: 3 -> 3; matrix products, arithmetic and copies ran while one was open for 1% -> 1% of each run, Pallas kernels for 21% -> 17%
where the time goes in v6:
time: 105 us; the launch traced here: 104 us
  waiting for transfers between devices  33.2 us (32%)
  Pallas kernels  26 us (25%)
  blocking collectives  19.7 us (19%)
  starting transfers between devices  18.3 us (17%)
  local copies, waits for them, and re-layouts  6.87 us (7%)
    pallas_call x9, Pallas kernels, whole_call(): pl.pallas_call(kernel, in_specs=[read] * len(inputs), out_specs=[written]...  26 us
    all_to_all x1, blocking collectives, exchange(): return lax.all_to_all(block, GROUP, split_axis=0, concat_axis=0, tiled=True)  19.7 us
    all_to_all x2, waiting for transfers between devices, exchange(): return lax.all_to_all(block, GROUP, split_axis=0, concat_axis=0, tiled=True)  17.6 us
    ppermute x2, waiting for transfers between devices, local(): came = lax.ppermute(sent, 'span', [(0, 1), (1, 0)] if both else [(0, 1)])  15.6 us
    all_to_all x2, starting transfers between devices, exchange(): return lax.all_to_all(block, GROUP, split_axis=0, concat_axis=0, tiled=True)  10.2 us
    ppermute x2, starting transfers between devices, local(): came = lax.ppermute(sent, 'span', [(0, 1), (1, 0)] if both else [(0, 1)])  8.14 us
    unnamed x23, local copies, waits for them, and re-layouts  6.77 us
  transfers between devices with their start and end apart: 4, of which 3 were waited for; matrix products, arithmetic and copies ran while one was open for 1% of the time, Pallas kernels for 17%

profile of v6, /device:TPU:0, one launch (start us, length us, event | category | flops | bytes accessed | tf_op | source)
XLA Modules:
  0.0 104.3 jit_solution(8888953282594070391)
XLA Ops:
  0.0 2.8 %shard_map.65 = bf16[16,3,128,128]{3,2,1,0:T(8,128)(2,1)} custom-call(bf16[128,4096]{1,0:T(8,128)(2,1)} %refs_0_.3, bf16[128,4096]{1,0:T(8,128)(2,1)} %refs_1_.3, bf16[128,4096]{1,0:T(8,128)(2,1)} %refs_2_.3), custom_call_target="tpu_custom_call" | custom-call | flops 1000 | bytes 1000 | tf_op jit(solution)/shard_map/pallas_call | solution.py:214
  2.8 6.3 %all-to-all-start.1 = ((bf16[16,3,128,128]{3,2,1,0:T(8,128)(2,1)}), bf16[16,3,128,128]{3,2,1,0:T(8,128)(2,1)S(1)}, u32[]{:S(2)}, u32[]{:S(2)}) async-start(bf16[16,3,128,128]{3,2,1,0:T(8,128)(2,1)} %shard_map.65), calls=%async_computation.1 | async-start | bytes 3145728 | tf_op jit(solution)/shard_map/all_to_all | solution.py:234
  9.2 0.0 copy-start.4
  9.2 1.2 %copy-done.4 = bf16[128,4096]{1,0:T(8,128)(2,1)S(1)} copy-done((bf16[128,4096]{1,0:T(8,128)(2,1)S(1)}, bf16[128,4096]{1,0:T(8,128)(2,1)}, u32[]{:S(2)}) %copy-start.4) | copy-done | bytes 1048600
  10.4 1.2 %copy-done.5 = bf16[128,4096]{1,0:T(8,128)(2,1)S(1)} copy-done((bf16[128,4096]{1,0:T(8,128)(2,1)S(1)}, bf16[128,4096]{1,0:T(8,128)(2,1)}, u32[]{:S(2)}) %copy-start.5) | copy-done | bytes 1048600
  11.6 1.2 %copy-done.6 = bf16[128,4096]{1,0:T(8,128)(2,1)S(1)} copy-done((bf16[128,4096]{1,0:T(8,128)(2,1)S(1)}, bf16[128,4096]{1,0:T(8,128)(2,1)}, u32[]{:S(2)}) %copy-start.6) | copy-done | bytes 1048600
  12.8 0.3 shard_map.64
  13.1 1.2 %copy-done.3 = bf16[16,3,128,128]{3,2,1,0:T(8,128)(2,1)} copy-done((bf16[16,3,128,128]{3,2,1,0:T(8,128)(2,1)}, bf16[16,3,128,128]{3,2,1,0:T(8,128)(2,1)S(1)}, u32[]{:S(2)}) %copy-start.3) | copy-done | bytes 1572888
  14.3 17.6 %all-to-all-done.1.x_ref = bf16[16,3,128,128]{3,2,1,0:T(8,128)(2,1)S(1)} async-done(((bf16[16,3,128,128]{3,2,1,0:T(8,128)(2,1)}), bf16[16,3,128,128]{3,2,1,0:T(8,128)(2,1)S(1)}, u32[]{:S(2)}, u32[]{:S(2)}) %all-to-all-start.1) | async-done | bytes 1572896 | tf_op jit(solution)/shard_map/all_to_all | solution.py:234
  31.9 3.9 %all-to-all-start = ((bf16[16,3,128,128]{3,2,1,0:T(8,128)(2,1)}), bf16[16,3,128,128]{3,2,1,0:T(8,128)(2,1)S(1)}, u32[]{:S(2)}, u32[]{:S(2)}) async-start(bf16[16,3,128,128]{3,2,1,0:T(8,128)(2,1)} %copy-done.3), calls=%async_computation | async-start | bytes 3145728 | tf_op jit(solution)/shard_map/all_to_all | solution.py:234
  35.8 0.0 copy-start.10
  35.9 1.1 %copy.7 = bf16[128,1024]{0,1:T(8,128)(2,1)S(1)} copy(bf16[128,1024]{1,0:T(8,128)(2,1)} %map_ref.7) | data formatting | bytes 524288 | tf_op args[4]
  37.0 0.0 copy-start
  37.0 2.6 %shard_map.66 = bf16[1072,128]{1,0:T(8,128)(2,1)S(1)} custom-call(bf16[16,3,128,128]{3,2,1,0:T(8,128)(2,1)S(1)} %all-to-all-done.1.x_ref, bf16[3,16,128]{2,1,0:T(8,128)(2,1)S(1)} %broadcast_1_halo_ref.2.halo_ref, f32[3,4,128]{2,1,0:T(4,128)S(1)} %get-tuple-element.16.w_ref, bf16[1024,128]{1,0:T(8,128)(2,1)S(1)} %bitcast.2), custom_call_target="tpu_custom_call" | custom-call | flops 1000 | bytes 1000 | tf_op jit(solution)/shard_map/pallas_call | solution.py:214
  39.6 4.7 %collective-permute-start = (bf16[1072,128]{1,0:T(8,128)(2,1)S(1)}, bf16[1072,128]{1,0:T(8,128)(2,1)S(1)}, u32[]{:S(2)}, u32[]{:S(2)}) collective-permute-start(bf16[1072,128]{1,0:T(8,128)(2,1)S(1)} %shard_map.66), channel_id=1, source_target_pairs={{0,16},{1,17},{2,18},{3,19},{4,20},{5,21},{6,22},{7,23},{8,24},{9,... | collective-permute-start | bytes 823304 | tf_op jit(solution)/shard_map/ppermute | solution.py:297
  44.3 0.1 dynamic_slice.7
  44.4 6.1 %shard_map.67 = (f32[8,256,128]{2,1,0:T(8,128)S(1)}, bf16[8,256,1024]{2,1,0:T(8,128)(2,1)S(1)}) custom-call(bf16[16,3,128,128]{3,2,1,0:T(8,128)(2,1)S(1)} %all-to-all-done.1.x_ref, f32[3,4,128]{2,1,0:T(4,128)S(1)} %get-tuple-element.16.w_ref, bf16[128,1024]{1,0:T(8,128)(2,1)S(1)} %copy-done, bf16[1024,128]{1,0:T(8,128)(2,1)S(1)} %bitcast.3), custom_call_target="tpu_custom_call" | custom-call | flops 1000 | bytes 1000 | tf_op jit(solution)/shard_map/pallas_call | solution.py:214
  50.5 9.4 %collective-permute-done.came_ref = bf16[1072,128]{1,0:T(8,128)(2,1)S(1)} collective-permute-done((bf16[1072,128]{1,0:T(8,128)(2,1)S(1)}, bf16[1072,128]{1,0:T(8,128)(2,1)S(1)}, u32[]{:S(2)}, u32[]{:S(2)}) %collective-permute-start) | collective-permute-done | bytes 274464 | tf_op jit(solution)/shard_map/ppermute | solution.py:297
  60.0 2.0 %shard_map.68.refs_0_ = bf16[16,1,128,128]{3,2,1,0:T(8,128)(2,1)S(1)} custom-call(bf16[16,3,128,128]{3,2,1,0:T(8,128)(2,1)S(1)} %all-to-all-done.1.x_ref, bf16[1072,128]{1,0:T(8,128)(2,1)S(1)} %collective-permute-done.came_ref, f32[3,4,128]{2,1,0:T(4,128)S(1)} %get-tuple-element.16.w_ref, bf16[128,1024]{1,0:T(8,128)(2,1)S(1)} %copy-done, ...), custom_call_target="tpu_custom_call" | custom-call | flops 1000 | bytes 1000 | tf_op jit(solution)/shard_map/pallas_call | solution.py:214
  62.0 0.0 copy-start.7
  62.0 0.8 copy-done.7
  62.8 0.0 all-to-all-done.x_ref
  62.8 2.6 %shard_map.69 = bf16[1072,128]{1,0:T(8,128)(2,1)S(1)} custom-call(bf16[16,3,128,128]{3,2,1,0:T(8,128)(2,1)S(1)} %all-to-all-done.x_ref, bf16[3,16,128]{2,1,0:T(8,128)(2,1)S(1)} %broadcast_1_halo_ref.2.halo_ref, f32[3,4,128]{2,1,0:T(4,128)S(1)} %get-tuple-element.15.w_ref, bf16[1024,128]{1,0:T(8,128)(2,1)S(1)} %bitcast.5), custom_call_target="tpu_custom_call" | custom-call | flops 1000 | bytes 1000 | tf_op jit(solution)/shard_map/pallas_call | solution.py:214
  65.4 0.0 copy-start.2
  65.4 0.0 copy-start.8
  65.4 3.4 %collective-permute-start.1 = (bf16[1072,128]{1,0:T(8,128)(2,1)S(1)}, bf16[1072,128]{1,0:T(8,128)(2,1)S(1)}, u32[]{:S(2)}, u32[]{:S(2)}) collective-permute-start(bf16[1072,128]{1,0:T(8,128)(2,1)S(1)} %shard_map.69), channel_id=1, source_target_pairs={{0,16},{16,0},{1,17},{17,1},{2,18},{18,2},{3,19},{19,3},{4,20},{20... | collective-permute-start | bytes 823304 | tf_op jit(solution)/shard_map/ppermute | solution.py:297
  68.8 6.4 %shard_map.70 = (f32[8,256,128]{2,1,0:T(8,128)S(1)}, bf16[8,256,1024]{2,1,0:T(8,128)(2,1)S(1)}) custom-call(bf16[16,3,128,128]{3,2,1,0:T(8,128)(2,1)S(1)} %all-to-all-done.x_ref, f32[3,4,128]{2,1,0:T(4,128)S(1)} %get-tuple-element.15.w_ref, bf16[128,1024]{1,0:T(8,128)(2,1)S(1)} %copy-done.1, bf16[1024,128]{1,0:T(8,128)(2,1)S(1)} %bitcast.6), custom_call_target="tpu_custom_call" | custom-call | flops 1000 | bytes 1000 | tf_op jit(solution)/shard_map/pallas_call | solution.py:214
  75.2 6.1 %collective-permute-done.1.came_ref = bf16[1072,128]{1,0:T(8,128)(2,1)S(1)} collective-permute-done((bf16[1072,128]{1,0:T(8,128)(2,1)S(1)}, bf16[1072,128]{1,0:T(8,128)(2,1)S(1)}, u32[]{:S(2)}, u32[]{:S(2)}) %collective-permute-start.1) | collective-permute-done | bytes 274464 | tf_op jit(solution)/shard_map/ppermute | solution.py:297
  81.4 0.0 copy-done.8
  81.4 2.0 %shard_map.71 = bf16[16,2,128,128]{3,2,1,0:T(8,128)(2,1)S(1)} custom-call(bf16[16,3,128,128]{3,2,1,0:T(8,128)(2,1)S(1)} %all-to-all-done.x_ref, bf16[1072,128]{1,0:T(8,128)(2,1)S(1)} %collective-permute-done.1.came_ref, f32[3,4,128]{2,1,0:T(4,128)S(1)} %get-tuple-element.15.w_ref, bf16[128,1024]{1,0:T(8,128)(2,1)S(1)} %copy-done.2, ...), custom_call_target="tpu_custom_call" | custom-call | flops 1000 | bytes 1000 | tf_op jit(solution)/shard_map/pallas_call | solution.py:214
  83.4 19.7 %all_to_all.15.x_ref = bf16[16,2,128,128]{3,2,1,0:T(8,128)(2,1)S(1)} all-to-all(bf16[16,2,128,128]{3,2,1,0:T(8,128)(2,1)S(1)} %shard_map.71), channel_id=1, replica_groups=mesh['span'=2,'part'=2,'sp'=8] {'part','sp'}, dimensions={0} | all-to-all | bytes 2097152 | tf_op jit(solution)/shard_map/all_to_all | solution.py:234
  103.1 1.2 %shard_map.72 = bf16[128,4096]{1,0:T(8,128)(2,1)} custom-call(bf16[16,2,128,128]{3,2,1,0:T(8,128)(2,1)S(1)} %all_to_all.15.x_ref), custom_call_target="tpu_custom_call" | custom-call | flops 1000 | bytes 1000 | tf_op jit(solution)/shard_map/pallas_call | solution.py:214
  (13 shorter events, 0.0 us)
Async XLA Ops:
  2.8 29.1 %all-to-all-start.1 = ((bf16[16,3,128,128]{3,2,1,0:T(8,128)(2,1)}), bf16[16,3,128,128]{3,2,1,0:T(8,128)(2,1)S(1)}, u32[]{:S(2)}, u32[]{:S(2)}) async-start(bf16[16,3,128,128]{3,2,1,0:T(8,128)(2,1)} %shard_map.65), calls=%async_computation.1 | async-start | bytes 3145728 | tf_op jit(solution)/shard_map/all_to_all | solution.py:234
  9.2 1.2 %copy-start.4 = (bf16[128,4096]{1,0:T(8,128)(2,1)S(1)}, bf16[128,4096]{1,0:T(8,128)(2,1)}, u32[]{:S(2)}) copy-start(bf16[128,4096]{1,0:T(8,128)(2,1)} %refs_0_.3) | copy-start | bytes 3145732
  10.4 1.2 %copy-start.5 = (bf16[128,4096]{1,0:T(8,128)(2,1)S(1)}, bf16[128,4096]{1,0:T(8,128)(2,1)}, u32[]{:S(2)}) copy-start(bf16[128,4096]{1,0:T(8,128)(2,1)} %refs_1_.3) | copy-start | bytes 3145732
  11.6 1.2 %copy-start.6 = (bf16[128,4096]{1,0:T(8,128)(2,1)S(1)}, bf16[128,4096]{1,0:T(8,128)(2,1)}, u32[]{:S(2)}) copy-start(bf16[128,4096]{1,0:T(8,128)(2,1)} %refs_2_.3) | copy-start | bytes 3145732
  13.1 1.2 %copy-start.3 = (bf16[16,3,128,128]{3,2,1,0:T(8,128)(2,1)}, bf16[16,3,128,128]{3,2,1,0:T(8,128)(2,1)S(1)}, u32[]{:S(2)}) copy-start(bf16[16,3,128,128]{3,2,1,0:T(8,128)(2,1)S(1)} %shard_map.64) | copy-start | bytes 4718596
  14.3 22.7 %copy-start.9 = (f32[3,4,512]{2,1,0:T(4,128)S(1)}, f32[3,4,512]{2,1,0:T(4,128)}, u32[]{:S(2)}) copy-start(f32[3,4,512]{2,1,0:T(4,128)} %param.9) | copy-start | bytes 73732
  31.9 30.9 %all-to-all-start = ((bf16[16,3,128,128]{3,2,1,0:T(8,128)(2,1)}), bf16[16,3,128,128]{3,2,1,0:T(8,128)(2,1)S(1)}, u32[]{:S(2)}, u32[]{:S(2)}) async-start(bf16[16,3,128,128]{3,2,1,0:T(8,128)(2,1)} %copy-done.3), calls=%async_computation | async-start | bytes 3145728 | tf_op jit(solution)/shard_map/all_to_all | solution.py:234
  35.8 8.5 %copy-start.10 = (f32[512]{0:T(512)S(1)}, f32[512]{0:T(512)}, u32[]{:S(2)}) copy-start(f32[512]{0:T(512)} %param.11) | copy-start | bytes 6148
  37.0 7.4 %copy-start = (bf16[128,1024]{1,0:T(8,128)(2,1)S(1)}, bf16[128,1024]{1,0:T(8,128)(2,1)}, u32[]{:S(2)}) copy-start(bf16[128,1024]{1,0:T(8,128)(2,1)} %map_ref.7) | copy-start | bytes 786436
  39.6 20.4 %collective-permute-start = (bf16[1072,128]{1,0:T(8,128)(2,1)S(1)}, bf16[1072,128]{1,0:T(8,128)(2,1)S(1)}, u32[]{:S(2)}, u32[]{:S(2)}) collective-permute-start(bf16[1072,128]{1,0:T(8,128)(2,1)S(1)} %shard_map.66), channel_id=1, source_target_pairs={{0,16},{1,17},{2,18},{3,19},{4,20},{5,21},{6,22},{7,23},{8,24},{9,... | collective-permute-start | bytes 823304 | tf_op jit(solution)/shard_map/ppermute | solution.py:297
  62.0 0.8 copy-start.7
  62.8 6.1 %copy-start.1 = (bf16[128,1024]{1,0:T(8,128)(2,1)S(1)}, bf16[128,1024]{1,0:T(8,128)(2,1)}, u32[]{:S(2)}) copy-start(bf16[128,1024]{1,0:T(8,128)(2,1)} %map_ref.7) | copy-start | bytes 786436
  65.4 16.0 %copy-start.2 = (bf16[128,1024]{1,0:T(8,128)(2,1)S(1)}, bf16[128,1024]{1,0:T(8,128)(2,1)}, u32[]{:S(2)}) copy-start(bf16[128,1024]{1,0:T(8,128)(2,1)} %map_ref.7) | copy-start | bytes 786436
  65.4 16.0 %copy-start.8 = (bf16[16,1,128,128]{3,2,1,0:T(8,128)(2,1)S(1)}, bf16[16,1,128,128]{3,2,1,0:T(8,128)(2,1)}, u32[]{:S(2)}) copy-start(bf16[16,1,128,128]{3,2,1,0:T(8,128)(2,1)} %copy-done.7) | copy-start | bytes 1572868
  65.4 16.0 %collective-permute-start.1 = (bf16[1072,128]{1,0:T(8,128)(2,1)S(1)}, bf16[1072,128]{1,0:T(8,128)(2,1)S(1)}, u32[]{:S(2)}, u32[]{:S(2)}) collective-permute-start(bf16[1072,128]{1,0:T(8,128)(2,1)S(1)} %shard_map.69), channel_id=1, source_target_pairs={{0,16},{16,0},{1,17},{17,1},{2,18},{18,2},{3,19},{19,3},{4,20},{20... | collective-permute-start | bytes 823304 | tf_op jit(solution)/shard_map/ppermute | solution.py:297

commit v7 on v5

--- a/solution.py
+++ b/solution.py
@@ -204,7 +204,7 @@
         put(begin, end, part_ref[begin:end].reshape(extent, DH) + folded(dot(feats, later)))
 
 
-LIMIT = 24 * 1024 * 1024
+LIMIT = 14 * 1024 * 1024
 MOST = 60 * 1024 * 1024
 VMEM = pl.BlockSpec(memory_space=pltpu.VMEM)
 HBM = pl.BlockSpec(memory_space=pltpu.HBM)

time: 104 us -> 104 us (level)
  no operation moved by 1% of the time
where the time goes in v7:
time: 104 us; the launch traced here: 103 us
  Pallas kernels  27.6 us (27%)
  waiting for transfers between devices  22.6 us (22%)
  blocking collectives  22.1 us (21%)
  starting transfers between devices  19.5 us (19%)
  local copies, waits for them, and re-layouts  11.2 us (11%)
    pallas_call x9, Pallas kernels, whole_call(): pl.pallas_call(kernel, in_specs=[read] * len(inputs), out_specs=[written]...  27.6 us
    all_to_all x1, blocking collectives, exchange(): return lax.all_to_all(block, GROUP, split_axis=0, concat_axis=0, tiled=True)  22.1 us
    all_to_all x2, waiting for transfers between devices, exchange(): return lax.all_to_all(block, GROUP, split_axis=0, concat_axis=0, tiled=True)  21.7 us
    unnamed x25, local copies, waits for them, and re-layouts  11.1 us
    all_to_all x2, starting transfers between devices, exchange(): return lax.all_to_all(block, GROUP, split_axis=0, concat_axis=0, tiled=True)  10.2 us
    ppermute x2, starting transfers between devices, local(): came = lax.ppermute(sent, 'span', [(0, 1), (1, 0)] if both else [(0, 1)])  9.25 us
  transfers between devices with their start and end apart: 4, of which 3 were waited for; matrix products, arithmetic and copies ran while one was open for 1% of the time, Pallas kernels for 21%

profile of v7, /device:TPU:0, one launch (start us, length us, event | category | flops | bytes accessed | tf_op | source)
XLA Modules:
  0.0 103.1 jit_solution(10581163608262144344)
XLA Ops:
  0.0 2.8 %shard_map.65 = bf16[16,3,128,128]{3,2,1,0:T(8,128)(2,1)} custom-call(bf16[128,4096]{1,0:T(8,128)(2,1)} %refs_0_.3, bf16[128,4096]{1,0:T(8,128)(2,1)} %refs_1_.3, bf16[128,4096]{1,0:T(8,128)(2,1)} %refs_2_.3), custom_call_target="tpu_custom_call" | custom-call | flops 1000 | bytes 1000 | tf_op jit(solution)/shard_map/pallas_call | solution.py:217
  2.8 6.3 %all-to-all-start.1 = ((bf16[16,3,128,128]{3,2,1,0:T(8,128)(2,1)}), bf16[16,3,128,128]{3,2,1,0:T(8,128)(2,1)S(1)}, u32[]{:S(2)}, u32[]{:S(2)}) async-start(bf16[16,3,128,128]{3,2,1,0:T(8,128)(2,1)} %shard_map.65), calls=%async_computation.1 | async-start | bytes 3145728 | tf_op jit(solution)/shard_map/all_to_all | solution.py:237
  9.2 0.0 copy-start.5
  9.2 1.2 %copy-done.5 = bf16[128,4096]{1,0:T(8,128)(2,1)S(1)} copy-done((bf16[128,4096]{1,0:T(8,128)(2,1)S(1)}, bf16[128,4096]{1,0:T(8,128)(2,1)}, u32[]{:S(2)}) %copy-start.5) | copy-done | bytes 1048600
  10.4 1.2 %copy-done.6 = bf16[128,4096]{1,0:T(8,128)(2,1)S(1)} copy-done((bf16[128,4096]{1,0:T(8,128)(2,1)S(1)}, bf16[128,4096]{1,0:T(8,128)(2,1)}, u32[]{:S(2)}) %copy-start.6) | copy-done | bytes 1048600
  11.6 1.2 %copy-done.7 = bf16[128,4096]{1,0:T(8,128)(2,1)S(1)} copy-done((bf16[128,4096]{1,0:T(8,128)(2,1)S(1)}, bf16[128,4096]{1,0:T(8,128)(2,1)}, u32[]{:S(2)}) %copy-start.7) | copy-done | bytes 1048600
  12.8 0.3 shard_map.64
  13.1 1.2 %copy-done.2 = bf16[16,3,128,128]{3,2,1,0:T(8,128)(2,1)} copy-done((bf16[16,3,128,128]{3,2,1,0:T(8,128)(2,1)}, bf16[16,3,128,128]{3,2,1,0:T(8,128)(2,1)S(1)}, u32[]{:S(2)}) %copy-start.2) | copy-done | bytes 1572888
  14.3 17.6 %all-to-all-done.1.x_ref = bf16[16,3,128,128]{3,2,1,0:T(8,128)(2,1)S(1)} async-done(((bf16[16,3,128,128]{3,2,1,0:T(8,128)(2,1)}), bf16[16,3,128,128]{3,2,1,0:T(8,128)(2,1)S(1)}, u32[]{:S(2)}, u32[]{:S(2)}) %all-to-all-start.1) | async-done | bytes 1572896 | tf_op jit(solution)/shard_map/all_to_all | solution.py:237
  31.9 3.9 %all-to-all-start = ((bf16[16,3,128,128]{3,2,1,0:T(8,128)(2,1)}), bf16[16,3,128,128]{3,2,1,0:T(8,128)(2,1)S(1)}, u32[]{:S(2)}, u32[]{:S(2)}) async-start(bf16[16,3,128,128]{3,2,1,0:T(8,128)(2,1)} %copy-done.2), calls=%async_computation | async-start | bytes 3145728 | tf_op jit(solution)/shard_map/all_to_all | solution.py:237
  35.8 1.1 %copy.7 = bf16[128,1024]{0,1:T(8,128)(2,1)S(1)} copy(bf16[128,1024]{1,0:T(8,128)(2,1)} %map_ref.7) | data formatting | bytes 524288 | tf_op args[4]
  37.0 0.0 copy-start
  37.0 3.3 %shard_map.69 = bf16[1072,128]{1,0:T(8,128)(2,1)} custom-call(bf16[16,3,128,128]{3,2,1,0:T(8,128)(2,1)S(1)} %all-to-all-done.1.x_ref, bf16[3,16,128]{2,1,0:T(8,128)(2,1)S(1)} %broadcast_1_halo_ref.2.halo_ref, f32[3,4,128]{2,1,0:T(4,128)S(1)} %get-tuple-element.18.w_ref, bf16[1024,128]{1,0:T(8,128)(2,1)S(1)} %bitcast.3), custom_call_target="tpu_custom_call" | custom-call | flops 1000 | bytes 1000 | tf_op jit(solution)/shard_map/pallas_call | solution.py:217
  40.3 5.2 %collective-permute-start.1 = (bf16[1072,128]{1,0:T(8,128)(2,1)}, bf16[1072,128]{1,0:T(8,128)(2,1)}, u32[]{:S(2)}, u32[]{:S(2)}) collective-permute-start(bf16[1072,128]{1,0:T(8,128)(2,1)} %shard_map.69), channel_id=1, source_target_pairs={{0,16},{1,17},{2,18},{3,19},{4,20},{5,21},{6,22},{7,23},{8,24},{9,... | collective-permute-start | bytes 823304 | tf_op jit(solution)/shard_map/ppermute | solution.py:300
  45.5 6.1 %shard_map.66 = (f32[8,256,128]{2,1,0:T(8,128)S(1)}, bf16[8,256,1024]{2,1,0:T(8,128)(2,1)S(1)}) custom-call(bf16[16,3,128,128]{3,2,1,0:T(8,128)(2,1)S(1)} %all-to-all-done.1.x_ref, f32[3,4,128]{2,1,0:T(4,128)S(1)} %get-tuple-element.18.w_ref, bf16[128,1024]{1,0:T(8,128)(2,1)S(1)} %copy-done, bf16[1024,128]{1,0:T(8,128)(2,1)S(1)} %bitcast.4), custom_call_target="tpu_custom_call" | custom-call | flops 1000 | bytes 1000 | tf_op jit(solution)/shard_map/pallas_call | solution.py:217
  51.6 0.0 copy-start.3
  51.6 1.9 %copy-done.3 = bf16[8,256,1024]{2,1,0:T(8,128)(2,1)} copy-done((bf16[8,256,1024]{2,1,0:T(8,128)(2,1)}, bf16[8,256,1024]{2,1,0:T(8,128)(2,1)S(1)}, u32[]{:S(2)}) %copy-start.3) | copy-done | bytes 4194328
  53.6 1.0 copy-done.8
  54.6 4.1 %all-to-all-done.x_ref = bf16[16,3,128,128]{3,2,1,0:T(8,128)(2,1)S(1)} async-done(((bf16[16,3,128,128]{3,2,1,0:T(8,128)(2,1)}), bf16[16,3,128,128]{3,2,1,0:T(8,128)(2,1)S(1)}, u32[]{:S(2)}, u32[]{:S(2)}) %all-to-all-start) | async-done | bytes 1572896 | tf_op jit(solution)/shard_map/all_to_all | solution.py:237
  58.6 2.6 %shard_map.67 = bf16[1072,128]{1,0:T(8,128)(2,1)S(1)} custom-call(bf16[16,3,128,128]{3,2,1,0:T(8,128)(2,1)S(1)} %all-to-all-done.x_ref, bf16[3,16,128]{2,1,0:T(8,128)(2,1)S(1)} %broadcast_1_halo_ref.2.halo_ref, f32[3,4,128]{2,1,0:T(4,128)S(1)} %get-tuple-element.17.w_ref, bf16[1024,128]{1,0:T(8,128)(2,1)S(1)} %bitcast.5), custom_call_target="tpu_custom_call" | custom-call | flops 1000 | bytes 1000 | tf_op jit(solution)/shard_map/pallas_call | solution.py:217
  61.2 0.0 copy-start.9
  61.2 4.1 %collective-permute-start = (bf16[1072,128]{1,0:T(8,128)(2,1)S(1)}, bf16[1072,128]{1,0:T(8,128)(2,1)S(1)}, u32[]{:S(2)}, u32[]{:S(2)}) collective-permute-start(bf16[1072,128]{1,0:T(8,128)(2,1)S(1)} %shard_map.67), channel_id=1, source_target_pairs={{0,16},{16,0},{1,17},{17,1},{2,18},{18,2},{3,19},{19,3},{4,20},{20... | collective-permute-start | bytes 823304 | tf_op jit(solution)/shard_map/ppermute | solution.py:300
  65.3 0.0 copy-done.11
  65.3 0.1 dynamic_slice.7
  65.3 6.3 %shard_map.68 = (f32[8,256,128]{2,1,0:T(8,128)S(1)}, bf16[8,256,1024]{2,1,0:T(8,128)(2,1)S(1)}) custom-call(bf16[16,3,128,128]{3,2,1,0:T(8,128)(2,1)S(1)} %all-to-all-done.x_ref, f32[3,4,128]{2,1,0:T(4,128)S(1)} %get-tuple-element.17.w_ref, bf16[128,1024]{1,0:T(8,128)(2,1)S(1)} %copy-done.1, bf16[1024,128]{1,0:T(8,128)(2,1)S(1)} %bitcast.6), custom_call_target="tpu_custom_call" | custom-call | flops 1000 | bytes 1000 | tf_op jit(solution)/shard_map/pallas_call | solution.py:217
  71.7 0.0 collective-permute-done.1.came_ref
  71.7 2.2 %copy-done.4 = bf16[8,256,1024]{2,1,0:T(8,128)(2,1)S(1)} copy-done((bf16[8,256,1024]{2,1,0:T(8,128)(2,1)S(1)}, bf16[8,256,1024]{2,1,0:T(8,128)(2,1)}, u32[]{:S(2)}) %copy-start.4) | copy-done | bytes 4194328
  73.9 2.9 %shard_map.70.refs_0_ = bf16[16,1,128,128]{3,2,1,0:T(8,128)(2,1)S(1)} custom-call(bf16[16,3,128,128]{3,2,1,0:T(8,128)(2,1)S(1)} %all-to-all-done.1.x_ref, bf16[1072,128]{1,0:T(8,128)(2,1)} %collective-permute-done.1.came_ref, f32[3,4,128]{2,1,0:T(4,128)S(1)} %get-tuple-element.18.w_ref, bf16[128,1024]{1,0:T(8,128)(2,1)S(1)} %copy-done.1, ...), custom_call_target="tpu_custom_call" | custom-call | flops 1000 | bytes 1000 | tf_op jit(solution)/shard_map/pallas_call | solution.py:217
  76.8 1.0 collective-permute-done.came_ref
  77.8 2.0 %shard_map.71 = bf16[16,2,128,128]{3,2,1,0:T(8,128)(2,1)S(1)} custom-call(bf16[16,3,128,128]{3,2,1,0:T(8,128)(2,1)S(1)} %all-to-all-done.x_ref, bf16[1072,128]{1,0:T(8,128)(2,1)S(1)} %collective-permute-done.came_ref, f32[3,4,128]{2,1,0:T(4,128)S(1)} %get-tuple-element.17.w_ref, bf16[128,1024]{1,0:T(8,128)(2,1)S(1)} %copy-done.1, ...), custom_call_target="tpu_custom_call" | custom-call | flops 1000 | bytes 1000 | tf_op jit(solution)/shard_map/pallas_call | solution.py:217
  79.8 22.1 %all_to_all.15 = bf16[16,2,128,128]{3,2,1,0:T(8,128)(2,1)S(1)} all-to-all(bf16[16,2,128,128]{3,2,1,0:T(8,128)(2,1)S(1)} %shard_map.71), channel_id=1, replica_groups=mesh['span'=2,'part'=2,'sp'=8] {'part','sp'}, dimensions={0} | all-to-all | bytes 2097152 | tf_op jit(solution)/shard_map/all_to_all | solution.py:237
  101.9 1.2 %shard_map.72 = bf16[128,4096]{1,0:T(8,128)(2,1)} custom-call(bf16[2,8,2,128,128]{4,3,2,1,0:T(8,128)(2,1)S(1)} %bitcast.9), custom_call_target="tpu_custom_call" | custom-call | flops 1000 | bytes 1000 | tf_op jit(solution)/shard_map/pallas_call | solution.py:217
  (15 shorter events, 0.0 us)
Async XLA Ops:
  2.8 29.1 %all-to-all-start.1 = ((bf16[16,3,128,128]{3,2,1,0:T(8,128)(2,1)}), bf16[16,3,128,128]{3,2,1,0:T(8,128)(2,1)S(1)}, u32[]{:S(2)}, u32[]{:S(2)}) async-start(bf16[16,3,128,128]{3,2,1,0:T(8,128)(2,1)} %shard_map.65), calls=%async_computation.1 | async-start | bytes 3145728 | tf_op jit(solution)/shard_map/all_to_all | solution.py:237
  9.2 1.2 %copy-start.5 = (bf16[128,4096]{1,0:T(8,128)(2,1)S(1)}, bf16[128,4096]{1,0:T(8,128)(2,1)}, u32[]{:S(2)}) copy-start(bf16[128,4096]{1,0:T(8,128)(2,1)} %refs_0_.3) | copy-start | bytes 3145732
  10.4 1.2 %copy-start.6 = (bf16[128,4096]{1,0:T(8,128)(2,1)S(1)}, bf16[128,4096]{1,0:T(8,128)(2,1)}, u32[]{:S(2)}) copy-start(bf16[128,4096]{1,0:T(8,128)(2,1)} %refs_1_.3) | copy-start | bytes 3145732
  11.6 1.2 %copy-start.7 = (bf16[128,4096]{1,0:T(8,128)(2,1)S(1)}, bf16[128,4096]{1,0:T(8,128)(2,1)}, u32[]{:S(2)}) copy-start(bf16[128,4096]{1,0:T(8,128)(2,1)} %refs_2_.3) | copy-start | bytes 3145732
  13.1 1.2 %copy-start.2 = (bf16[16,3,128,128]{3,2,1,0:T(8,128)(2,1)}, bf16[16,3,128,128]{3,2,1,0:T(8,128)(2,1)S(1)}, u32[]{:S(2)}) copy-start(bf16[16,3,128,128]{3,2,1,0:T(8,128)(2,1)S(1)} %shard_map.64) | copy-start | bytes 4718596
  14.3 22.7 %copy-start.10 = (f32[3,4,512]{2,1,0:T(4,128)S(1)}, f32[3,4,512]{2,1,0:T(4,128)}, u32[]{:S(2)}) copy-start(f32[3,4,512]{2,1,0:T(4,128)} %param.9) | copy-start | bytes 73732
  31.9 26.7 %all-to-all-start = ((bf16[16,3,128,128]{3,2,1,0:T(8,128)(2,1)}), bf16[16,3,128,128]{3,2,1,0:T(8,128)(2,1)S(1)}, u32[]{:S(2)}, u32[]{:S(2)}) async-start(bf16[16,3,128,128]{3,2,1,0:T(8,128)(2,1)} %copy-done.2), calls=%async_computation | async-start | bytes 3145728 | tf_op jit(solution)/shard_map/all_to_all | solution.py:237
  37.0 8.5 %copy-start = (bf16[128,1024]{1,0:T(8,128)(2,1)S(1)}, bf16[128,1024]{1,0:T(8,128)(2,1)}, u32[]{:S(2)}) copy-start(bf16[128,1024]{1,0:T(8,128)(2,1)} %map_ref.7) | copy-start | bytes 786436
  40.3 31.4 %collective-permute-start.1 = (bf16[1072,128]{1,0:T(8,128)(2,1)}, bf16[1072,128]{1,0:T(8,128)(2,1)}, u32[]{:S(2)}, u32[]{:S(2)}) collective-permute-start(bf16[1072,128]{1,0:T(8,128)(2,1)} %shard_map.69), channel_id=1, source_target_pairs={{0,16},{1,17},{2,18},{3,19},{4,20},{5,21},{6,22},{7,23},{8,24},{9,... | collective-permute-start | bytes 823304 | tf_op jit(solution)/shard_map/ppermute | solution.py:300
  51.6 1.9 %copy-start.3 = (bf16[8,256,1024]{2,1,0:T(8,128)(2,1)}, bf16[8,256,1024]{2,1,0:T(8,128)(2,1)S(1)}, u32[]{:S(2)}) copy-start(bf16[8,256,1024]{2,1,0:T(8,128)(2,1)S(1)} %get-tuple-element.11.feat_ref) | copy-start | bytes 12582916
  53.6 1.0 copy-start.8
  54.6 10.7 %copy-start.11 = (f32[512]{0:T(512)S(1)}, f32[512]{0:T(512)}, u32[]{:S(2)}) copy-start(f32[512]{0:T(512)} %param.11) | copy-start | bytes 6148
  58.6 6.7 %copy-start.1 = (bf16[128,1024]{1,0:T(8,128)(2,1)S(1)}, bf16[128,1024]{1,0:T(8,128)(2,1)}, u32[]{:S(2)}) copy-start(bf16[128,1024]{1,0:T(8,128)(2,1)} %map_ref.7) | copy-start | bytes 786436
  61.2 10.5 %copy-start.9 = (f32[8,256,128]{2,1,0:T(8,128)S(1)}, f32[8,256,128]{2,1,0:T(8,128)}, u32[]{:S(2)}) copy-start(f32[8,256,128]{2,1,0:T(8,128)} %copy-done.8) | copy-start | bytes 3145732
  61.2 16.6 %collective-permute-start = (bf16[1072,128]{1,0:T(8,128)(2,1)S(1)}, bf16[1072,128]{1,0:T(8,128)(2,1)S(1)}, u32[]{:S(2)}, u32[]{:S(2)}) collective-permute-start(bf16[1072,128]{1,0:T(8,128)(2,1)S(1)} %shard_map.67), channel_id=1, source_target_pairs={{0,16},{16,0},{1,17},{17,1},{2,18},{18,2},{3,19},{19,3},{4,20},{20... | collective-permute-start | bytes 823304 | tf_op jit(solution)/shard_map/ppermute | solution.py:300
  71.7 2.2 %copy-start.4 = (bf16[8,256,1024]{2,1,0:T(8,128)(2,1)S(1)}, bf16[8,256,1024]{2,1,0:T(8,128)(2,1)}, u32[]{:S(2)}) copy-start(bf16[8,256,1024]{2,1,0:T(8,128)(2,1)} %copy-done.3) | copy-start | bytes 12582916

commit v8 on v4

--- a/solution.py
+++ b/solution.py
@@ -329,6 +329,17 @@
             shaped((features + 3 * RIM, DH)),
             [tall, tall, whole_state],
         )
+        done = whole_call(
+            span_kernel,
+            [x, taps, feature_map, map_t],
+            [
+                shaped((blocks, BLOCK, DH), jnp.float32),
+                shaped((blocks, BLOCK, features)),
+            ],
+            [tall, tall, tall, whole_state],
+        )
+        if head < heads - 1:
+            sent = after(sent, done[0])
         if spans == 2:
             both = head == heads - 1
             came = lax.ppermute(sent, "span", [(0, 1), (1, 0)] if both else [(0, 1)])
@@ -338,15 +349,6 @@
             earlier = jnp.where((jnp.arange(spans) < mine)[:, None, None], gathered, 0.0)
             state = jnp.sum(earlier, 0).astype(jnp.bfloat16)
             came = jnp.concatenate([state, halo.reshape(3 * RIM, DH)])
-        done = whole_call(
-            span_kernel,
-            [x, taps, feature_map, map_t],
-            [
-                shaped((blocks, BLOCK, DH), jnp.float32),
-                shaped((blocks, BLOCK, features)),
-            ],
-            [tall, tall, tall, whole_state],
-        )
         xs.append((x, came, taps))
         sents.append(sent)
         spans_done.append(done)
@@ -368,16 +370,8 @@
         )
         attended.append(out)
     landed = exchange(attended[-1]).reshape(parts, members, heads, rows, DH)
-    held = max(1, members // 4)
-    return stepped(
-        unpack_kernel,
-        members // held,
-        [landed],
-        [pl.BlockSpec((parts, held, heads, rows, DH), lambda i: (0, i, 0, 0, 0))],
-        pl.BlockSpec((rows, held * parts * width), lambda i: (0, i)),
-        shaped((rows, model)),
-        [],
-    )
+    (result,) = whole_call(unpack_kernel, [landed], [shaped((rows, model))])
+    return result
 
 
 def solution(mesh):

time: 103 us -> 113 us (1.097)
  waiting for transfers between devices: 24.5 us -> 35.4 us
  blocking collectives: 20.3 us -> 25.2 us
  starting transfers between devices: 19.4 us -> 15 us
  Pallas kernels: 28.9 us -> 26.8 us
    all_to_all x2, waiting for transfers between devices: 21.2 us -> 29.2 us  [exchange(): return lax.all_to_all(block, GROUP, split_axis=0, concat_axis=0, tiled=True)]
    all_to_all x1, blocking collectives: 20.3 us -> 25.2 us  [exchange(): return lax.all_to_all(block, GROUP, split_axis=0, concat_axis=0, tiled=True)]
    ppermute x2, starting transfers between devices: 9.23 us -> 4.76 us  [local(): came = lax.ppermute(sent, 'span', [(0, 1), (1, 0)] if both else [(0, 1)])]
    ppermute x2, waiting for transfers between devices: 3.33 us -> 6.24 us  [local(): came = lax.ppermute(sent, 'span', [(0, 1), (1, 0)] if both else [(0, 1)])]
    pallas_call x3 -> x2, Pallas kernels: 8.51 us -> 6.13 us  [stepped(): pl.pallas_call(kernel, grid=(steps,), in_specs=specs, out_specs=out_specs...]
    pallas_call x6 -> x7, Pallas kernels: 20.3 us -> 20.6 us  [whole_call(): pl.pallas_call(kernel, in_specs=[read] * len(inputs), out_specs=[written]...]
  transfers between devices with their start and end apart: 4 -> 4, of which waited for: 3 -> 3; matrix products, arithmetic and copies ran while one was open for 1% -> 1% of each run, Pallas kernels for 22% -> 16%
where the time goes in v8:
time: 113 us
  waiting for transfers between devices  35.4 us (31%)
  Pallas kernels  26.8 us (24%)
  blocking collectives  25.2 us (22%)
  starting transfers between devices  15 us (13%)
  local copies, waits for them, and re-layouts  9.96 us (9%)
    all_to_all x2, waiting for transfers between devices, exchange(): return lax.all_to_all(block, GROUP, split_axis=0, concat_axis=0, tiled=True)  29.2 us
    all_to_all x1, blocking collectives, exchange(): return lax.all_to_all(block, GROUP, split_axis=0, concat_axis=0, tiled=True)  25.2 us
    pallas_call x7, Pallas kernels, whole_call(): pl.pallas_call(kernel, in_specs=[read] * len(inputs), out_specs=[written]...  20.6 us
    all_to_all x2, starting transfers between devices, exchange(): return lax.all_to_all(block, GROUP, split_axis=0, concat_axis=0, tiled=True)  10.2 us
    unnamed x25, local copies, waits for them, and re-layouts  9.86 us
    ppermute x2, waiting for transfers between devices, local(): came = lax.ppermute(sent, 'span', [(0, 1), (1, 0)] if both else [(0, 1)])  6.24 us
    pallas_call x2, Pallas kernels, stepped(): pl.pallas_call(kernel, grid=(steps,), in_specs=specs, out_specs=out_specs...  6.13 us
    ppermute x2, starting transfers between devices, local(): came = lax.ppermute(sent, 'span', [(0, 1), (1, 0)] if both else [(0, 1)])  4.76 us
  transfers between devices with their start and end apart: 4, of which 3 were waited for; matrix products, arithmetic and copies ran while one was open for 1% of the time, Pallas kernels for 16%

profile of v8, /device:TPU:0, one launch (start us, length us, event | category | flops | bytes accessed | tf_op | source)
XLA Modules:
  0.0 112.6 jit_solution(7902423066310119274)
XLA Ops:
  0.0 2.8 %shard_map.65 = bf16[16,3,128,128]{3,2,1,0:T(8,128)(2,1)} custom-call(bf16[128,4096]{1,0:T(8,128)(2,1)} %refs_0_.3, bf16[128,4096]{1,0:T(8,128)(2,1)} %refs_1_.3, bf16[128,4096]{1,0:T(8,128)(2,1)} %refs_2_.3), custom_call_target="tpu_custom_call" | custom-call | flops 1000 | bytes 1000 | tf_op jit(solution)/shard_map/pallas_call | solution.py:225
  2.8 6.3 %all-to-all-start.1 = ((bf16[16,3,128,128]{3,2,1,0:T(8,128)(2,1)}), bf16[16,3,128,128]{3,2,1,0:T(8,128)(2,1)S(1)}, u32[]{:S(2)}, u32[]{:S(2)}) async-start(bf16[16,3,128,128]{3,2,1,0:T(8,128)(2,1)} %shard_map.65), calls=%async_computation.1 | async-start | bytes 3145728 | tf_op jit(solution)/shard_map/all_to_all | solution.py:263
  9.2 0.0 copy-start.5
  9.2 1.2 %copy-done.5 = bf16[128,4096]{1,0:T(8,128)(2,1)S(1)} copy-done((bf16[128,4096]{1,0:T(8,128)(2,1)S(1)}, bf16[128,4096]{1,0:T(8,128)(2,1)}, u32[]{:S(2)}) %copy-start.5) | copy-done | bytes 1048600
  10.4 1.2 %copy-done.6 = bf16[128,4096]{1,0:T(8,128)(2,1)S(1)} copy-done((bf16[128,4096]{1,0:T(8,128)(2,1)S(1)}, bf16[128,4096]{1,0:T(8,128)(2,1)}, u32[]{:S(2)}) %copy-start.6) | copy-done | bytes 1048600
  11.6 1.2 %copy-done.7 = bf16[128,4096]{1,0:T(8,128)(2,1)S(1)} copy-done((bf16[128,4096]{1,0:T(8,128)(2,1)S(1)}, bf16[128,4096]{1,0:T(8,128)(2,1)}, u32[]{:S(2)}) %copy-start.7) | copy-done | bytes 1048600
  12.8 0.3 shard_map.64
  13.1 1.2 %copy-done.2 = bf16[16,3,128,128]{3,2,1,0:T(8,128)(2,1)} copy-done((bf16[16,3,128,128]{3,2,1,0:T(8,128)(2,1)}, bf16[16,3,128,128]{3,2,1,0:T(8,128)(2,1)S(1)}, u32[]{:S(2)}) %copy-start.2) | copy-done | bytes 1572888
  14.3 17.6 %all-to-all-done.1.x_ref.k_ref.v_ref.rim_ref = bf16[16,3,128,128]{3,2,1,0:T(8,128)(2,1)S(1)} async-done(((bf16[16,3,128,128]{3,2,1,0:T(8,128)(2,1)}), bf16[16,3,128,128]{3,2,1,0:T(8,128)(2,1)S(1)}, u32[]{:S(2)}, u32[]{:S(2)}) %all-to-all-start.1) | async-done | bytes 1572896 | tf_op jit(solution)/shard_map/all_to_all | solution.py:263
  31.9 3.9 %all-to-all-start = ((bf16[16,3,128,128]{3,2,1,0:T(8,128)(2,1)}), bf16[16,3,128,128]{3,2,1,0:T(8,128)(2,1)S(1)}, u32[]{:S(2)}, u32[]{:S(2)}) async-start(bf16[16,3,128,128]{3,2,1,0:T(8,128)(2,1)} %copy-done.2), calls=%async_computation | async-start | bytes 3145728 | tf_op jit(solution)/shard_map/all_to_all | solution.py:263
  35.8 1.1 copy.7
  37.0 0.0 copy-start
  37.0 0.9 copy-done
  38.0 6.1 %shard_map.66 = (f32[8,256,128]{2,1,0:T(8,128)S(1)}, bf16[8,256,1024]{2,1,0:T(8,128)(2,1)S(1)}) custom-call(bf16[16,3,128,128]{3,2,1,0:T(8,128)(2,1)S(1)} %all-to-all-done.1.x_ref.k_ref.v_ref.rim_ref, f32[3,4,128]{2,1,0:T(4,128)S(1)} %get-tuple-element.20.w_ref, bf16[128,1024]{1,0:T(8,128)(2,1)S(1)} %copy-done, bf16[1024,128]{1,0:T(8,128)(2,1)S(1)} %bitcast.3), custom_call_target="tpu_custom_call" | custom-call | flops 1000 | bytes 1000 | tf_op jit(solution)/shard_map/pallas_call | solution.py:225
  44.1 1.9 %copy-done.3 = bf16[8,256,1024]{2,1,0:T(8,128)(2,1)} copy-done((bf16[8,256,1024]{2,1,0:T(8,128)(2,1)}, bf16[8,256,1024]{2,1,0:T(8,128)(2,1)S(1)}, u32[]{:S(2)}) %copy-start.3) | copy-done | bytes 4194328
  46.0 1.0 copy-done.8
  47.0 11.6 %all-to-all-done.k_ref.v_ref.rim_ref.x_ref = bf16[16,3,128,128]{3,2,1,0:T(8,128)(2,1)S(1)} async-done(((bf16[16,3,128,128]{3,2,1,0:T(8,128)(2,1)}), bf16[16,3,128,128]{3,2,1,0:T(8,128)(2,1)S(1)}, u32[]{:S(2)}, u32[]{:S(2)}) %all-to-all-start) | async-done | bytes 1572896 | tf_op jit(solution)/shard_map/all_to_all | solution.py:263
  58.6 3.1 %shard_map.69 = bf16[1072,128]{1,0:T(8,128)(2,1)S(1)} custom-call(bf16[16,3,128,128]{3,2,1,0:T(8,128)(2,1)S(1)} %all-to-all-done.1.x_ref.k_ref.v_ref.rim_ref, bf16[16,3,128,128]{3,2,1,0:T(8,128)(2,1)S(1)} %all-to-all-done.1.x_ref.k_ref.v_ref.rim_ref, bf16[16,3,128,128]{3,2,1,0:T(8,128)(2,1)S(1)} %all-to-all-done.1.x_ref.k_ref.v_ref.rim_ref, ...), custom_call_target="tpu_custom_call" | custom-call | flops 1000 | bytes 1000 | tf_op jit(solution)/shard_map/pallas_call | solution.py:237
  61.7 4.7 %collective-permute-start.1 = (bf16[1072,128]{1,0:T(8,128)(2,1)S(1)}, bf16[1072,128]{1,0:T(8,128)(2,1)S(1)}, u32[]{:S(2)}, u32[]{:S(2)}) collective-permute-start(bf16[1072,128]{1,0:T(8,128)(2,1)S(1)} %shard_map.69), channel_id=1, source_target_pairs={{0,16},{1,17},{2,18},{3,19},{4,20},{5,21},{6,22},{7,23},{8,24},{9,... | collective-permute-start | bytes 823304 | tf_op jit(solution)/shard_map/ppermute | solution.py:345
  66.4 0.0 copy-start.11
  66.4 0.0 copy-start.1
  66.4 3.1 %shard_map.67 = bf16[1072,128]{1,0:T(8,128)(2,1)S(1)} custom-call(bf16[16,3,128,128]{3,2,1,0:T(8,128)(2,1)S(1)} %all-to-all-done.k_ref.v_ref.rim_ref.x_ref, bf16[16,3,128,128]{3,2,1,0:T(8,128)(2,1)S(1)} %all-to-all-done.k_ref.v_ref.rim_ref.x_ref, bf16[16,3,128,128]{3,2,1,0:T(8,128)(2,1)S(1)} %all-to-all-done.k_ref.v_ref.rim_ref.x_ref, ...), custom_call_target="tpu_custom_call" | custom-call | flops 1000 | bytes 1000 | tf_op jit(solution)/shard_map/pallas_call | solution.py:237
  69.5 0.0 copy-start.9
  69.5 0.1 collective-permute-start
  69.6 0.1 dynamic_slice.7
  69.7 6.1 %shard_map.68 = (f32[8,256,128]{2,1,0:T(8,128)S(1)}, bf16[8,256,1024]{2,1,0:T(8,128)(2,1)S(1)}) custom-call(bf16[16,3,128,128]{3,2,1,0:T(8,128)(2,1)S(1)} %all-to-all-done.k_ref.v_ref.rim_ref.x_ref, f32[3,4,128]{2,1,0:T(4,128)S(1)} %get-tuple-element.19.w_ref, bf16[128,1024]{1,0:T(8,128)(2,1)S(1)} %copy-done.1, bf16[1024,128]{1,0:T(8,128)(2,1)S(1)} %bitcast.6), custom_call_target="tpu_custom_call" | custom-call | flops 1000 | bytes 1000 | tf_op jit(solution)/shard_map/pallas_call | solution.py:225
  75.8 0.0 collective-permute-done.1.came_ref
  75.8 2.0 %shard_map.70.refs_0_ = bf16[16,1,128,128]{3,2,1,0:T(8,128)(2,1)S(1)} custom-call(bf16[16,3,128,128]{3,2,1,0:T(8,128)(2,1)S(1)} %all-to-all-done.1.x_ref.k_ref.v_ref.rim_ref, bf16[1072,128]{1,0:T(8,128)(2,1)S(1)} %collective-permute-done.1.came_ref, f32[3,4,128]{2,1,0:T(4,128)S(1)} %get-tuple-element.20.w_ref, bf16[128,1024]{1,0:T(8,128)(2,1)S(1)} %copy-done.1, ...), custom_call_target="tpu_custom_call" | custom-call | flops 1000 | bytes 1000 | tf_op jit(solution)/shard_map/pallas_call | solution.py:225
  77.9 6.2 %collective-permute-done.came_ref = bf16[1072,128]{1,0:T(8,128)(2,1)S(1)} collective-permute-done((bf16[1072,128]{1,0:T(8,128)(2,1)S(1)}, bf16[1072,128]{1,0:T(8,128)(2,1)S(1)}, u32[]{:S(2)}, u32[]{:S(2)}) %collective-permute-start) | collective-permute-done | bytes 274464 | tf_op jit(solution)/shard_map/ppermute | solution.py:345
  84.1 2.0 %shard_map.71 = bf16[16,2,128,128]{3,2,1,0:T(8,128)(2,1)S(1)} custom-call(bf16[16,3,128,128]{3,2,1,0:T(8,128)(2,1)S(1)} %all-to-all-done.k_ref.v_ref.rim_ref.x_ref, bf16[1072,128]{1,0:T(8,128)(2,1)S(1)} %collective-permute-done.came_ref, f32[3,4,128]{2,1,0:T(4,128)S(1)} %get-tuple-element.19.w_ref, bf16[128,1024]{1,0:T(8,128)(2,1)S(1)} %copy-done.1, ...), custom_call_target="tpu_custom_call" | custom-call | flops 1000 | bytes 1000 | tf_op jit(solution)/shard_map/pallas_call | solution.py:225
  86.1 25.2 %all_to_all.15 = bf16[16,2,128,128]{3,2,1,0:T(8,128)(2,1)S(1)} all-to-all(bf16[16,2,128,128]{3,2,1,0:T(8,128)(2,1)S(1)} %shard_map.71), channel_id=1, replica_groups=mesh['span'=2,'part'=2,'sp'=8] {'part','sp'}, dimensions={0} | all-to-all | bytes 2097152 | tf_op jit(solution)/shard_map/all_to_all | solution.py:263
  111.4 1.2 %shard_map.72 = bf16[128,4096]{1,0:T(8,128)(2,1)} custom-call(bf16[2,8,2,128,128]{4,3,2,1,0:T(8,128)(2,1)S(1)} %bitcast.9), custom_call_target="tpu_custom_call" | custom-call | flops 1000 | bytes 1000 | tf_op jit(solution)/shard_map/pallas_call | solution.py:225
  (15 shorter events, 0.0 us)
Async XLA Ops:
  2.8 29.1 %all-to-all-start.1 = ((bf16[16,3,128,128]{3,2,1,0:T(8,128)(2,1)}), bf16[16,3,128,128]{3,2,1,0:T(8,128)(2,1)S(1)}, u32[]{:S(2)}, u32[]{:S(2)}) async-start(bf16[16,3,128,128]{3,2,1,0:T(8,128)(2,1)} %shard_map.65), calls=%async_computation.1 | async-start | bytes 3145728 | tf_op jit(solution)/shard_map/all_to_all | solution.py:263
  9.2 1.2 %copy-start.5 = (bf16[128,4096]{1,0:T(8,128)(2,1)S(1)}, bf16[128,4096]{1,0:T(8,128)(2,1)}, u32[]{:S(2)}) copy-start(bf16[128,4096]{1,0:T(8,128)(2,1)} %refs_0_.3) | copy-start | bytes 3145732
  10.4 1.2 %copy-start.6 = (bf16[128,4096]{1,0:T(8,128)(2,1)S(1)}, bf16[128,4096]{1,0:T(8,128)(2,1)}, u32[]{:S(2)}) copy-start(bf16[128,4096]{1,0:T(8,128)(2,1)} %refs_1_.3) | copy-start | bytes 3145732
  11.6 1.2 %copy-start.7 = (bf16[128,4096]{1,0:T(8,128)(2,1)S(1)}, bf16[128,4096]{1,0:T(8,128)(2,1)}, u32[]{:S(2)}) copy-start(bf16[128,4096]{1,0:T(8,128)(2,1)} %refs_2_.3) | copy-start | bytes 3145732
  13.1 1.2 %copy-start.2 = (bf16[16,3,128,128]{3,2,1,0:T(8,128)(2,1)}, bf16[16,3,128,128]{3,2,1,0:T(8,128)(2,1)S(1)}, u32[]{:S(2)}) copy-start(bf16[16,3,128,128]{3,2,1,0:T(8,128)(2,1)S(1)} %shard_map.64) | copy-start | bytes 4718596
  14.3 22.7 %copy-start.10 = (f32[3,4,512]{2,1,0:T(4,128)S(1)}, f32[3,4,512]{2,1,0:T(4,128)}, u32[]{:S(2)}) copy-start(f32[3,4,512]{2,1,0:T(4,128)} %param.9) | copy-start | bytes 73732
  31.9 26.7 %all-to-all-start = ((bf16[16,3,128,128]{3,2,1,0:T(8,128)(2,1)}), bf16[16,3,128,128]{3,2,1,0:T(8,128)(2,1)S(1)}, u32[]{:S(2)}, u32[]{:S(2)}) async-start(bf16[16,3,128,128]{3,2,1,0:T(8,128)(2,1)} %copy-done.2), calls=%async_computation | async-start | bytes 3145728 | tf_op jit(solution)/shard_map/all_to_all | solution.py:263
  37.0 1.0 copy-start
  44.1 1.9 %copy-start.3 = (bf16[8,256,1024]{2,1,0:T(8,128)(2,1)}, bf16[8,256,1024]{2,1,0:T(8,128)(2,1)S(1)}, u32[]{:S(2)}) copy-start(bf16[8,256,1024]{2,1,0:T(8,128)(2,1)S(1)} %get-tuple-element.12.feat_ref) | copy-start | bytes 12582916
  46.0 1.0 copy-start.8
  61.7 14.1 %collective-permute-start.1 = (bf16[1072,128]{1,0:T(8,128)(2,1)S(1)}, bf16[1072,128]{1,0:T(8,128)(2,1)S(1)}, u32[]{:S(2)}, u32[]{:S(2)}) collective-permute-start(bf16[1072,128]{1,0:T(8,128)(2,1)S(1)} %shard_map.69), channel_id=1, source_target_pairs={{0,16},{1,17},{2,18},{3,19},{4,20},{5,21},{6,22},{7,23},{8,24},{9,... | collective-permute-start | bytes 823304 | tf_op jit(solution)/shard_map/ppermute | solution.py:345
  66.4 3.2 %copy-start.11 = (f32[512]{0:T(512)S(1)}, f32[512]{0:T(512)}, u32[]{:S(2)}) copy-start(f32[512]{0:T(512)} %param.11) | copy-start | bytes 6148
  66.4 3.3 %copy-start.1 = (bf16[128,1024]{1,0:T(8,128)(2,1)S(1)}, bf16[128,1024]{1,0:T(8,128)(2,1)}, u32[]{:S(2)}) copy-start(bf16[128,1024]{1,0:T(8,128)(2,1)} %map_ref.7) | copy-start | bytes 786436
  66.4 9.4 %copy-start.4 = (bf16[8,256,1024]{2,1,0:T(8,128)(2,1)S(1)}, bf16[8,256,1024]{2,1,0:T(8,128)(2,1)}, u32[]{:S(2)}) copy-start(bf16[8,256,1024]{2,1,0:T(8,128)(2,1)} %copy-done.3) | copy-start | bytes 12582916
  69.5 6.3 %copy-start.9 = (f32[8,256,128]{2,1,0:T(8,128)S(1)}, f32[8,256,128]{2,1,0:T(8,128)}, u32[]{:S(2)}) copy-start(f32[8,256,128]{2,1,0:T(8,128)} %copy-done.8) | copy-start | bytes 3145732
  69.5 14.6 %collective-permute-start = (bf16[1072,128]{1,0:T(8,128)(2,1)S(1)}, bf16[1072,128]{1,0:T(8,128)(2,1)S(1)}, u32[]{:S(2)}, u32[]{:S(2)}) collective-permute-start(bf16[1072,128]{1,0:T(8,128)(2,1)S(1)} %shard_map.67), channel_id=1, source_target_pairs={{0,16},{16,0},{1,17},{17,1},{2,18},{18,2},{3,19},{19,3},{4,20},{20... | collective-permute-start | bytes 823304 | tf_op jit(solution)/shard_map/ppermute | solution.py:345

commit v9 on v4

--- a/solution.py
+++ b/solution.py
@@ -368,16 +368,8 @@
         )
         attended.append(out)
     landed = exchange(attended[-1]).reshape(parts, members, heads, rows, DH)
-    held = max(1, members // 4)
-    return stepped(
-        unpack_kernel,
-        members // held,
-        [landed],
-        [pl.BlockSpec((parts, held, heads, rows, DH), lambda i: (0, i, 0, 0, 0))],
-        pl.BlockSpec((rows, held * parts * width), lambda i: (0, i)),
-        shaped((rows, model)),
-        [],
-    )
+    (result,) = whole_call(unpack_kernel, [landed], [shaped((rows, model))])
+    return result
 
 
 def solution(mesh):

time: 103 us -> 102 us (level)
    pallas_call x3 -> x2, Pallas kernels: 8.51 us -> 6.81 us  [stepped(): pl.pallas_call(kernel, grid=(steps,), in_specs=specs, out_specs=out_specs...]
    pallas_call x6 -> x7, Pallas kernels: 20.3 us -> 21.6 us  [whole_call(): pl.pallas_call(kernel, in_specs=[read] * len(inputs), out_specs=[written]...]
where the time goes in v9:
time: 102 us
  Pallas kernels  28.4 us (28%)
  waiting for transfers between devices  24.5 us (24%)
  blocking collectives  20.3 us (20%)
  starting transfers between devices  19.4 us (19%)
  local copies, waits for them, and re-layouts  9.01 us (9%)
    pallas_call x7, Pallas kernels, whole_call(): pl.pallas_call(kernel, in_specs=[read] * len(inputs), out_specs=[written]...  21.6 us
    all_to_all x2, waiting for transfers between devices, exchange(): return lax.all_to_all(block, GROUP, split_axis=0, concat_axis=0, tiled=True)  21.2 us
    all_to_all x1, blocking collectives, exchange(): return lax.all_to_all(block, GROUP, split_axis=0, concat_axis=0, tiled=True)  20.3 us
    all_to_all x2, starting transfers between devices, exchange(): return lax.all_to_all(block, GROUP, split_axis=0, concat_axis=0, tiled=True)  10.2 us
    ppermute x2, starting transfers between devices, local(): came = lax.ppermute(sent, 'span', [(0, 1), (1, 0)] if both else [(0, 1)])  9.23 us
    unnamed x25, local copies, waits for them, and re-layouts  8.91 us
    pallas_call x2, Pallas kernels, stepped(): pl.pallas_call(kernel, grid=(steps,), in_specs=specs, out_specs=out_specs...  6.81 us
    ppermute x2, waiting for transfers between devices, local(): came = lax.ppermute(sent, 'span', [(0, 1), (1, 0)] if both else [(0, 1)])  3.33 us
  transfers between devices with their start and end apart: 4, of which 3 were waited for; matrix products, arithmetic and copies ran while one was open for 1% of the time, Pallas kernels for 22%

profile of v9, /device:TPU:0, one launch (start us, length us, event | category | flops | bytes accessed | tf_op | source)
XLA Modules:
  0.0 101.8 jit_solution(7367863469192120381)
XLA Ops:
  0.0 2.8 %shard_map.65 = bf16[16,3,128,128]{3,2,1,0:T(8,128)(2,1)} custom-call(bf16[128,4096]{1,0:T(8,128)(2,1)} %refs_0_.3, bf16[128,4096]{1,0:T(8,128)(2,1)} %refs_1_.3, bf16[128,4096]{1,0:T(8,128)(2,1)} %refs_2_.3), custom_call_target="tpu_custom_call" | custom-call | flops 1000 | bytes 1000 | tf_op jit(solution)/shard_map/pallas_call | solution.py:225
  2.8 6.3 %all-to-all-start.1 = ((bf16[16,3,128,128]{3,2,1,0:T(8,128)(2,1)}), bf16[16,3,128,128]{3,2,1,0:T(8,128)(2,1)S(1)}, u32[]{:S(2)}, u32[]{:S(2)}) async-start(bf16[16,3,128,128]{3,2,1,0:T(8,128)(2,1)} %shard_map.65), calls=%async_computation.1 | async-start | bytes 3145728 | tf_op jit(solution)/shard_map/all_to_all | solution.py:263
  9.2 0.0 copy-start.5
  9.2 1.2 %copy-done.5 = bf16[128,4096]{1,0:T(8,128)(2,1)S(1)} copy-done((bf16[128,4096]{1,0:T(8,128)(2,1)S(1)}, bf16[128,4096]{1,0:T(8,128)(2,1)}, u32[]{:S(2)}) %copy-start.5) | copy-done | bytes 1048600
  10.4 1.2 %copy-done.6 = bf16[128,4096]{1,0:T(8,128)(2,1)S(1)} copy-done((bf16[128,4096]{1,0:T(8,128)(2,1)S(1)}, bf16[128,4096]{1,0:T(8,128)(2,1)}, u32[]{:S(2)}) %copy-start.6) | copy-done | bytes 1048600
  11.6 1.2 %copy-done.7 = bf16[128,4096]{1,0:T(8,128)(2,1)S(1)} copy-done((bf16[128,4096]{1,0:T(8,128)(2,1)S(1)}, bf16[128,4096]{1,0:T(8,128)(2,1)}, u32[]{:S(2)}) %copy-start.7) | copy-done | bytes 1048600
  12.8 0.3 shard_map.64
  13.1 0.0 copy-start.2
  13.1 1.2 %copy-done.2 = bf16[16,3,128,128]{3,2,1,0:T(8,128)(2,1)} copy-done((bf16[16,3,128,128]{3,2,1,0:T(8,128)(2,1)}, bf16[16,3,128,128]{3,2,1,0:T(8,128)(2,1)S(1)}, u32[]{:S(2)}) %copy-start.2) | copy-done | bytes 1572888
  14.3 17.6 %all-to-all-done.1.x_ref.k_ref.v_ref.rim_ref = bf16[16,3,128,128]{3,2,1,0:T(8,128)(2,1)S(1)} async-done(((bf16[16,3,128,128]{3,2,1,0:T(8,128)(2,1)}), bf16[16,3,128,128]{3,2,1,0:T(8,128)(2,1)S(1)}, u32[]{:S(2)}, u32[]{:S(2)}) %all-to-all-start.1) | async-done | bytes 1572896 | tf_op jit(solution)/shard_map/all_to_all | solution.py:263
  31.9 3.9 %all-to-all-start = ((bf16[16,3,128,128]{3,2,1,0:T(8,128)(2,1)}), bf16[16,3,128,128]{3,2,1,0:T(8,128)(2,1)S(1)}, u32[]{:S(2)}, u32[]{:S(2)}) async-start(bf16[16,3,128,128]{3,2,1,0:T(8,128)(2,1)} %copy-done.2), calls=%async_computation | async-start | bytes 3145728 | tf_op jit(solution)/shard_map/all_to_all | solution.py:263
  35.8 1.1 %copy.7 = bf16[128,1024]{0,1:T(8,128)(2,1)S(1)} copy(bf16[128,1024]{1,0:T(8,128)(2,1)} %map_ref.7) | data formatting | bytes 524288 | tf_op args[4]
  37.0 0.0 copy-start
  37.0 3.8 %shard_map.69 = bf16[1072,128]{1,0:T(8,128)(2,1)} custom-call(bf16[16,3,128,128]{3,2,1,0:T(8,128)(2,1)S(1)} %all-to-all-done.1.x_ref.k_ref.v_ref.rim_ref, bf16[16,3,128,128]{3,2,1,0:T(8,128)(2,1)S(1)} %all-to-all-done.1.x_ref.k_ref.v_ref.rim_ref, bf16[16,3,128,128]{3,2,1,0:T(8,128)(2,1)S(1)} %all-to-all-done.1.x_ref.k_ref.v_ref.rim_ref, ...), custom_call_target="tpu_custom_call" | custom-call | flops 1000 | bytes 1000 | tf_op jit(solution)/shard_map/pallas_call | solution.py:237
  40.8 5.2 %collective-permute-start.1 = (bf16[1072,128]{1,0:T(8,128)(2,1)}, bf16[1072,128]{1,0:T(8,128)(2,1)}, u32[]{:S(2)}, u32[]{:S(2)}) collective-permute-start(bf16[1072,128]{1,0:T(8,128)(2,1)} %shard_map.69), channel_id=1, source_target_pairs={{0,16},{1,17},{2,18},{3,19},{4,20},{5,21},{6,22},{7,23},{8,24},{9,... | collective-permute-start | bytes 823304 | tf_op jit(solution)/shard_map/ppermute | solution.py:334
  46.0 6.1 %shard_map.66 = (f32[8,256,128]{2,1,0:T(8,128)S(1)}, bf16[8,256,1024]{2,1,0:T(8,128)(2,1)S(1)}) custom-call(bf16[16,3,128,128]{3,2,1,0:T(8,128)(2,1)S(1)} %all-to-all-done.1.x_ref.k_ref.v_ref.rim_ref, f32[3,4,128]{2,1,0:T(4,128)S(1)} %get-tuple-element.18.w_ref, bf16[128,1024]{1,0:T(8,128)(2,1)S(1)} %copy-done, bf16[1024,128]{1,0:T(8,128)(2,1)S(1)} %bitcast.4), custom_call_target="tpu_custom_call" | custom-call | flops 1000 | bytes 1000 | tf_op jit(solution)/shard_map/pallas_call | solution.py:225
  52.1 0.0 copy-start.3
  52.1 1.9 %copy-done.3 = bf16[8,256,1024]{2,1,0:T(8,128)(2,1)} copy-done((bf16[8,256,1024]{2,1,0:T(8,128)(2,1)}, bf16[8,256,1024]{2,1,0:T(8,128)(2,1)S(1)}, u32[]{:S(2)}) %copy-start.3) | copy-done | bytes 4194328
  54.1 1.0 copy-done.8
  55.0 3.6 %all-to-all-done.k_ref.v_ref.rim_ref.x_ref = bf16[16,3,128,128]{3,2,1,0:T(8,128)(2,1)S(1)} async-done(((bf16[16,3,128,128]{3,2,1,0:T(8,128)(2,1)}), bf16[16,3,128,128]{3,2,1,0:T(8,128)(2,1)S(1)}, u32[]{:S(2)}, u32[]{:S(2)}) %all-to-all-start) | async-done | bytes 1572896 | tf_op jit(solution)/shard_map/all_to_all | solution.py:263
  58.6 3.1 %shard_map.67 = bf16[1072,128]{1,0:T(8,128)(2,1)S(1)} custom-call(bf16[16,3,128,128]{3,2,1,0:T(8,128)(2,1)S(1)} %all-to-all-done.k_ref.v_ref.rim_ref.x_ref, bf16[16,3,128,128]{3,2,1,0:T(8,128)(2,1)S(1)} %all-to-all-done.k_ref.v_ref.rim_ref.x_ref, bf16[16,3,128,128]{3,2,1,0:T(8,128)(2,1)S(1)} %all-to-all-done.k_ref.v_ref.rim_ref.x_ref, ...), custom_call_target="tpu_custom_call" | custom-call | flops 1000 | bytes 1000 | tf_op jit(solution)/shard_map/pallas_call | solution.py:237
  61.7 0.0 copy-start.9
  61.7 4.1 %collective-permute-start = (bf16[1072,128]{1,0:T(8,128)(2,1)S(1)}, bf16[1072,128]{1,0:T(8,128)(2,1)S(1)}, u32[]{:S(2)}, u32[]{:S(2)}) collective-permute-start(bf16[1072,128]{1,0:T(8,128)(2,1)S(1)} %shard_map.67), channel_id=1, source_target_pairs={{0,16},{16,0},{1,17},{17,1},{2,18},{18,2},{3,19},{19,3},{4,20},{20... | collective-permute-start | bytes 823304 | tf_op jit(solution)/shard_map/ppermute | solution.py:334
  65.7 0.1 dynamic_slice.7
  65.8 0.0 copy-done.1
  65.8 6.1 %shard_map.68 = (f32[8,256,128]{2,1,0:T(8,128)S(1)}, bf16[8,256,1024]{2,1,0:T(8,128)(2,1)S(1)}) custom-call(bf16[16,3,128,128]{3,2,1,0:T(8,128)(2,1)S(1)} %all-to-all-done.k_ref.v_ref.rim_ref.x_ref, f32[3,4,128]{2,1,0:T(4,128)S(1)} %get-tuple-element.17.w_ref, bf16[128,1024]{1,0:T(8,128)(2,1)S(1)} %copy-done.1, bf16[1024,128]{1,0:T(8,128)(2,1)S(1)} %bitcast.6), custom_call_target="tpu_custom_call" | custom-call | flops 1000 | bytes 1000 | tf_op jit(solution)/shard_map/pallas_call | solution.py:225
  72.0 0.0 collective-permute-done.1.came_ref
  72.0 3.0 %shard_map.70.refs_0_ = bf16[16,1,128,128]{3,2,1,0:T(8,128)(2,1)S(1)} custom-call(bf16[16,3,128,128]{3,2,1,0:T(8,128)(2,1)S(1)} %all-to-all-done.1.x_ref.k_ref.v_ref.rim_ref, bf16[1072,128]{1,0:T(8,128)(2,1)} %collective-permute-done.1.came_ref, f32[3,4,128]{2,1,0:T(4,128)S(1)} %get-tuple-element.18.w_ref, bf16[128,1024]{1,0:T(8,128)(2,1)S(1)} %copy-done.1, ...), custom_call_target="tpu_custom_call" | custom-call | flops 1000 | bytes 1000 | tf_op jit(solution)/shard_map/pallas_call | solution.py:225
  75.0 3.3 %collective-permute-done.came_ref = bf16[1072,128]{1,0:T(8,128)(2,1)S(1)} collective-permute-done((bf16[1072,128]{1,0:T(8,128)(2,1)S(1)}, bf16[1072,128]{1,0:T(8,128)(2,1)S(1)}, u32[]{:S(2)}, u32[]{:S(2)}) %collective-permute-start) | collective-permute-done | bytes 274464 | tf_op jit(solution)/shard_map/ppermute | solution.py:334
  78.3 2.0 %shard_map.71 = bf16[16,2,128,128]{3,2,1,0:T(8,128)(2,1)S(1)} custom-call(bf16[16,3,128,128]{3,2,1,0:T(8,128)(2,1)S(1)} %all-to-all-done.k_ref.v_ref.rim_ref.x_ref, bf16[1072,128]{1,0:T(8,128)(2,1)S(1)} %collective-permute-done.came_ref, f32[3,4,128]{2,1,0:T(4,128)S(1)} %get-tuple-element.17.w_ref, bf16[128,1024]{1,0:T(8,128)(2,1)S(1)} %copy-done.1, ...), custom_call_target="tpu_custom_call" | custom-call | flops 1000 | bytes 1000 | tf_op jit(solution)/shard_map/pallas_call | solution.py:225
  80.3 20.3 %all_to_all.15 = bf16[16,2,128,128]{3,2,1,0:T(8,128)(2,1)S(1)} all-to-all(bf16[16,2,128,128]{3,2,1,0:T(8,128)(2,1)S(1)} %shard_map.71), channel_id=1, replica_groups=mesh['span'=2,'part'=2,'sp'=8] {'part','sp'}, dimensions={0} | all-to-all | bytes 2097152 | tf_op jit(solution)/shard_map/all_to_all | solution.py:263
  100.6 1.2 %shard_map.72 = bf16[128,4096]{1,0:T(8,128)(2,1)} custom-call(bf16[2,8,2,128,128]{4,3,2,1,0:T(8,128)(2,1)S(1)} %bitcast.9), custom_call_target="tpu_custom_call" | custom-call | flops 1000 | bytes 1000 | tf_op jit(solution)/shard_map/pallas_call | solution.py:225
  (15 shorter events, 0.0 us)
Async XLA Ops:
  2.8 29.1 %all-to-all-start.1 = ((bf16[16,3,128,128]{3,2,1,0:T(8,128)(2,1)}), bf16[16,3,128,128]{3,2,1,0:T(8,128)(2,1)S(1)}, u32[]{:S(2)}, u32[]{:S(2)}) async-start(bf16[16,3,128,128]{3,2,1,0:T(8,128)(2,1)} %shard_map.65), calls=%async_computation.1 | async-start | bytes 3145728 | tf_op jit(solution)/shard_map/all_to_all | solution.py:263
  9.2 1.2 %copy-start.5 = (bf16[128,4096]{1,0:T(8,128)(2,1)S(1)}, bf16[128,4096]{1,0:T(8,128)(2,1)}, u32[]{:S(2)}) copy-start(bf16[128,4096]{1,0:T(8,128)(2,1)} %refs_0_.3) | copy-start | bytes 3145732
  10.4 1.2 %copy-start.6 = (bf16[128,4096]{1,0:T(8,128)(2,1)S(1)}, bf16[128,4096]{1,0:T(8,128)(2,1)}, u32[]{:S(2)}) copy-start(bf16[128,4096]{1,0:T(8,128)(2,1)} %refs_1_.3) | copy-start | bytes 3145732
  11.6 1.2 %copy-start.7 = (bf16[128,4096]{1,0:T(8,128)(2,1)S(1)}, bf16[128,4096]{1,0:T(8,128)(2,1)}, u32[]{:S(2)}) copy-start(bf16[128,4096]{1,0:T(8,128)(2,1)} %refs_2_.3) | copy-start | bytes 3145732
  13.1 1.2 %copy-start.2 = (bf16[16,3,128,128]{3,2,1,0:T(8,128)(2,1)}, bf16[16,3,128,128]{3,2,1,0:T(8,128)(2,1)S(1)}, u32[]{:S(2)}) copy-start(bf16[16,3,128,128]{3,2,1,0:T(8,128)(2,1)S(1)} %shard_map.64) | copy-start | bytes 4718596
  14.3 22.7 %copy-start.10 = (f32[3,4,512]{2,1,0:T(4,128)S(1)}, f32[3,4,512]{2,1,0:T(4,128)}, u32[]{:S(2)}) copy-start(f32[3,4,512]{2,1,0:T(4,128)} %param.9) | copy-start | bytes 73732
  31.9 26.7 %all-to-all-start = ((bf16[16,3,128,128]{3,2,1,0:T(8,128)(2,1)}), bf16[16,3,128,128]{3,2,1,0:T(8,128)(2,1)S(1)}, u32[]{:S(2)}, u32[]{:S(2)}) async-start(bf16[16,3,128,128]{3,2,1,0:T(8,128)(2,1)} %copy-done.2), calls=%async_computation | async-start | bytes 3145728 | tf_op jit(solution)/shard_map/all_to_all | solution.py:263
  37.0 9.0 %copy-start = (bf16[128,1024]{1,0:T(8,128)(2,1)S(1)}, bf16[128,1024]{1,0:T(8,128)(2,1)}, u32[]{:S(2)}) copy-start(bf16[128,1024]{1,0:T(8,128)(2,1)} %map_ref.7) | copy-start | bytes 786436
  40.8 31.2 %collective-permute-start.1 = (bf16[1072,128]{1,0:T(8,128)(2,1)}, bf16[1072,128]{1,0:T(8,128)(2,1)}, u32[]{:S(2)}, u32[]{:S(2)}) collective-permute-start(bf16[1072,128]{1,0:T(8,128)(2,1)} %shard_map.69), channel_id=1, source_target_pairs={{0,16},{1,17},{2,18},{3,19},{4,20},{5,21},{6,22},{7,23},{8,24},{9,... | collective-permute-start | bytes 823304 | tf_op jit(solution)/shard_map/ppermute | solution.py:334
  52.1 1.9 %copy-start.3 = (bf16[8,256,1024]{2,1,0:T(8,128)(2,1)}, bf16[8,256,1024]{2,1,0:T(8,128)(2,1)S(1)}, u32[]{:S(2)}) copy-start(bf16[8,256,1024]{2,1,0:T(8,128)(2,1)S(1)} %get-tuple-element.11.feat_ref) | copy-start | bytes 12582916
  54.1 1.0 copy-start.8
  58.6 7.1 %copy-start.11 = (f32[512]{0:T(512)S(1)}, f32[512]{0:T(512)}, u32[]{:S(2)}) copy-start(f32[512]{0:T(512)} %param.11) | copy-start | bytes 6148
  58.6 7.2 %copy-start.1 = (bf16[128,1024]{1,0:T(8,128)(2,1)S(1)}, bf16[128,1024]{1,0:T(8,128)(2,1)}, u32[]{:S(2)}) copy-start(bf16[128,1024]{1,0:T(8,128)(2,1)} %map_ref.7) | copy-start | bytes 786436
  58.6 13.4 %copy-start.4 = (bf16[8,256,1024]{2,1,0:T(8,128)(2,1)S(1)}, bf16[8,256,1024]{2,1,0:T(8,128)(2,1)}, u32[]{:S(2)}) copy-start(bf16[8,256,1024]{2,1,0:T(8,128)(2,1)} %copy-done.3) | copy-start | bytes 12582916
  61.7 10.3 %copy-start.9 = (f32[8,256,128]{2,1,0:T(8,128)S(1)}, f32[8,256,128]{2,1,0:T(8,128)}, u32[]{:S(2)}) copy-start(f32[8,256,128]{2,1,0:T(8,128)} %copy-done.8) | copy-start | bytes 3145732
  61.7 16.6 %collective-permute-start = (bf16[1072,128]{1,0:T(8,128)(2,1)S(1)}, bf16[1072,128]{1,0:T(8,128)(2,1)S(1)}, u32[]{:S(2)}, u32[]{:S(2)}) collective-permute-start(bf16[1072,128]{1,0:T(8,128)(2,1)S(1)} %shard_map.67), channel_id=1, source_target_pairs={{0,16},{16,0},{1,17},{17,1},{2,18},{18,2},{3,19},{19,3},{4,20},{20... | collective-permute-start | bytes 823304 | tf_op jit(solution)/shard_map/ppermute | solution.py:334

commit v10 on v9

--- a/solution.py
+++ b/solution.py
@@ -39,28 +39,28 @@
 def pack_kernel(starts, *refs):
     *sources, out_ref, held, packed, load_sems, store_sems = refs
     pieces = load_sems.shape[1]
-    width = held.shape[-1] // pieces
+    extent = held.shape[1] // pieces
     loads = {}
     for piece in range(pieces):
+        rows = pl.ds(piece * extent, extent)
         for member, source in enumerate(sources):
-            cols = pl.ds(piece * width, width)
             loads[piece, member] = pltpu.make_async_copy(
-                source.at[:, cols], held.at[member, :, cols], load_sems.at[member, piece]
+                source.at[rows], held.at[member, rows], load_sems.at[member, piece]
             )
             loads[piece, member].start()
     stores = []
     for piece in range(pieces):
-        owners = [owner for owner, start in enumerate(starts) if start // width == piece]
+        rows = pl.ds(piece * extent, extent)
         for member in range(len(sources)):
             loads[piece, member].wait()
-            for owner in owners:
-                start = starts[owner]
-                packed[owner, member] = held[member, :, start : start + DH]
-        for owner in owners:
-            stores.append(
-                pltpu.make_async_copy(packed.at[owner], out_ref.at[owner], store_sems.at[owner])
+            for owner, start in enumerate(starts):
+                packed[owner, member, rows] = held[member, rows, start : start + DH]
+        stores.append(
+            pltpu.make_async_copy(
+                packed.at[:, :, rows], out_ref.at[:, :, rows], store_sems.at[piece]
             )
-            stores[-1].start()
+        )
+        stores[-1].start()
     for store in stores:
         store.wait()
 
@@ -301,7 +301,7 @@
                     pltpu.VMEM((3, rows, model), jnp.bfloat16),
                     pltpu.VMEM(packed.shape, packed.dtype),
                     pltpu.SemaphoreType.DMA((3, 4)),
-                    pltpu.SemaphoreType.DMA((count,)),
+                    pltpu.SemaphoreType.DMA((4,)),
                 ],
                 read=HBM, written=HBM, limit=MOST,
             )

time: 102 us -> 102 us (level)
  no operation moved by 1% of the time
where the time goes in v10:
time: 102 us
  Pallas kernels  28.3 us (28%)
  waiting for transfers between devices  24.5 us (24%)
  blocking collectives  20.3 us (20%)
  starting transfers between devices  19.4 us (19%)
  local copies, waits for them, and re-layouts  9.01 us (9%)
    pallas_call x7, Pallas kernels, whole_call(): pl.pallas_call(kernel, in_specs=[read] * len(inputs), out_specs=[written]...  21.5 us
    all_to_all x2, waiting for transfers between devices, exchange(): return lax.all_to_all(block, GROUP, split_axis=0, concat_axis=0, tiled=True)  21.2 us
    all_to_all x1, blocking collectives, exchange(): return lax.all_to_all(block, GROUP, split_axis=0, concat_axis=0, tiled=True)  20.3 us
    all_to_all x2, starting transfers between devices, exchange(): return lax.all_to_all(block, GROUP, split_axis=0, concat_axis=0, tiled=True)  10.2 us
    ppermute x2, starting transfers between devices, local(): came = lax.ppermute(sent, 'span', [(0, 1), (1, 0)] if both else [(0, 1)])  9.23 us
    unnamed x25, local copies, waits for them, and re-layouts  8.91 us
    pallas_call x2, Pallas kernels, stepped(): pl.pallas_call(kernel, grid=(steps,), in_specs=specs, out_specs=out_specs...  6.82 us
    ppermute x2, waiting for transfers between devices, local(): came = lax.ppermute(sent, 'span', [(0, 1), (1, 0)] if both else [(0, 1)])  3.33 us
  transfers between devices with their start and end apart: 4, of which 3 were waited for; matrix products, arithmetic and copies ran while one was open for 1% of the time, Pallas kernels for 22%

profile of v10, /device:TPU:0, one launch (start us, length us, event | category | flops | bytes accessed | tf_op | source)
XLA Modules:
  0.0 101.8 jit_solution(3421932772852746584)
XLA Ops:
  0.0 2.8 %shard_map.65 = bf16[16,3,128,128]{3,2,1,0:T(8,128)(2,1)} custom-call(bf16[128,4096]{1,0:T(8,128)(2,1)} %refs_0_.3, bf16[128,4096]{1,0:T(8,128)(2,1)} %refs_1_.3, bf16[128,4096]{1,0:T(8,128)(2,1)} %refs_2_.3), custom_call_target="tpu_custom_call" | custom-call | flops 1000 | bytes 1000 | tf_op jit(solution)/shard_map/pallas_call | solution.py:225
  2.8 6.3 %all-to-all-start.1 = ((bf16[16,3,128,128]{3,2,1,0:T(8,128)(2,1)}), bf16[16,3,128,128]{3,2,1,0:T(8,128)(2,1)S(1)}, u32[]{:S(2)}, u32[]{:S(2)}) async-start(bf16[16,3,128,128]{3,2,1,0:T(8,128)(2,1)} %shard_map.65), calls=%async_computation.1 | async-start | bytes 3145728 | tf_op jit(solution)/shard_map/all_to_all | solution.py:263
  9.1 0.0 copy-start.5
  9.1 1.2 %copy-done.5 = bf16[128,4096]{1,0:T(8,128)(2,1)S(1)} copy-done((bf16[128,4096]{1,0:T(8,128)(2,1)S(1)}, bf16[128,4096]{1,0:T(8,128)(2,1)}, u32[]{:S(2)}) %copy-start.5) | copy-done | bytes 1048600
  10.3 1.2 %copy-done.6 = bf16[128,4096]{1,0:T(8,128)(2,1)S(1)} copy-done((bf16[128,4096]{1,0:T(8,128)(2,1)S(1)}, bf16[128,4096]{1,0:T(8,128)(2,1)}, u32[]{:S(2)}) %copy-start.6) | copy-done | bytes 1048600
  11.5 1.2 %copy-done.7 = bf16[128,4096]{1,0:T(8,128)(2,1)S(1)} copy-done((bf16[128,4096]{1,0:T(8,128)(2,1)S(1)}, bf16[128,4096]{1,0:T(8,128)(2,1)}, u32[]{:S(2)}) %copy-start.7) | copy-done | bytes 1048600
  12.8 0.3 shard_map.64
  13.0 1.2 %copy-done.2 = bf16[16,3,128,128]{3,2,1,0:T(8,128)(2,1)} copy-done((bf16[16,3,128,128]{3,2,1,0:T(8,128)(2,1)}, bf16[16,3,128,128]{3,2,1,0:T(8,128)(2,1)S(1)}, u32[]{:S(2)}) %copy-start.2) | copy-done | bytes 1572888
  14.2 17.6 %all-to-all-done.1.x_ref.k_ref.v_ref.rim_ref = bf16[16,3,128,128]{3,2,1,0:T(8,128)(2,1)S(1)} async-done(((bf16[16,3,128,128]{3,2,1,0:T(8,128)(2,1)}), bf16[16,3,128,128]{3,2,1,0:T(8,128)(2,1)S(1)}, u32[]{:S(2)}, u32[]{:S(2)}) %all-to-all-start.1) | async-done | bytes 1572896 | tf_op jit(solution)/shard_map/all_to_all | solution.py:263
  31.8 3.9 %all-to-all-start = ((bf16[16,3,128,128]{3,2,1,0:T(8,128)(2,1)}), bf16[16,3,128,128]{3,2,1,0:T(8,128)(2,1)S(1)}, u32[]{:S(2)}, u32[]{:S(2)}) async-start(bf16[16,3,128,128]{3,2,1,0:T(8,128)(2,1)} %copy-done.2), calls=%async_computation | async-start | bytes 3145728 | tf_op jit(solution)/shard_map/all_to_all | solution.py:263
  35.8 1.1 %copy.7 = bf16[128,1024]{0,1:T(8,128)(2,1)S(1)} copy(bf16[128,1024]{1,0:T(8,128)(2,1)} %map_ref.7) | data formatting | bytes 524288 | tf_op args[4]
  36.9 0.0 copy-start
  36.9 3.8 %shard_map.69 = bf16[1072,128]{1,0:T(8,128)(2,1)} custom-call(bf16[16,3,128,128]{3,2,1,0:T(8,128)(2,1)S(1)} %all-to-all-done.1.x_ref.k_ref.v_ref.rim_ref, bf16[16,3,128,128]{3,2,1,0:T(8,128)(2,1)S(1)} %all-to-all-done.1.x_ref.k_ref.v_ref.rim_ref, bf16[16,3,128,128]{3,2,1,0:T(8,128)(2,1)S(1)} %all-to-all-done.1.x_ref.k_ref.v_ref.rim_ref, ...), custom_call_target="tpu_custom_call" | custom-call | flops 1000 | bytes 1000 | tf_op jit(solution)/shard_map/pallas_call | solution.py:237
  40.7 5.2 %collective-permute-start.1 = (bf16[1072,128]{1,0:T(8,128)(2,1)}, bf16[1072,128]{1,0:T(8,128)(2,1)}, u32[]{:S(2)}, u32[]{:S(2)}) collective-permute-start(bf16[1072,128]{1,0:T(8,128)(2,1)} %shard_map.69), channel_id=1, source_target_pairs={{0,16},{1,17},{2,18},{3,19},{4,20},{5,21},{6,22},{7,23},{8,24},{9,... | collective-permute-start | bytes 823304 | tf_op jit(solution)/shard_map/ppermute | solution.py:334
  45.9 6.1 %shard_map.66 = (f32[8,256,128]{2,1,0:T(8,128)S(1)}, bf16[8,256,1024]{2,1,0:T(8,128)(2,1)S(1)}) custom-call(bf16[16,3,128,128]{3,2,1,0:T(8,128)(2,1)S(1)} %all-to-all-done.1.x_ref.k_ref.v_ref.rim_ref, f32[3,4,128]{2,1,0:T(4,128)S(1)} %get-tuple-element.18.w_ref, bf16[128,1024]{1,0:T(8,128)(2,1)S(1)} %copy-done, bf16[1024,128]{1,0:T(8,128)(2,1)S(1)} %bitcast.4), custom_call_target="tpu_custom_call" | custom-call | flops 1000 | bytes 1000 | tf_op jit(solution)/shard_map/pallas_call | solution.py:225
  52.0 1.9 %copy-done.3 = bf16[8,256,1024]{2,1,0:T(8,128)(2,1)} copy-done((bf16[8,256,1024]{2,1,0:T(8,128)(2,1)}, bf16[8,256,1024]{2,1,0:T(8,128)(2,1)S(1)}, u32[]{:S(2)}) %copy-start.3) | copy-done | bytes 4194328
  54.0 1.0 copy-done.8
  55.0 3.6 %all-to-all-done.k_ref.v_ref.rim_ref.x_ref = bf16[16,3,128,128]{3,2,1,0:T(8,128)(2,1)S(1)} async-done(((bf16[16,3,128,128]{3,2,1,0:T(8,128)(2,1)}), bf16[16,3,128,128]{3,2,1,0:T(8,128)(2,1)S(1)}, u32[]{:S(2)}, u32[]{:S(2)}) %all-to-all-start) | async-done | bytes 1572896 | tf_op jit(solution)/shard_map/all_to_all | solution.py:263
  58.5 3.1 %shard_map.67 = bf16[1072,128]{1,0:T(8,128)(2,1)S(1)} custom-call(bf16[16,3,128,128]{3,2,1,0:T(8,128)(2,1)S(1)} %all-to-all-done.k_ref.v_ref.rim_ref.x_ref, bf16[16,3,128,128]{3,2,1,0:T(8,128)(2,1)S(1)} %all-to-all-done.k_ref.v_ref.rim_ref.x_ref, bf16[16,3,128,128]{3,2,1,0:T(8,128)(2,1)S(1)} %all-to-all-done.k_ref.v_ref.rim_ref.x_ref, ...), custom_call_target="tpu_custom_call" | custom-call | flops 1000 | bytes 1000 | tf_op jit(solution)/shard_map/pallas_call | solution.py:237
  61.6 0.0 copy-start.9
  61.6 4.0 %collective-permute-start = (bf16[1072,128]{1,0:T(8,128)(2,1)S(1)}, bf16[1072,128]{1,0:T(8,128)(2,1)S(1)}, u32[]{:S(2)}, u32[]{:S(2)}) collective-permute-start(bf16[1072,128]{1,0:T(8,128)(2,1)S(1)} %shard_map.67), channel_id=1, source_target_pairs={{0,16},{16,0},{1,17},{17,1},{2,18},{18,2},{3,19},{19,3},{4,20},{20... | collective-permute-start | bytes 823304 | tf_op jit(solution)/shard_map/ppermute | solution.py:334
  65.7 0.0 copy-done.11
  65.7 0.1 dynamic_slice.7
  65.7 6.1 %shard_map.68 = (f32[8,256,128]{2,1,0:T(8,128)S(1)}, bf16[8,256,1024]{2,1,0:T(8,128)(2,1)S(1)}) custom-call(bf16[16,3,128,128]{3,2,1,0:T(8,128)(2,1)S(1)} %all-to-all-done.k_ref.v_ref.rim_ref.x_ref, f32[3,4,128]{2,1,0:T(4,128)S(1)} %get-tuple-element.17.w_ref, bf16[128,1024]{1,0:T(8,128)(2,1)S(1)} %copy-done.1, bf16[1024,128]{1,0:T(8,128)(2,1)S(1)} %bitcast.6), custom_call_target="tpu_custom_call" | custom-call | flops 1000 | bytes 1000 | tf_op jit(solution)/shard_map/pallas_call | solution.py:225
  71.9 0.0 collective-permute-done.1.came_ref
  71.9 0.0 copy-done.4
  71.9 0.0 copy-done.9
  71.9 3.0 %shard_map.70.refs_0_ = bf16[16,1,128,128]{3,2,1,0:T(8,128)(2,1)S(1)} custom-call(bf16[16,3,128,128]{3,2,1,0:T(8,128)(2,1)S(1)} %all-to-all-done.1.x_ref.k_ref.v_ref.rim_ref, bf16[1072,128]{1,0:T(8,128)(2,1)} %collective-permute-done.1.came_ref, f32[3,4,128]{2,1,0:T(4,128)S(1)} %get-tuple-element.18.w_ref, bf16[128,1024]{1,0:T(8,128)(2,1)S(1)} %copy-done.1, ...), custom_call_target="tpu_custom_call" | custom-call | flops 1000 | bytes 1000 | tf_op jit(solution)/shard_map/pallas_call | solution.py:225
  74.9 3.3 %collective-permute-done.came_ref = bf16[1072,128]{1,0:T(8,128)(2,1)S(1)} collective-permute-done((bf16[1072,128]{1,0:T(8,128)(2,1)S(1)}, bf16[1072,128]{1,0:T(8,128)(2,1)S(1)}, u32[]{:S(2)}, u32[]{:S(2)}) %collective-permute-start) | collective-permute-done | bytes 274464 | tf_op jit(solution)/shard_map/ppermute | solution.py:334
  78.2 2.0 %shard_map.71 = bf16[16,2,128,128]{3,2,1,0:T(8,128)(2,1)S(1)} custom-call(bf16[16,3,128,128]{3,2,1,0:T(8,128)(2,1)S(1)} %all-to-all-done.k_ref.v_ref.rim_ref.x_ref, bf16[1072,128]{1,0:T(8,128)(2,1)S(1)} %collective-permute-done.came_ref, f32[3,4,128]{2,1,0:T(4,128)S(1)} %get-tuple-element.17.w_ref, bf16[128,1024]{1,0:T(8,128)(2,1)S(1)} %copy-done.1, ...), custom_call_target="tpu_custom_call" | custom-call | flops 1000 | bytes 1000 | tf_op jit(solution)/shard_map/pallas_call | solution.py:225
  80.2 20.3 %all_to_all.15 = bf16[16,2,128,128]{3,2,1,0:T(8,128)(2,1)S(1)} all-to-all(bf16[16,2,128,128]{3,2,1,0:T(8,128)(2,1)S(1)} %shard_map.71), channel_id=1, replica_groups=mesh['span'=2,'part'=2,'sp'=8] {'part','sp'}, dimensions={0} | all-to-all | bytes 2097152 | tf_op jit(solution)/shard_map/all_to_all | solution.py:263
  100.5 1.2 %shard_map.72 = bf16[128,4096]{1,0:T(8,128)(2,1)} custom-call(bf16[2,8,2,128,128]{4,3,2,1,0:T(8,128)(2,1)S(1)} %bitcast.9), custom_call_target="tpu_custom_call" | custom-call | flops 1000 | bytes 1000 | tf_op jit(solution)/shard_map/pallas_call | solution.py:225
  (15 shorter events, 0.0 us)
Async XLA Ops:
  2.8 29.1 %all-to-all-start.1 = ((bf16[16,3,128,128]{3,2,1,0:T(8,128)(2,1)}), bf16[16,3,128,128]{3,2,1,0:T(8,128)(2,1)S(1)}, u32[]{:S(2)}, u32[]{:S(2)}) async-start(bf16[16,3,128,128]{3,2,1,0:T(8,128)(2,1)} %shard_map.65), calls=%async_computation.1 | async-start | bytes 3145728 | tf_op jit(solution)/shard_map/all_to_all | solution.py:263
  9.1 1.2 %copy-start.5 = (bf16[128,4096]{1,0:T(8,128)(2,1)S(1)}, bf16[128,4096]{1,0:T(8,128)(2,1)}, u32[]{:S(2)}) copy-start(bf16[128,4096]{1,0:T(8,128)(2,1)} %refs_0_.3) | copy-start | bytes 3145732
  10.3 1.2 %copy-start.6 = (bf16[128,4096]{1,0:T(8,128)(2,1)S(1)}, bf16[128,4096]{1,0:T(8,128)(2,1)}, u32[]{:S(2)}) copy-start(bf16[128,4096]{1,0:T(8,128)(2,1)} %refs_1_.3) | copy-start | bytes 3145732
  11.5 1.2 %copy-start.7 = (bf16[128,4096]{1,0:T(8,128)(2,1)S(1)}, bf16[128,4096]{1,0:T(8,128)(2,1)}, u32[]{:S(2)}) copy-start(bf16[128,4096]{1,0:T(8,128)(2,1)} %refs_2_.3) | copy-start | bytes 3145732
  13.0 1.2 %copy-start.2 = (bf16[16,3,128,128]{3,2,1,0:T(8,128)(2,1)}, bf16[16,3,128,128]{3,2,1,0:T(8,128)(2,1)S(1)}, u32[]{:S(2)}) copy-start(bf16[16,3,128,128]{3,2,1,0:T(8,128)(2,1)S(1)} %shard_map.64) | copy-start | bytes 4718596
  14.2 22.7 %copy-start.10 = (f32[3,4,512]{2,1,0:T(4,128)S(1)}, f32[3,4,512]{2,1,0:T(4,128)}, u32[]{:S(2)}) copy-start(f32[3,4,512]{2,1,0:T(4,128)} %param.9) | copy-start | bytes 73732
  31.8 26.7 %all-to-all-start = ((bf16[16,3,128,128]{3,2,1,0:T(8,128)(2,1)}), bf16[16,3,128,128]{3,2,1,0:T(8,128)(2,1)S(1)}, u32[]{:S(2)}, u32[]{:S(2)}) async-start(bf16[16,3,128,128]{3,2,1,0:T(8,128)(2,1)} %copy-done.2), calls=%async_computation | async-start | bytes 3145728 | tf_op jit(solution)/shard_map/all_to_all | solution.py:263
  36.9 9.0 %copy-start = (bf16[128,1024]{1,0:T(8,128)(2,1)S(1)}, bf16[128,1024]{1,0:T(8,128)(2,1)}, u32[]{:S(2)}) copy-start(bf16[128,1024]{1,0:T(8,128)(2,1)} %map_ref.7) | copy-start | bytes 786436
  40.7 31.2 %collective-permute-start.1 = (bf16[1072,128]{1,0:T(8,128)(2,1)}, bf16[1072,128]{1,0:T(8,128)(2,1)}, u32[]{:S(2)}, u32[]{:S(2)}) collective-permute-start(bf16[1072,128]{1,0:T(8,128)(2,1)} %shard_map.69), channel_id=1, source_target_pairs={{0,16},{1,17},{2,18},{3,19},{4,20},{5,21},{6,22},{7,23},{8,24},{9,... | collective-permute-start | bytes 823304 | tf_op jit(solution)/shard_map/ppermute | solution.py:334
  52.0 1.9 %copy-start.3 = (bf16[8,256,1024]{2,1,0:T(8,128)(2,1)}, bf16[8,256,1024]{2,1,0:T(8,128)(2,1)S(1)}, u32[]{:S(2)}) copy-start(bf16[8,256,1024]{2,1,0:T(8,128)(2,1)S(1)} %get-tuple-element.11.feat_ref) | copy-start | bytes 12582916
  54.0 1.0 copy-start.8
  58.5 7.1 %copy-start.11 = (f32[512]{0:T(512)S(1)}, f32[512]{0:T(512)}, u32[]{:S(2)}) copy-start(f32[512]{0:T(512)} %param.11) | copy-start | bytes 6148
  58.5 7.2 %copy-start.1 = (bf16[128,1024]{1,0:T(8,128)(2,1)S(1)}, bf16[128,1024]{1,0:T(8,128)(2,1)}, u32[]{:S(2)}) copy-start(bf16[128,1024]{1,0:T(8,128)(2,1)} %map_ref.7) | copy-start | bytes 786436
  58.5 13.4 %copy-start.4 = (bf16[8,256,1024]{2,1,0:T(8,128)(2,1)S(1)}, bf16[8,256,1024]{2,1,0:T(8,128)(2,1)}, u32[]{:S(2)}) copy-start(bf16[8,256,1024]{2,1,0:T(8,128)(2,1)} %copy-done.3) | copy-start | bytes 12582916
  61.6 10.3 %copy-start.9 = (f32[8,256,128]{2,1,0:T(8,128)S(1)}, f32[8,256,128]{2,1,0:T(8,128)}, u32[]{:S(2)}) copy-start(f32[8,256,128]{2,1,0:T(8,128)} %copy-done.8) | copy-start | bytes 3145732
  61.6 16.6 %collective-permute-start = (bf16[1072,128]{1,0:T(8,128)(2,1)S(1)}, bf16[1072,128]{1,0:T(8,128)(2,1)S(1)}, u32[]{:S(2)}, u32[]{:S(2)}) collective-permute-start(bf16[1072,128]{1,0:T(8,128)(2,1)S(1)} %shard_map.67), channel_id=1, source_target_pairs={{0,16},{16,0},{1,17},{17,1},{2,18},{18,2},{3,19},{19,3},{4,20},{20... | collective-permute-start | bytes 823304 | tf_op jit(solution)/shard_map/ppermute | solution.py:334

commit v11 on v10

--- a/solution.py
+++ b/solution.py
@@ -135,6 +135,41 @@
         for member in range(3):
             held = slice(features + member * RIM, features + (member + 1) * RIM)
             sent_ref[held] = rim_ref[0, member, rows - RIM :]
+
+
+def whole_totals_kernel(x_ref, halo_ref, w_ref, map_t_ref, sent_ref, k_pad, v_pad, state):
+    count, _, rows, _ = x_ref.shape
+    features, size = map_t_ref.shape[0], k_pad.shape[0] - TAIL
+    chunks = size // rows
+    for member in range(3):
+        held = slice(features + member * RIM, features + (member + 1) * RIM)
+        sent_ref[held] = x_ref[count - 1, member, rows - RIM :]
+    k_pad[:TAIL] = halo_ref[1, RIM - TAIL :].astype(jnp.float32)
+    v_pad[:TAIL] = halo_ref[2, RIM - TAIL :].astype(jnp.float32)
+    extent = 2 * BLOCK if size % (2 * BLOCK) == 0 else BLOCK
+
+    def step(i):
+        fill(k_pad, x_ref[pl.ds(i * chunks, chunks), 1])
+        fill(v_pad, x_ref[pl.ds(i * chunks, chunks), 2])
+        for begin in range(0, size, extent):
+            keys = conv(k_pad, w_ref[1], begin, extent)
+            values = conv(v_pad, w_ref[2], begin, extent)
+            update = dot(relu16(dot_nt(map_t_ref[...], keys)), values)
+            if isinstance(i, int) and begin == 0:
+                state[...] = update
+            else:
+                state[...] += update
+
+    step(0)
+
+    def later(i, carry):
+        for pad in (k_pad, v_pad):
+            pad[:TAIL] = pad[size:]
+        step(i)
+        return carry
+
+    lax.fori_loop(1, count // chunks, later, 0)
+    sent_ref[:features] = state[...].astype(jnp.bfloat16)
 
 
 def causal_scores(feats, feats_t):
@@ -315,20 +350,28 @@
             halo = next_span(x[count - 1, :, rows - RIM :], spans)
         big = chunks * (2 if count % (2 * chunks) == 0 else 1)
         tall = pltpu.VMEM((TAIL + big * rows, DH), jnp.float32)
-        sent = stepped(
-            totals_kernel,
-            count // big,
-            [x, x, x, halo, taps, map_t],
-            [
-                pl.BlockSpec((big, 1, rows, DH), lambda i: (i, 1, 0, 0)),
-                pl.BlockSpec((big, 1, rows, DH), lambda i: (i, 2, 0, 0)),
-                pl.BlockSpec((1, 3, rows, DH), lambda i: (count - 1, 0, 0, 0)),
-                whole(halo), whole(taps), whole(map_t),
-            ],
-            pl.BlockSpec((features + 3 * RIM, DH), lambda i: (0, 0)),
-            shaped((features + 3 * RIM, DH)),
-            [tall, tall, whole_state],
-        )
+        if head < heads - 1:
+            sent = stepped(
+                totals_kernel,
+                count // big,
+                [x, x, x, halo, taps, map_t],
+                [
+                    pl.BlockSpec((big, 1, rows, DH), lambda i: (i, 1, 0, 0)),
+                    pl.BlockSpec((big, 1, rows, DH), lambda i: (i, 2, 0, 0)),
+                    pl.BlockSpec((1, 3, rows, DH), lambda i: (count - 1, 0, 0, 0)),
+                    whole(halo), whole(taps), whole(map_t),
+                ],
+                pl.BlockSpec((features + 3 * RIM, DH), lambda i: (0, 0)),
+                shaped((features + 3 * RIM, DH)),
+                [tall, tall, whole_state],
+            )
+        else:
+            (sent,) = whole_call(
+                whole_totals_kernel,
+                [x, halo, taps, map_t],
+                [shaped((features + 3 * RIM, DH))],
+                [tall, tall, whole_state],
+            )
         if spans == 2:
             both = head == heads - 1
             came = lax.ppermute(sent, "span", [(0, 1), (1, 0)] if both else [(0, 1)])

time: 102 us -> 104 us (1.020)
  waiting for transfers between devices: 24.5 us -> 22.1 us
  local copies, waits for them, and re-layouts: 9.01 us -> 11.2 us
  blocking collectives: 20.3 us -> 22.1 us
    pallas_call x2 -> x1, Pallas kernels: 6.82 us -> 3.76 us  [stepped(): pl.pallas_call(kernel, grid=(steps,), in_specs=specs, out_specs=out_specs...]
    pallas_call x7 -> x8, Pallas kernels: 21.5 us -> 24.3 us  [whole_call(): pl.pallas_call(kernel, in_specs=[read] * len(inputs), out_specs=[written]...]
    ppermute x2, waiting for transfers between devices: 3.33 us -> 0.95 us  [local(): came = lax.ppermute(sent, 'span', [(0, 1), (1, 0)] if both else [(0, 1)])]
    unnamed x25, local copies, waits for them, and re-layouts: 8.91 us -> 11.1 us
    all_to_all x1, blocking collectives: 20.3 us -> 22.1 us  [exchange(): return lax.all_to_all(block, GROUP, split_axis=0, concat_axis=0, tiled=True)]
  transfers between devices with their start and end apart: 4 -> 4, of which waited for: 3 -> 3; matrix products, arithmetic and copies ran while one was open for 1% -> 1% of each run, Pallas kernels for 22% -> 21%
where the time goes in v11:
time: 104 us; the launch traced here: 103 us
  Pallas kernels  28 us (27%)
  waiting for transfers between devices  22.1 us (21%)
  blocking collectives  22.1 us (21%)
  starting transfers between devices  19.4 us (19%)
  local copies, waits for them, and re-layouts  11.2 us (11%)
    pallas_call x8, Pallas kernels, whole_call(): pl.pallas_call(kernel, in_specs=[read] * len(inputs), out_specs=[written]...  24.3 us
    all_to_all x1, blocking collectives, exchange(): return lax.all_to_all(block, GROUP, split_axis=0, concat_axis=0, tiled=True)  22.1 us
    all_to_all x2, waiting for transfers between devices, exchange(): return lax.all_to_all(block, GROUP, split_axis=0, concat_axis=0, tiled=True)  21.2 us
    unnamed x25, local copies, waits for them, and re-layouts  11.1 us
    all_to_all x2, starting transfers between devices, exchange(): return lax.all_to_all(block, GROUP, split_axis=0, concat_axis=0, tiled=True)  10.2 us
    ppermute x2, starting transfers between devices, local(): came = lax.ppermute(sent, 'span', [(0, 1), (1, 0)] if both else [(0, 1)])  9.23 us
    pallas_call x1, Pallas kernels, stepped(): pl.pallas_call(kernel, grid=(steps,), in_specs=specs, out_specs=out_specs...  3.76 us
  transfers between devices with their start and end apart: 4, of which 3 were waited for; matrix products, arithmetic and copies ran while one was open for 1% of the time, Pallas kernels for 21%

profile of v11, /device:TPU:0, one launch (start us, length us, event | category | flops | bytes accessed | tf_op | source)
XLA Modules:
  0.0 103.1 jit_solution(14329695431773619023)
XLA Ops:
  0.0 2.8 %shard_map.65 = bf16[16,3,128,128]{3,2,1,0:T(8,128)(2,1)} custom-call(bf16[128,4096]{1,0:T(8,128)(2,1)} %refs_0_.3, bf16[128,4096]{1,0:T(8,128)(2,1)} %refs_1_.3, bf16[128,4096]{1,0:T(8,128)(2,1)} %refs_2_.3), custom_call_target="tpu_custom_call" | custom-call | flops 1000 | bytes 1000 | tf_op jit(solution)/shard_map/pallas_call | solution.py:260
  2.8 6.3 %all-to-all-start.1 = ((bf16[16,3,128,128]{3,2,1,0:T(8,128)(2,1)}), bf16[16,3,128,128]{3,2,1,0:T(8,128)(2,1)S(1)}, u32[]{:S(2)}, u32[]{:S(2)}) async-start(bf16[16,3,128,128]{3,2,1,0:T(8,128)(2,1)} %shard_map.65), calls=%async_computation.1 | async-start | bytes 3145728 | tf_op jit(solution)/shard_map/all_to_all | solution.py:298
  9.1 0.0 copy-start.5
  9.1 1.2 %copy-done.5 = bf16[128,4096]{1,0:T(8,128)(2,1)S(1)} copy-done((bf16[128,4096]{1,0:T(8,128)(2,1)S(1)}, bf16[128,4096]{1,0:T(8,128)(2,1)}, u32[]{:S(2)}) %copy-start.5) | copy-done | bytes 1048600
  10.3 1.2 %copy-done.6 = bf16[128,4096]{1,0:T(8,128)(2,1)S(1)} copy-done((bf16[128,4096]{1,0:T(8,128)(2,1)S(1)}, bf16[128,4096]{1,0:T(8,128)(2,1)}, u32[]{:S(2)}) %copy-start.6) | copy-done | bytes 1048600
  11.5 1.2 %copy-done.7 = bf16[128,4096]{1,0:T(8,128)(2,1)S(1)} copy-done((bf16[128,4096]{1,0:T(8,128)(2,1)S(1)}, bf16[128,4096]{1,0:T(8,128)(2,1)}, u32[]{:S(2)}) %copy-start.7) | copy-done | bytes 1048600
  12.8 0.3 shard_map.64
  13.0 0.0 copy-start.2
  13.0 1.2 %copy-done.2 = bf16[16,3,128,128]{3,2,1,0:T(8,128)(2,1)} copy-done((bf16[16,3,128,128]{3,2,1,0:T(8,128)(2,1)}, bf16[16,3,128,128]{3,2,1,0:T(8,128)(2,1)S(1)}, u32[]{:S(2)}) %copy-start.2) | copy-done | bytes 1572888
  14.2 17.6 %all-to-all-done.1.x_ref.k_ref.v_ref.rim_ref = bf16[16,3,128,128]{3,2,1,0:T(8,128)(2,1)S(1)} async-done(((bf16[16,3,128,128]{3,2,1,0:T(8,128)(2,1)}), bf16[16,3,128,128]{3,2,1,0:T(8,128)(2,1)S(1)}, u32[]{:S(2)}, u32[]{:S(2)}) %all-to-all-start.1) | async-done | bytes 1572896 | tf_op jit(solution)/shard_map/all_to_all | solution.py:298
  31.8 3.9 %all-to-all-start = ((bf16[16,3,128,128]{3,2,1,0:T(8,128)(2,1)}), bf16[16,3,128,128]{3,2,1,0:T(8,128)(2,1)S(1)}, u32[]{:S(2)}, u32[]{:S(2)}) async-start(bf16[16,3,128,128]{3,2,1,0:T(8,128)(2,1)} %copy-done.2), calls=%async_computation | async-start | bytes 3145728 | tf_op jit(solution)/shard_map/all_to_all | solution.py:298
  35.8 1.1 %copy.7 = bf16[128,1024]{0,1:T(8,128)(2,1)S(1)} copy(bf16[128,1024]{1,0:T(8,128)(2,1)} %map_ref.7) | data formatting | bytes 524288 | tf_op args[4]
  36.9 0.0 copy-done.10
  36.9 0.0 copy-start
  36.9 3.8 %shard_map.69 = bf16[1072,128]{1,0:T(8,128)(2,1)} custom-call(bf16[16,3,128,128]{3,2,1,0:T(8,128)(2,1)S(1)} %all-to-all-done.1.x_ref.k_ref.v_ref.rim_ref, bf16[16,3,128,128]{3,2,1,0:T(8,128)(2,1)S(1)} %all-to-all-done.1.x_ref.k_ref.v_ref.rim_ref, bf16[16,3,128,128]{3,2,1,0:T(8,128)(2,1)S(1)} %all-to-all-done.1.x_ref.k_ref.v_ref.rim_ref, ...), custom_call_target="tpu_custom_call" | custom-call | flops 1000 | bytes 1000 | tf_op jit(solution)/shard_map/pallas_call | solution.py:272
  40.7 5.2 %collective-permute-start.1 = (bf16[1072,128]{1,0:T(8,128)(2,1)}, bf16[1072,128]{1,0:T(8,128)(2,1)}, u32[]{:S(2)}, u32[]{:S(2)}) collective-permute-start(bf16[1072,128]{1,0:T(8,128)(2,1)} %shard_map.69), channel_id=1, source_target_pairs={{0,16},{1,17},{2,18},{3,19},{4,20},{5,21},{6,22},{7,23},{8,24},{9,... | collective-permute-start | bytes 823304 | tf_op jit(solution)/shard_map/ppermute | solution.py:377
  45.9 6.1 %shard_map.66 = (f32[8,256,128]{2,1,0:T(8,128)S(1)}, bf16[8,256,1024]{2,1,0:T(8,128)(2,1)S(1)}) custom-call(bf16[16,3,128,128]{3,2,1,0:T(8,128)(2,1)S(1)} %all-to-all-done.1.x_ref.k_ref.v_ref.rim_ref, f32[3,4,128]{2,1,0:T(4,128)S(1)} %get-tuple-element.18.w_ref, bf16[128,1024]{1,0:T(8,128)(2,1)S(1)} %copy-done, bf16[1024,128]{1,0:T(8,128)(2,1)S(1)} %bitcast.4), custom_call_target="tpu_custom_call" | custom-call | flops 1000 | bytes 1000 | tf_op jit(solution)/shard_map/pallas_call | solution.py:260
  52.0 1.9 %copy-done.3 = bf16[8,256,1024]{2,1,0:T(8,128)(2,1)} copy-done((bf16[8,256,1024]{2,1,0:T(8,128)(2,1)}, bf16[8,256,1024]{2,1,0:T(8,128)(2,1)S(1)}, u32[]{:S(2)}) %copy-start.3) | copy-done | bytes 4194328
  54.0 1.0 copy-done.8
  55.0 3.6 %all-to-all-done.x_ref = bf16[16,3,128,128]{3,2,1,0:T(8,128)(2,1)S(1)} async-done(((bf16[16,3,128,128]{3,2,1,0:T(8,128)(2,1)}), bf16[16,3,128,128]{3,2,1,0:T(8,128)(2,1)S(1)}, u32[]{:S(2)}, u32[]{:S(2)}) %all-to-all-start) | async-done | bytes 1572896 | tf_op jit(solution)/shard_map/all_to_all | solution.py:298
  58.5 2.6 %shard_map.67 = bf16[1072,128]{1,0:T(8,128)(2,1)S(1)} custom-call(bf16[16,3,128,128]{3,2,1,0:T(8,128)(2,1)S(1)} %all-to-all-done.x_ref, bf16[3,16,128]{2,1,0:T(8,128)(2,1)S(1)} %broadcast_1_halo_ref.2.halo_ref, f32[3,4,128]{2,1,0:T(4,128)S(1)} %get-tuple-element.17.w_ref, bf16[1024,128]{1,0:T(8,128)(2,1)S(1)} %bitcast.5), custom_call_target="tpu_custom_call" | custom-call | flops 1000 | bytes 1000 | tf_op jit(solution)/shard_map/pallas_call | solution.py:260
  61.1 0.0 copy-start.9
  61.1 4.1 %collective-permute-start = (bf16[1072,128]{1,0:T(8,128)(2,1)S(1)}, bf16[1072,128]{1,0:T(8,128)(2,1)S(1)}, u32[]{:S(2)}, u32[]{:S(2)}) collective-permute-start(bf16[1072,128]{1,0:T(8,128)(2,1)S(1)} %shard_map.67), channel_id=1, source_target_pairs={{0,16},{16,0},{1,17},{17,1},{2,18},{18,2},{3,19},{19,3},{4,20},{20... | collective-permute-start | bytes 823304 | tf_op jit(solution)/shard_map/ppermute | solution.py:377
  65.2 0.1 dynamic_slice.7
  65.3 6.3 %shard_map.68 = (f32[8,256,128]{2,1,0:T(8,128)S(1)}, bf16[8,256,1024]{2,1,0:T(8,128)(2,1)S(1)}) custom-call(bf16[16,3,128,128]{3,2,1,0:T(8,128)(2,1)S(1)} %all-to-all-done.x_ref, f32[3,4,128]{2,1,0:T(4,128)S(1)} %get-tuple-element.17.w_ref, bf16[128,1024]{1,0:T(8,128)(2,1)S(1)} %copy-done.1, bf16[1024,128]{1,0:T(8,128)(2,1)S(1)} %bitcast.6), custom_call_target="tpu_custom_call" | custom-call | flops 1000 | bytes 1000 | tf_op jit(solution)/shard_map/pallas_call | solution.py:260
  71.6 0.0 collective-permute-done.1.came_ref
  71.6 2.2 %copy-done.4 = bf16[8,256,1024]{2,1,0:T(8,128)(2,1)S(1)} copy-done((bf16[8,256,1024]{2,1,0:T(8,128)(2,1)S(1)}, bf16[8,256,1024]{2,1,0:T(8,128)(2,1)}, u32[]{:S(2)}) %copy-start.4) | copy-done | bytes 4194328
  73.8 2.9 %shard_map.70.refs_0_ = bf16[16,1,128,128]{3,2,1,0:T(8,128)(2,1)S(1)} custom-call(bf16[16,3,128,128]{3,2,1,0:T(8,128)(2,1)S(1)} %all-to-all-done.1.x_ref.k_ref.v_ref.rim_ref, bf16[1072,128]{1,0:T(8,128)(2,1)} %collective-permute-done.1.came_ref, f32[3,4,128]{2,1,0:T(4,128)S(1)} %get-tuple-element.18.w_ref, bf16[128,1024]{1,0:T(8,128)(2,1)S(1)} %copy-done.1, ...), custom_call_target="tpu_custom_call" | custom-call | flops 1000 | bytes 1000 | tf_op jit(solution)/shard_map/pallas_call | solution.py:260
  76.8 1.0 collective-permute-done.came_ref
  77.7 2.0 %shard_map.71 = bf16[16,2,128,128]{3,2,1,0:T(8,128)(2,1)S(1)} custom-call(bf16[16,3,128,128]{3,2,1,0:T(8,128)(2,1)S(1)} %all-to-all-done.x_ref, bf16[1072,128]{1,0:T(8,128)(2,1)S(1)} %collective-permute-done.came_ref, f32[3,4,128]{2,1,0:T(4,128)S(1)} %get-tuple-element.17.w_ref, bf16[128,1024]{1,0:T(8,128)(2,1)S(1)} %copy-done.1, ...), custom_call_target="tpu_custom_call" | custom-call | flops 1000 | bytes 1000 | tf_op jit(solution)/shard_map/pallas_call | solution.py:260
  79.7 22.1 %all_to_all.15 = bf16[16,2,128,128]{3,2,1,0:T(8,128)(2,1)S(1)} all-to-all(bf16[16,2,128,128]{3,2,1,0:T(8,128)(2,1)S(1)} %shard_map.71), channel_id=1, replica_groups=mesh['span'=2,'part'=2,'sp'=8] {'part','sp'}, dimensions={0} | all-to-all | bytes 2097152 | tf_op jit(solution)/shard_map/all_to_all | solution.py:298
  101.8 1.2 %shard_map.72 = bf16[128,4096]{1,0:T(8,128)(2,1)} custom-call(bf16[2,8,2,128,128]{4,3,2,1,0:T(8,128)(2,1)S(1)} %bitcast.9), custom_call_target="tpu_custom_call" | custom-call | flops 1000 | bytes 1000 | tf_op jit(solution)/shard_map/pallas_call | solution.py:260
  (15 shorter events, 0.0 us)
Async XLA Ops:
  2.8 29.1 %all-to-all-start.1 = ((bf16[16,3,128,128]{3,2,1,0:T(8,128)(2,1)}), bf16[16,3,128,128]{3,2,1,0:T(8,128)(2,1)S(1)}, u32[]{:S(2)}, u32[]{:S(2)}) async-start(bf16[16,3,128,128]{3,2,1,0:T(8,128)(2,1)} %shard_map.65), calls=%async_computation.1 | async-start | bytes 3145728 | tf_op jit(solution)/shard_map/all_to_all | solution.py:298
  9.1 1.2 %copy-start.5 = (bf16[128,4096]{1,0:T(8,128)(2,1)S(1)}, bf16[128,4096]{1,0:T(8,128)(2,1)}, u32[]{:S(2)}) copy-start(bf16[128,4096]{1,0:T(8,128)(2,1)} %refs_0_.3) | copy-start | bytes 3145732
  10.3 1.2 %copy-start.6 = (bf16[128,4096]{1,0:T(8,128)(2,1)S(1)}, bf16[128,4096]{1,0:T(8,128)(2,1)}, u32[]{:S(2)}) copy-start(bf16[128,4096]{1,0:T(8,128)(2,1)} %refs_1_.3) | copy-start | bytes 3145732
  11.5 1.2 %copy-start.7 = (bf16[128,4096]{1,0:T(8,128)(2,1)S(1)}, bf16[128,4096]{1,0:T(8,128)(2,1)}, u32[]{:S(2)}) copy-start(bf16[128,4096]{1,0:T(8,128)(2,1)} %refs_2_.3) | copy-start | bytes 3145732
  13.0 1.2 %copy-start.2 = (bf16[16,3,128,128]{3,2,1,0:T(8,128)(2,1)}, bf16[16,3,128,128]{3,2,1,0:T(8,128)(2,1)S(1)}, u32[]{:S(2)}) copy-start(bf16[16,3,128,128]{3,2,1,0:T(8,128)(2,1)S(1)} %shard_map.64) | copy-start | bytes 4718596
  14.2 22.7 %copy-start.10 = (f32[3,4,512]{2,1,0:T(4,128)S(1)}, f32[3,4,512]{2,1,0:T(4,128)}, u32[]{:S(2)}) copy-start(f32[3,4,512]{2,1,0:T(4,128)} %param.9) | copy-start | bytes 73732
  31.8 26.7 %all-to-all-start = ((bf16[16,3,128,128]{3,2,1,0:T(8,128)(2,1)}), bf16[16,3,128,128]{3,2,1,0:T(8,128)(2,1)S(1)}, u32[]{:S(2)}, u32[]{:S(2)}) async-start(bf16[16,3,128,128]{3,2,1,0:T(8,128)(2,1)} %copy-done.2), calls=%async_computation | async-start | bytes 3145728 | tf_op jit(solution)/shard_map/all_to_all | solution.py:298
  36.9 9.0 %copy-start = (bf16[128,1024]{1,0:T(8,128)(2,1)S(1)}, bf16[128,1024]{1,0:T(8,128)(2,1)}, u32[]{:S(2)}) copy-start(bf16[128,1024]{1,0:T(8,128)(2,1)} %map_ref.7) | copy-start | bytes 786436
  40.7 30.9 %collective-permute-start.1 = (bf16[1072,128]{1,0:T(8,128)(2,1)}, bf16[1072,128]{1,0:T(8,128)(2,1)}, u32[]{:S(2)}, u32[]{:S(2)}) collective-permute-start(bf16[1072,128]{1,0:T(8,128)(2,1)} %shard_map.69), channel_id=1, source_target_pairs={{0,16},{1,17},{2,18},{3,19},{4,20},{5,21},{6,22},{7,23},{8,24},{9,... | collective-permute-start | bytes 823304 | tf_op jit(solution)/shard_map/ppermute | solution.py:377
  52.0 1.9 %copy-start.3 = (bf16[8,256,1024]{2,1,0:T(8,128)(2,1)}, bf16[8,256,1024]{2,1,0:T(8,128)(2,1)S(1)}, u32[]{:S(2)}) copy-start(bf16[8,256,1024]{2,1,0:T(8,128)(2,1)S(1)} %get-tuple-element.11.feat_ref) | copy-start | bytes 12582916
  54.0 1.0 copy-start.8
  55.0 10.2 %copy-start.11 = (f32[512]{0:T(512)S(1)}, f32[512]{0:T(512)}, u32[]{:S(2)}) copy-start(f32[512]{0:T(512)} %param.11) | copy-start | bytes 6148
  58.5 6.7 %copy-start.1 = (bf16[128,1024]{1,0:T(8,128)(2,1)S(1)}, bf16[128,1024]{1,0:T(8,128)(2,1)}, u32[]{:S(2)}) copy-start(bf16[128,1024]{1,0:T(8,128)(2,1)} %map_ref.7) | copy-start | bytes 786436
  61.1 10.5 %copy-start.9 = (f32[8,256,128]{2,1,0:T(8,128)S(1)}, f32[8,256,128]{2,1,0:T(8,128)}, u32[]{:S(2)}) copy-start(f32[8,256,128]{2,1,0:T(8,128)} %copy-done.8) | copy-start | bytes 3145732
  61.1 16.6 %collective-permute-start = (bf16[1072,128]{1,0:T(8,128)(2,1)S(1)}, bf16[1072,128]{1,0:T(8,128)(2,1)S(1)}, u32[]{:S(2)}, u32[]{:S(2)}) collective-permute-start(bf16[1072,128]{1,0:T(8,128)(2,1)S(1)} %shard_map.67), channel_id=1, source_target_pairs={{0,16},{16,0},{1,17},{17,1},{2,18},{18,2},{3,19},{19,3},{4,20},{20... | collective-permute-start | bytes 823304 | tf_op jit(solution)/shard_map/ppermute | solution.py:377
  71.6 2.2 %copy-start.4 = (bf16[8,256,1024]{2,1,0:T(8,128)(2,1)S(1)}, bf16[8,256,1024]{2,1,0:T(8,128)(2,1)}, u32[]{:S(2)}) copy-start(bf16[8,256,1024]{2,1,0:T(8,128)(2,1)} %copy-done.3) | copy-start | bytes 12582916
